TPU v7x, 128 devices: a whole 4x4x4 slice. The times are simulated.
128 devices in a mesh: tile: 8 (over y_hi, x), orient: 16 (over z, y_lo, core).
Axes of the slice: x: 4, y: 4 (y_hi: 2, y_lo: 2; y = y_hi * 2 + y_lo), z: 4, core: 2. Of those that a mesh axis runs over, the one named last changes fastest.
Arguments:
- tile_images: bfloat16 [32, 256, 256], P('tile', 'orient'), may hold values from -6 to 6
- templates: bfloat16 [192, 128, 128], P('orient'), may hold values from -6 to 6
- filters: float32 [8, 256, 256], P('tile'), may hold values from 0.25 to 4
- tile_bins: int32 [32], replicated, may hold values from 0 to 7, as said below
Outputs:
- best_snr: float32 [32, 256, 256], P('tile', 'orient')
Inputs may be any that keep to these rules, and one draw needn't show every extreme that they name: `tile_bins`: every bin is named by 1 to 8 tiles, and one bin by exactly 8.
All inputs are finite; a program needn't handle non-finite values.
Results may differ from a plain program's by a relative error of at most 0.0031.
Values may be sent and summed in bfloat16 or wider, within the bound.
No kernel may reach another device: no remote copies, remote signals or barrier semaphores. Data moves between devices by JAX's collectives and lax.ppermute only.
A program may use at most 64 MiB of HBM per device.

v0:
```python
import math

import jax
import jax.numpy as jnp
from jax import lax
from jax.sharding import PartitionSpec as P


def tables(side_length, count):
    row_index = jnp.arange(side_length, dtype=jnp.int32)[:, None]
    col_index = jnp.arange(count, dtype=jnp.int32)[None, :]
    phases = (row_index * col_index % side_length).astype(jnp.float32) * (
        2.0 * math.pi / side_length
    )
    return (jnp.cos(phases).astype(jnp.bfloat16), jnp.sin(phases).astype(jnp.bfloat16))


def product(pattern, first_op, second_op):
    return jnp.einsum(pattern, first_op, second_op, preferred_element_type=jnp.float32)


def correlate(spec_re, spec_im, temp_re, temp_im, filter_map, cosine, sine):
    tile_re = spec_re.astype(jnp.float32)
    tile_im = spec_im.astype(jnp.float32)
    proj_re = temp_re.astype(jnp.float32)[None]
    proj_im = temp_im.astype(jnp.float32)[None]
    prod_re = ((proj_re * tile_re + proj_im * tile_im) * filter_map).astype(jnp.bfloat16)
    prod_im = ((proj_re * tile_im - proj_im * tile_re) * filter_map).astype(jnp.bfloat16)
    half_re = (
        product("xk,sky->sxy", cosine, prod_re) - product("xk,sky->sxy", sine, prod_im)
    ).astype(jnp.bfloat16)
    half_im = (
        product("xk,sky->sxy", cosine, prod_im) + product("xk,sky->sxy", sine, prod_re)
    ).astype(jnp.bfloat16)
    correlation = product("sxk,ky->sxy", half_re, cosine) - product("sxk,ky->sxy", half_im, sine)
    norm_scale = lax.rsqrt(jnp.mean(correlation * correlation, axis=(1, 2), keepdims=True) + 1e-06)
    return correlation * norm_scale


def shards(tile_images, templates, filters, tile_bins):
    own_tiles = tile_images.shape[0]
    row_count = tile_images.shape[1]
    side_length = tile_images.shape[2]
    template_side = templates.shape[1]
    tile_count = tile_bins.shape[0]
    capacity = 2 * own_tiles
    group_index = lax.axis_index("tile")
    shard_index = lax.axis_index("orient")
    cosine, sine = tables(side_length, side_length)
    cos_part, sin_part = tables(side_length, template_side)
    row_re = product("tak,ky->tay", tile_images, cosine).astype(jnp.bfloat16)
    row_im = (-product("tak,ky->tay", tile_images, sine)).astype(jnp.bfloat16)
    positions = jnp.arange(tile_count, dtype=jnp.int32)
    same_bin = (tile_bins[:, None] == tile_bins[None, :]) & (
        positions[None, :] < positions[:, None]
    )
    bin_rank = jnp.sum(same_bin.astype(jnp.int32), axis=1)
    first_tile = group_index * own_tiles
    own_bins = lax.dynamic_slice_in_dim(tile_bins, first_tile, own_tiles, 0)
    own_ranks = lax.dynamic_slice_in_dim(bin_rank, first_tile, own_tiles, 0)
    in_group = tile_bins == group_index
    slot_ids = jnp.arange(capacity, dtype=jnp.int32)
    selector = (in_group[None, :] & (bin_rank[None, :] == slot_ids[:, None])).astype(jnp.bfloat16)
    slot_re = product("st,tay->say", selector, lax.all_gather(row_re, "tile", axis=0, tiled=True))
    slot_im = product("st,tay->say", selector, lax.all_gather(row_im, "tile", axis=0, tiled=True))
    slot_re = slot_re.astype(jnp.bfloat16)
    slot_im = slot_im.astype(jnp.bfloat16)
    slot_total = slot_re.shape[0]
    part_re = lax.all_gather(slot_re, "orient", axis=1, tiled=True)
    part_im = lax.all_gather(slot_im, "orient", axis=1, tiled=True)
    spec_re = product("xa,say->sxy", cosine, part_re) + product("xa,say->sxy", sine, part_im)
    spec_im = product("xa,say->sxy", cosine, part_im) - product("xa,say->sxy", sine, part_re)
    spec_re = spec_re.astype(jnp.bfloat16)
    spec_im = spec_im.astype(jnp.bfloat16)
    temp_row_re = product("oak,yk->oay", templates, cos_part).astype(jnp.bfloat16)
    temp_row_im = (-product("oak,yk->oay", templates, sin_part)).astype(jnp.bfloat16)
    temp_re = (
        product("xa,oay->oxy", cos_part, temp_row_re)
        + product("xa,oay->oxy", sin_part, temp_row_im)
    ).astype(jnp.bfloat16)
    temp_im = (
        product("xa,oay->oxy", cos_part, temp_row_im)
        - product("xa,oay->oxy", sin_part, temp_row_re)
    ).astype(jnp.bfloat16)

    def fold_step(running, batch_pair):
        scores = correlate(spec_re, spec_im, batch_pair[0], batch_pair[1], filters, cosine, sine)
        return (jnp.maximum(running, scores), None)

    initial = jnp.full((slot_total, side_length, side_length), -jnp.inf, dtype=jnp.float32)
    running, _ = lax.scan(fold_step, initial, (temp_re, temp_im))
    merged = lax.pmax(running, "orient")
    own_rows = lax.dynamic_slice_in_dim(merged, shard_index * row_count, row_count, 1)
    collected = lax.all_gather(own_rows, "tile", axis=0, tiled=True)
    slot_index = own_bins * capacity + own_ranks
    return jnp.take(collected, slot_index, axis=0)


def solution(mesh):
    placed = (P("tile", "orient", None), P("orient", None, None), P("tile", None, None), P())
    return jax.shard_map(
        shards, mesh=mesh, in_specs=placed, out_specs=P("tile", "orient", None), check_vma=False
    )
```

profile of v0, /device:TPU:1, one launch (start us, length us, event | category | flops | bytes accessed | tf_op | source)
XLA Modules:
  0.0 563.7 jit_solution(6366856187222771006)
XLA Ops:
  10.0 29.6 %all_gather.15 = bf16[32,16,256]{2,1,0:T(8,128)(2,1)S(1)} all-gather(bf16[4,16,256]{2,1,0:T(8,128)(2,1)S(1)} %fusion.67), channel_id=1, replica_groups=mesh['tile'=8,'orient'=16] {'tile'}, dimensions={0}, use_global_device_ids=true | all-gather | bytes 294912 | tf_op jit(solution)/shard_map/all_gather | solution.py:64
  42.3 28.4 %all_gather.17 = bf16[32,16,256]{2,1,0:T(8,128)(2,1)S(1)} all-gather(bf16[4,16,256]{2,1,0:T(8,128)(2,1)S(1)} %fusion.68), channel_id=1, replica_groups=mesh['tile'=8,'orient'=16] {'tile'}, dimensions={0}, use_global_device_ids=true | all-gather | bytes 294912 | tf_op jit(solution)/shard_map/all_gather | solution.py:65
  81.5 4.0 fusion.73
  85.4 33.3 %all-gather.6.cloned.1.call-done = bf16[8,256,256]{2,0,1:T(8,128)(2,1)} async-done(((bf16[8,16,256]{2,0,1:T(8,128)(2,1)}), bf16[8,256,256]{2,0,1:T(8,128)(2,1)}) %all-gather.6.cloned.1.call-update) | async-done | bytes 1048592 | tf_op jit(solution)/shard_map/all_gather | solution.py:70
  124.5 256.4 %while.12 = (s32[]{:T(128)}, f32[8,256,256]{2,1,0:T(8,128)}, bf16[12,256,256]{1,2,0:T(8,128)(2,1)}, bf16[8,256,256]{1,2,0:T(8,128)(2,1)S(1)}, bf16[12,256,256]{1...) while((s32[]{:T(128)}, f32[8,256,256]{2,1,0:T(8,128)}, ...), condition=%wide.region_3.4_spmd.clone.clone, body=%wide.region_1.3_spmd.clone.clone.sunk | while | flops 1636564992 | bytes 33292520 | solution.py:91
  128.7 5.1 fusion.198
  136.6 5.6 %multiply_reduce_fusion.2 = (f32[8]{0:T(128)S(1)}, f32[8,256,256]{2,1,0:T(8,128)}) fusion(f32[8,256,256]{2,1,0:T(8,128)} %fusion.198, f32[8,256,256]{2,1,0:T(8,128)} %fusion.199, bf16[8,256,256]{1,2,0:T(8,128)(2,1)S(1)} %get-tuple-element.240, bf16[8,256,256]{1,2,0:T(8,128)(2,1)S(1)} %get-tuple-element.242, f32[256,256]{0,1:T(8,128)S(1)} %bitcast.103, ...), kind=kOutput, calls=%fused_computation.14.clone.1 | convolution fusion | flops 545128448 | bytes 9175072 | tf_op jit(solution)/shard_map/while/body/eval_jaxpr/sxk,ky->sxy/dot_general | solution.py:19
  142.3 3.3 select_maximum_fusion.2
  149.4 5.1 fusion.198
  157.4 5.7 %multiply_reduce_fusion.2 = (f32[8]{0:T(128)S(1)}, f32[8,256,256]{2,1,0:T(8,128)}) fusion(f32[8,256,256]{2,1,0:T(8,128)} %fusion.198, f32[8,256,256]{2,1,0:T(8,128)} %fusion.199, bf16[8,256,256]{1,2,0:T(8,128)(2,1)S(1)} %get-tuple-element.240, bf16[8,256,256]{1,2,0:T(8,128)(2,1)S(1)} %get-tuple-element.242, f32[256,256]{0,1:T(8,128)S(1)} %bitcast.103, ...), kind=kOutput, calls=%fused_computation.14.clone.1 | convolution fusion | flops 545128448 | bytes 9175072 | tf_op jit(solution)/shard_map/while/body/eval_jaxpr/sxk,ky->sxy/dot_general | solution.py:19
  163.1 3.9 select_maximum_fusion.2
  170.8 5.1 fusion.198
  178.8 5.6 %multiply_reduce_fusion.2 = (f32[8]{0:T(128)S(1)}, f32[8,256,256]{2,1,0:T(8,128)}) fusion(f32[8,256,256]{2,1,0:T(8,128)} %fusion.198, f32[8,256,256]{2,1,0:T(8,128)} %fusion.199, bf16[8,256,256]{1,2,0:T(8,128)(2,1)S(1)} %get-tuple-element.240, bf16[8,256,256]{1,2,0:T(8,128)(2,1)S(1)} %get-tuple-element.242, f32[256,256]{0,1:T(8,128)S(1)} %bitcast.103, ...), kind=kOutput, calls=%fused_computation.14.clone.1 | convolution fusion | flops 545128448 | bytes 9175072 | tf_op jit(solution)/shard_map/while/body/eval_jaxpr/sxk,ky->sxy/dot_general | solution.py:19
  184.5 3.9 select_maximum_fusion.2
  189.3 2.9 fusion.197
  192.2 5.1 fusion.198
  200.2 5.6 %multiply_reduce_fusion.2 = (f32[8]{0:T(128)S(1)}, f32[8,256,256]{2,1,0:T(8,128)}) fusion(f32[8,256,256]{2,1,0:T(8,128)} %fusion.198, f32[8,256,256]{2,1,0:T(8,128)} %fusion.199, bf16[8,256,256]{1,2,0:T(8,128)(2,1)S(1)} %get-tuple-element.240, bf16[8,256,256]{1,2,0:T(8,128)(2,1)S(1)} %get-tuple-element.242, f32[256,256]{0,1:T(8,128)S(1)} %bitcast.103, ...), kind=kOutput, calls=%fused_computation.14.clone.1 | convolution fusion | flops 545128448 | bytes 9175072 | tf_op jit(solution)/shard_map/while/body/eval_jaxpr/sxk,ky->sxy/dot_general | solution.py:19
  205.9 3.9 select_maximum_fusion.2
  210.7 2.9 fusion.197
  213.6 5.1 fusion.198
  221.6 5.6 %multiply_reduce_fusion.2 = (f32[8]{0:T(128)S(1)}, f32[8,256,256]{2,1,0:T(8,128)}) fusion(f32[8,256,256]{2,1,0:T(8,128)} %fusion.198, f32[8,256,256]{2,1,0:T(8,128)} %fusion.199, bf16[8,256,256]{1,2,0:T(8,128)(2,1)S(1)} %get-tuple-element.240, bf16[8,256,256]{1,2,0:T(8,128)(2,1)S(1)} %get-tuple-element.242, f32[256,256]{0,1:T(8,128)S(1)} %bitcast.103, ...), kind=kOutput, calls=%fused_computation.14.clone.1 | convolution fusion | flops 545128448 | bytes 9175072 | tf_op jit(solution)/shard_map/while/body/eval_jaxpr/sxk,ky->sxy/dot_general | solution.py:19
  227.2 3.9 select_maximum_fusion.2
  235.0 5.1 fusion.198
  243.0 5.6 %multiply_reduce_fusion.2 = (f32[8]{0:T(128)S(1)}, f32[8,256,256]{2,1,0:T(8,128)}) fusion(f32[8,256,256]{2,1,0:T(8,128)} %fusion.198, f32[8,256,256]{2,1,0:T(8,128)} %fusion.199, bf16[8,256,256]{1,2,0:T(8,128)(2,1)S(1)} %get-tuple-element.240, bf16[8,256,256]{1,2,0:T(8,128)(2,1)S(1)} %get-tuple-element.242, f32[256,256]{0,1:T(8,128)S(1)} %bitcast.103, ...), kind=kOutput, calls=%fused_computation.14.clone.1 | convolution fusion | flops 545128448 | bytes 9175072 | tf_op jit(solution)/shard_map/while/body/eval_jaxpr/sxk,ky->sxy/dot_general | solution.py:19
  248.6 3.9 select_maximum_fusion.2
  253.5 2.9 fusion.197
  256.4 5.1 fusion.198
  264.4 5.6 %multiply_reduce_fusion.2 = (f32[8]{0:T(128)S(1)}, f32[8,256,256]{2,1,0:T(8,128)}) fusion(f32[8,256,256]{2,1,0:T(8,128)} %fusion.198, f32[8,256,256]{2,1,0:T(8,128)} %fusion.199, bf16[8,256,256]{1,2,0:T(8,128)(2,1)S(1)} %get-tuple-element.240, bf16[8,256,256]{1,2,0:T(8,128)(2,1)S(1)} %get-tuple-element.242, f32[256,256]{0,1:T(8,128)S(1)} %bitcast.103, ...), kind=kOutput, calls=%fused_computation.14.clone.1 | convolution fusion | flops 545128448 | bytes 9175072 | tf_op jit(solution)/shard_map/while/body/eval_jaxpr/sxk,ky->sxy/dot_general | solution.py:19
  270.0 3.9 select_maximum_fusion.2
  274.9 2.9 fusion.197
  277.8 5.1 fusion.198
  285.8 5.6 %multiply_reduce_fusion.2 = (f32[8]{0:T(128)S(1)}, f32[8,256,256]{2,1,0:T(8,128)}) fusion(f32[8,256,256]{2,1,0:T(8,128)} %fusion.198, f32[8,256,256]{2,1,0:T(8,128)} %fusion.199, bf16[8,256,256]{1,2,0:T(8,128)(2,1)S(1)} %get-tuple-element.240, bf16[8,256,256]{1,2,0:T(8,128)(2,1)S(1)} %get-tuple-element.242, f32[256,256]{0,1:T(8,128)S(1)} %bitcast.103, ...), kind=kOutput, calls=%fused_computation.14.clone.1 | convolution fusion | flops 545128448 | bytes 9175072 | tf_op jit(solution)/shard_map/while/body/eval_jaxpr/sxk,ky->sxy/dot_general | solution.py:19
  291.4 3.9 select_maximum_fusion.2
  299.2 5.1 fusion.198
  307.2 5.6 %multiply_reduce_fusion.2 = (f32[8]{0:T(128)S(1)}, f32[8,256,256]{2,1,0:T(8,128)}) fusion(f32[8,256,256]{2,1,0:T(8,128)} %fusion.198, f32[8,256,256]{2,1,0:T(8,128)} %fusion.199, bf16[8,256,256]{1,2,0:T(8,128)(2,1)S(1)} %get-tuple-element.240, bf16[8,256,256]{1,2,0:T(8,128)(2,1)S(1)} %get-tuple-element.242, f32[256,256]{0,1:T(8,128)S(1)} %bitcast.103, ...), kind=kOutput, calls=%fused_computation.14.clone.1 | convolution fusion | flops 545128448 | bytes 9175072 | tf_op jit(solution)/shard_map/while/body/eval_jaxpr/sxk,ky->sxy/dot_general | solution.py:19
  312.8 3.9 select_maximum_fusion.2
  320.6 5.1 fusion.198
  328.6 5.6 %multiply_reduce_fusion.2 = (f32[8]{0:T(128)S(1)}, f32[8,256,256]{2,1,0:T(8,128)}) fusion(f32[8,256,256]{2,1,0:T(8,128)} %fusion.198, f32[8,256,256]{2,1,0:T(8,128)} %fusion.199, bf16[8,256,256]{1,2,0:T(8,128)(2,1)S(1)} %get-tuple-element.240, bf16[8,256,256]{1,2,0:T(8,128)(2,1)S(1)} %get-tuple-element.242, f32[256,256]{0,1:T(8,128)S(1)} %bitcast.103, ...), kind=kOutput, calls=%fused_computation.14.clone.1 | convolution fusion | flops 545128448 | bytes 9175072 | tf_op jit(solution)/shard_map/while/body/eval_jaxpr/sxk,ky->sxy/dot_general | solution.py:19
  334.2 3.9 select_maximum_fusion.2
  339.1 2.9 fusion.197
  342.0 5.1 fusion.198
  350.0 5.6 %multiply_reduce_fusion.2 = (f32[8]{0:T(128)S(1)}, f32[8,256,256]{2,1,0:T(8,128)}) fusion(f32[8,256,256]{2,1,0:T(8,128)} %fusion.198, f32[8,256,256]{2,1,0:T(8,128)} %fusion.199, bf16[8,256,256]{1,2,0:T(8,128)(2,1)S(1)} %get-tuple-element.240, bf16[8,256,256]{1,2,0:T(8,128)(2,1)S(1)} %get-tuple-element.242, f32[256,256]{0,1:T(8,128)S(1)} %bitcast.103, ...), kind=kOutput, calls=%fused_computation.14.clone.1 | convolution fusion | flops 545128448 | bytes 9175072 | tf_op jit(solution)/shard_map/while/body/eval_jaxpr/sxk,ky->sxy/dot_general | solution.py:19
  355.6 3.9 select_maximum_fusion.2
  363.4 5.1 fusion.198
  371.4 5.6 %multiply_reduce_fusion.2 = (f32[8]{0:T(128)S(1)}, f32[8,256,256]{2,1,0:T(8,128)}) fusion(f32[8,256,256]{2,1,0:T(8,128)} %fusion.198, f32[8,256,256]{2,1,0:T(8,128)} %fusion.199, bf16[8,256,256]{1,2,0:T(8,128)(2,1)S(1)} %get-tuple-element.240, bf16[8,256,256]{1,2,0:T(8,128)(2,1)S(1)} %get-tuple-element.242, f32[256,256]{0,1:T(8,128)S(1)} %bitcast.103, ...), kind=kOutput, calls=%fused_computation.14.clone.1 | convolution fusion | flops 545128448 | bytes 9175072 | tf_op jit(solution)/shard_map/while/body/eval_jaxpr/sxk,ky->sxy/dot_general | solution.py:19
  377.0 3.9 select_maximum_fusion.2
  381.0 123.9 %all-reduce.2.cloned.1.call-done = f32[8,256,256]{2,1,0:T(8,128)} async-done(((f32[8,256,256]{2,1,0:T(8,128)}), f32[8,256,256]{2,1,0:T(8,128)}) %all-reduce.2.cloned.1.call-update) | async-done | bytes 2097168 | tf_op jit(solution)/shard_map/pmax | solution.py:92
  506.6 48.1 %all-gather.8.cloned.1.call-done = f32[64,16,256]{2,1,0:T(8,128)} async-done(((f32[8,16,256]{2,1,0:T(8,128)}), f32[64,16,256]{2,1,0:T(8,128)}) %all-gather.8.cloned.1.call-update) | async-done | bytes 1048592 | tf_op jit(solution)/shard_map/all_gather | solution.py:94
  (86 shorter events, 93.4 us)
Async XLA Ops:
  6.5 65.2 %copy-start = (bf16[12,128,128]{2,1,0:T(8,128)(2,1)S(1)}, bf16[12,128,128]{2,1,0:T(8,128)(2,1)}, u32[]{:S(2)}) copy-start(bf16[12,128,128]{2,1,0:T(8,128)(2,1)} %param.7) | copy-start | bytes 1179652
  6.5 74.9 %all-gather.4.cloned.1.call-start = ((), (), s32[]{:S(2)}) async-start(), calls=%async_computation | async-start | bytes 1114112 | tf_op jit(solution)/shard_map/all_gather | solution.py:69
  10.0 62.6 %copy-start.4 = (f32[1,256,256]{2,1,0:T(8,128)S(1)}, f32[1,256,256]{2,1,0:T(8,128)}, u32[]{:S(2)}) copy-start(f32[1,256,256]{2,1,0:T(8,128)} %param.8) | copy-start | bytes 786436
  40.4 78.3 %all-gather.6.cloned.1.call-start = ((), (), s32[]{:S(2)}) async-start(), calls=%async_computation.1 | async-start | bytes 1114112 | tf_op jit(solution)/shard_map/all_gather | solution.py:70
  71.5 433.4 %all-reduce.2.cloned.1.call-start = ((), (), s32[]{:S(2)}) async-start(), calls=%async_computation.2 | async-start | bytes 4194304 | tf_op jit(solution)/shard_map/pmax | solution.py:92
  118.7 2.8 copy-start.1
  118.7 2.8 copy-start.3
  121.6 1.5 copy-start.2
  380.9 125.6 %copy-start.5 = (s32[32]{0:T(128)S(1)}, s32[32]{0:T(128)}, u32[]{:S(2)}) copy-start(s32[32]{0:T(128)} %param.9) | copy-start | bytes 388
  380.9 173.7 %all-gather.8.cloned.1.call-start = ((), (), s32[]{:S(2)}) async-start(), calls=%async_computation.3 | async-start | bytes 1179648 | tf_op jit(solution)/shard_map/all_gather | solution.py:94
Sparse Core Ops, SparseCore 0:
  40.5 40.8 all-gather.3
  83.2 35.5 all-gather.5
  381.0 123.8 all-reduce.1
  507.4 47.2 all-gather.7
where the time goes:
time: 565 us; the launch traced here: 564 us
  matrix products  221 us (39%)
  waiting for transfers between devices  207 us (37%)
  other arithmetic  60.5 us (11%)
  blocking collectives  58 us (10%)
  between operations  13.3 us (2%)
    dot_general x62, matrix products, product(): jnp.einsum(pattern, first_op, second_op, preferred_element_type=jnp.float32)  221 us
    pmax x1, waiting for transfers between devices, shards(): merged = lax.pmax(running, 'orient')  124 us
    all_gather x1, waiting for transfers between devices, shards(): collected = lax.all_gather(own_rows, 'tile', axis=0, tiled=True)  48.1 us
    max x12, other arithmetic, fold_step(): return (jnp.maximum(running, scores), None)  46 us
    all_gather x1, waiting for transfers between devices, shards(): part_im = lax.all_gather(slot_im, 'orient', axis=1, tiled=True)  33.3 us
    all_gather x1, blocking collectives, shards(): lax.all_gather(row_re, 'tile', axis=0, tiled=True)  29.6 us
    all_gather x1, blocking collectives, shards(): lax.all_gather(row_im, 'tile', axis=0, tiled=True)  28.4 us
    mul x12, other arithmetic, correlate(): proj_im * tile_im  12 us
  transfers between devices with their start and end apart: 4, of which 4 were waited for; matrix products, arithmetic and copies ran while one was open for 3% of the time, Pallas kernels for 0%

commit v1 on v0

v1 whole, which is shorter than its diff:
```python
import functools

import jax
import jax.numpy as jnp
import ml_dtypes
import numpy as np
from jax import lax
from jax.experimental import pallas as pl
from jax.experimental.pallas import tpu as pltpu
from jax.sharding import Mesh
from jax.sharding import PartitionSpec as P

BF = jnp.bfloat16
F32 = jnp.float32
S = 256
Q = 128
HR = 144
OD = 12
MAXB = 24


def tables():
    idx = np.arange(S)
    phase = 2.0 * np.pi * ((idx[:, None] * idx[None, :]) % S) / S
    cos = np.cos(phase).astype(ml_dtypes.bfloat16).astype(np.float32)
    sin = np.sin(phase).astype(ml_dtypes.bfloat16).astype(np.float32)
    return cos, sin


def constants():
    c, s = tables()
    cat = np.concatenate
    bf = lambda a: np.asarray(a, np.float32).astype(ml_dtypes.bfloat16)
    row = bf(cat([c, -s], 1))
    col = bf(cat([c, s], 1)[:HR])
    trow = bf(cat([c[:Q], -s[:Q]], 1))
    tcol = bf(cat([c[:, :Q], s[:, :Q]], 1)[:HR])
    inv1 = bf(cat([cat([c, s], 1), cat([-s, c], 1)], 0))
    wre = 2.0 * c[:, :Q]
    wre[:, 0] = c[:, 0]
    wim = -2.0 * s[:, :Q]
    wim[:, 0] = c[:, Q]
    inv2 = bf(cat([wre, wim], 1))
    flip = np.zeros((S, S), np.float32)
    flip[np.arange(S), (-np.arange(S)) % S] = 1.0
    return row, col, trow, tcol, inv1, inv2, bf(flip)


def dot(a, b):
    return jnp.dot(a, b, preferred_element_type=F32)


def filter_kernel(core_ref, f_ref, flip_ref, out_ref):
    f = f_ref[...]
    hi = f.astype(BF)
    lo = (f - hi.astype(F32)).astype(BF)
    flip = flip_ref[...]
    rows = flip[:HR]
    turned = dot(dot(rows, hi).astype(BF), flip) + dot(dot(rows, lo).astype(BF), flip)
    sym = (0.5 * (f[:HR] + turned)).astype(BF)
    out_ref[...] = jnp.where(core_ref[0] == 0, sym[:, :Q], sym[:, Q:])


def template_kernel(t_ref, trow_ref, tcol_ref, out_ref, nyq_ref, rhs_ref):
    count = t_ref.shape[0]
    rows = dot(t_ref[...].reshape(count * Q, Q), trow_ref[...]).astype(BF)
    for o in range(count):
        re = rows[o * Q : (o + 1) * Q, :S]
        im = rows[o * Q : (o + 1) * Q, S:]
        rhs_ref[o, :Q, :S] = re
        rhs_ref[o, :Q, S:] = im
        rhs_ref[o, Q:, :S] = im
        rhs_ref[o, Q:, S:] = -re
        spec = dot(tcol_ref[...], rhs_ref[o])
        out_ref[o] = spec[:Q].astype(BF)
        first = lax.broadcasted_iota(jnp.int32, (8, 2 * S), 0) == 0
        nyq_ref[o] = jnp.where(first, spec[Q : Q + 8].astype(BF).astype(F32), 0.0)


def main_kernel(
    meta_ref, img_ref, fil_ref, t0_ref, t1_ref, n0_ref, n1_ref,
    row_ref, col_ref, inv1_ref, inv2_ref,
    out_ref,
    x_ref, r_ref, h_ref, hn_ref, p_ref, q_ref, c_ref,
):
    step = pl.program_id(0)

    @pl.when(step == 0)
    def _():
        z, yl, core = meta_ref[0], meta_ref[1], meta_ref[2]
        for t in range(2):
            for zs in range(4):
                for ys in range(2):
                    for cs in range(2):
                        block = (
                            ((z - zs + 4) % 4) * 4
                            + (yl + ys) % 2 * 2
                            + (core + cs) % 2
                        )
                        at = pl.multiple_of(block * 16, 16)
                        x_ref[t, pl.ds(at, 16), :] = img_ref[zs, ys, cs, t]
        for t in range(2):
            rows = dot(x_ref[t], row_ref[...]).astype(BF)
            re, im = rows[:, :S], rows[:, S:]
            r_ref[:S, :S] = re
            r_ref[:S, S:] = im
            r_ref[S:, :S] = im
            r_ref[S:, S:] = -re
            spec = dot(col_ref[...], r_ref[...])
            slot = meta_ref[3 + t]
            f_lo = fil_ref[core, slot].astype(F32)
            f_hi = fil_ref[1 - core, slot].astype(F32)
            f = jnp.concatenate([f_lo, f_hi, f_lo, f_hi], axis=1)
            spec = spec * f
            h_ref[t] = spec[:Q]
            hn_ref[t] = spec[Q : Q + 8]
        out_ref[...] = jnp.full(out_ref.shape, -jnp.inf, F32)

    temps = [(t0_ref, n0_ref, k) for k in range(t0_ref.shape[0])]
    temps += [(t1_ref, n1_ref, k) for k in range(t1_ref.shape[0])]
    for t in range(2):
        hr, hi = h_ref[t, :, :S], h_ref[t, :, S:]
        mr, mi = hn_ref[t, :, :S], hn_ref[t, :, S:]
        for j, (t_ref, n_ref, k) in enumerate(temps):
            tr = t_ref[k, :, :S].astype(F32)
            ti = t_ref[k, :, S:].astype(F32)
            nr, ni = n_ref[k, :, :S], n_ref[k, :, S:]
            pr = tr * hr + ti * hi
            pi = tr * hi - ti * hr
            pr0 = pr[:8] - (nr * mi - ni * mr)
            pi0 = pi[:8] + (nr * mr + ni * mi)
            pr = jnp.concatenate([pr0, pr[8:]], axis=0)
            pi = jnp.concatenate([pi0, pi[8:]], axis=0)
            p_ref[j * Q : (j + 1) * Q, :S] = pr.astype(BF)
            p_ref[j * Q : (j + 1) * Q, S:] = pi.astype(BF)
        half = dot(p_ref[...], inv1_ref[...]).astype(BF)
        for j in range(len(temps)):
            q_ref[j, :Q] = half[j * Q : (j + 1) * Q, :S]
            q_ref[j, Q:] = half[j * Q : (j + 1) * Q, S:]
        for j in range(len(temps)):
            corr = dot(inv2_ref[...], q_ref[j])
            c_ref[j] = corr
            power = jnp.sum(corr * corr) * (1.0 / (S * S))
            scale = lax.rsqrt(power + 1e-06)
            best = out_ref[:, t].reshape(S, S)
            out_ref[:, t] = jnp.maximum(best, c_ref[j] * scale).reshape(16, 16, S)


def shards(tile_images, templates, filters, tile_bins):
    row, col, trow, tcol, inv1, inv2, flip = [jnp.asarray(a) for a in constants()]
    yh, x = lax.axis_index("yh"), lax.axis_index("x")
    z, yl, core = lax.axis_index("z"), lax.axis_index("yl"), lax.axis_index("c")
    swap = [(0, 1), (1, 0)]
    ring = lambda s: [(i, (i + s) % 4) for i in range(4)]
    core1 = core.reshape(1)
    smem = pl.BlockSpec(memory_space=pltpu.SMEM)
    vmem = pl.BlockSpec(memory_space=pltpu.VMEM)

    fil = pl.pallas_call(
        filter_kernel,
        out_shape=jax.ShapeDtypeStruct((HR, Q), BF),
        in_specs=[smem, vmem, vmem],
        out_specs=vmem,
        name="filter",
    )(core1, filters[0], flip)
    other_templates = lax.ppermute(templates, "c", swap)
    keep = lax.dynamic_slice_in_dim(tile_images, 2 * core, 2, 0)
    give = lax.dynamic_slice_in_dim(tile_images, 2 - 2 * core, 2, 0)
    img = jnp.stack([keep, lax.ppermute(give, "c", swap)])
    pairs = [(0, 3), (3, 0), (1, 2), (2, 1)]
    fil = jnp.stack([fil, lax.ppermute(fil, ("yh", "yl"), pairs)])
    img = jnp.stack([img, lax.ppermute(img, "yl", swap)])
    fil = jnp.stack([fil] + [lax.ppermute(fil, "x", ring(s)) for s in (1, 2, 3)])
    img = jnp.stack([img] + [lax.ppermute(img, "z", ring(s)) for s in (1, 2, 3)])
    fil = jnp.stack([fil, lax.ppermute(fil, "c", swap)]).reshape(2, 8, HR, Q)

    def spectra(t):
        return pl.pallas_call(
            template_kernel,
            grid=(3,),
            out_shape=(
                jax.ShapeDtypeStruct((OD, Q, 2 * S), BF),
                jax.ShapeDtypeStruct((OD, 8, 2 * S), F32),
            ),
            in_specs=[pl.BlockSpec((4, Q, Q), lambda i: (i, 0, 0)), vmem, vmem],
            out_specs=(
                pl.BlockSpec((4, Q, 2 * S), lambda i: (i, 0, 0)),
                pl.BlockSpec((4, 8, 2 * S), lambda i: (i, 0, 0)),
            ),
            scratch_shapes=[pltpu.VMEM((4, 2 * Q, 2 * S), BF)],
            cost_estimate=pl.CostEstimate(
                flops=OD * 2 * 40_000_000, bytes_accessed=2_000_000, transcendentals=0
            ),
            name="templates",
        )(t, trow, tcol)

    t0, n0 = spectra(templates)
    t1, n1 = spectra(other_templates)

    own = lax.dynamic_slice_in_dim(tile_bins, (yh * 4 + x) * 4 + 2 * core, 2, 0)
    slots = ((x - own % 4 + 4) % 4) * 2 + (own // 4 + yh) % 2
    meta = jnp.concatenate([jnp.stack([z, yl, core]), slots])

    nb = 2
    part = pl.pallas_call(
        main_kernel,
        grid=(OD // nb,),
        out_shape=jax.ShapeDtypeStruct((16, 2, 16, S), F32),
        in_specs=[
            smem, vmem, vmem,
            pl.BlockSpec((nb, Q, 2 * S), lambda i: (i, 0, 0)),
            pl.BlockSpec((nb, Q, 2 * S), lambda i: (i, 0, 0)),
            pl.BlockSpec((nb, 8, 2 * S), lambda i: (i, 0, 0)),
            pl.BlockSpec((nb, 8, 2 * S), lambda i: (i, 0, 0)),
            vmem, vmem, vmem, vmem,
        ],
        out_specs=pl.BlockSpec((16, 2, 16, S), lambda i: (0, 0, 0, 0)),
        scratch_shapes=[
            pltpu.VMEM((2, S, S), BF),
            pltpu.VMEM((2 * S, 2 * S), BF),
            pltpu.VMEM((2, Q, 2 * S), F32),
            pltpu.VMEM((2, 8, 2 * S), F32),
            pltpu.VMEM((2 * nb * Q, 2 * S), BF),
            pltpu.VMEM((2 * nb, S, S), BF),
            pltpu.VMEM((2 * nb, S, S), F32),
        ],
        compiler_params=pltpu.CompilerParams(vmem_limit_bytes=40 * 1024 * 1024),
        name="correlate",
    )(meta, img, fil, t0, t1, n0, n1, row, col, inv1, inv2)

    got = lax.all_to_all(part, ("z", "yl", "c"), 0, 0)
    return jnp.max(got.reshape(8, 4, 16, S), axis=0)


def solution(mesh):
    fine = Mesh(mesh.devices.reshape(2, 4, 4, 2, 2), ("yh", "x", "z", "yl", "c"))
    tile, orient = ("yh", "x"), ("z", "yl", "c")
    placed = (P(tile, orient, None), P(orient, None, None), P(tile, None, None), P())
    return jax.shard_map(
        shards, mesh=fine, in_specs=placed, out_specs=P(tile, orient, None), check_vma=False
    )
```

time: 565 us -> 60.6 us (0.11)
  matrix products: 221 us -> 0 us
  waiting for transfers between devices: 207 us -> 0.73 us
  other arithmetic: 60.5 us -> 3.38 us
  blocking collectives: 58 us -> 12.6 us
  Pallas kernels: 0 us -> 21.2 us
  starting transfers between devices: 0.31 us -> 18.9 us
  between operations: 13.3 us -> 0.18 us
    dot_general x62 -> x0, matrix products: 221 us -> none  [product(): jnp.einsum(pattern, first_op, second_op, preferred_element_type=jnp.float32)]
    pmax x1 -> x0, waiting for transfers between devices: 124 us -> none  [shards(): merged = lax.pmax(running, 'orient')]
    all_gather x3 -> x0, waiting for transfers between devices: 82.8 us -> none  [the longest x1 48.1 us: shards(): collected = lax.all_gather(own_rows, 'tile', axis=0, tiled=True)]
    all_gather x2 -> x0, blocking collectives: 58 us -> none  [the longest x1 29.6 us: shards(): lax.all_gather(row_re, 'tile', axis=0, tiled=True)]
    max x12 -> x0, other arithmetic: 46 us -> none  [fold_step(): return (jnp.maximum(running, scores), None)]
    pallas_call x0 -> x4, Pallas kernels: none -> 21.2 us  [the longest x1 11.2 us: shards(): pl.pallas_call(main_kernel, grid=(OD // nb,), out_shape=jax.ShapeDtypeStr...]
    ppermute x0 -> x11, starting transfers between devices: none -> 18.9 us  [the longest x3 6.35 us: shards(): lax.ppermute(img, 'z', ring(s))]
    all_to_all x0 -> x1, blocking collectives: none -> 12.6 us  [shards(): got = lax.all_to_all(part, ('z', 'yl', 'c'), 0, 0)]
  transfers between devices with their start and end apart: 4 -> 11, of which waited for: 4 -> 1; matrix products, arithmetic and copies ran while one was open for 3% -> 3% of each run, Pallas kernels for 0% -> 17%
where the time goes in v1:
time: 60.6 us; the launch traced here: 60.1 us
  Pallas kernels  21.2 us (35%)
  starting transfers between devices  18.9 us (31%)
  blocking collectives  12.6 us (21%)
  other arithmetic  3.38 us (6%)
  local copies, waits for them, and re-layouts  3.1 us (5%)
  waiting for transfers between devices  0.73 us (1%)
    all_to_all x1, blocking collectives, shards(): got = lax.all_to_all(part, ('z', 'yl', 'c'), 0, 0)  12.6 us
    pallas_call x1, Pallas kernels, shards(): pl.pallas_call(main_kernel, grid=(OD // nb,), out_shape=jax.ShapeDtypeStr...  11.2 us
    pallas_call x2, Pallas kernels, spectra(): pl.pallas_call(template_kernel, grid=(3,), out_shape=(jax.ShapeDtypeStruc...  7.97 us
    ppermute x3, starting transfers between devices, shards(): lax.ppermute(img, 'z', ring(s))  6.35 us
    ppermute x3, starting transfers between devices, shards(): lax.ppermute(fil, 'x', ring(s))  5.13 us
    ppermute x1, starting transfers between devices, shards(): fil = jnp.stack([fil, lax.ppermute(fil, 'c', swap)]).reshape(2, 8, HR, Q)  2.85 us
    ppermute x1, starting transfers between devices, shards(): fil = jnp.stack([fil, lax.ppermute(fil, ('yh', 'yl'), pairs)])  2.82 us
    unnamed x16, local copies, waits for them, and re-layouts  2.36 us
  transfers between devices with their start and end apart: 11, of which 1 were waited for; matrix products, arithmetic and copies ran while one was open for 3% of the time, Pallas kernels for 17%

profile of v1, /device:TPU:1, one launch (start us, length us, event | category | flops | bytes accessed | tf_op | source)
XLA Modules:
  0.0 60.1 jit_solution(5719026464002575734)
XLA Ops:
  0.0 0.7 %dynamic-slice_bitcast_fusion = (bf16[1,2,16,256]{3,2,1,0:T(8,128)(2,1)S(1)}, bf16[2,16,256]{2,1,0:T(8,128)(2,1)S(1)}) fusion(bf16[4,16,256]{2,1,0:T(8,128)(2,1)} %param.11, s32[]{:T(128)S(6)} %select_n.34, s32[]{:T(128)S(6)} %select_n.35), kind=kLoop, calls=%fused_computation.7 | loop fusion | bytes 65544 | tf_op jit(solution)/shard_map/stack | solution.py:169
  0.7 1.4 %collective-permute-start = (bf16[2,16,256]{2,1,0:T(8,128)(2,1)S(1)}, bf16[2,16,256]{2,1,0:T(8,128)(2,1)S(1)}, u32[]{:S(2)}, u32[]{:S(2)}) collective-permute-start(bf16[2,16,256]{2,1,0:T(8,128)(2,1)S(1)} %get-tuple-element.20), channel_id=1, source_target_pairs={{0,1},{1,0},{2,3},{3,2},{4,5},{5,4},{6,7},{7,6},{8,9},{9,8},{10,11... | collective-permute-start | bytes 49160 | tf_op jit(solution)/shard_map/ppermute | solution.py:169
  2.2 2.0 %filter.1 = bf16[144,128]{1,0:T(8,128)(2,1)} custom-call(s32[1]{0:T(128)} %bitcast.2.core_ref, f32[256,256]{1,0:T(8,128)} %bitcast.29, bf16[256,256]{1,0:T(8,128)(2,1)} %constant.90.clone.flip_ref), custom_call_target="tpu_custom_call" | custom-call | tf_op jit(solution)/shard_map/filter/pallas_call | solution.py:159
  4.1 2.8 %collective-permute-start.5 = (bf16[144,128]{1,0:T(8,128)(2,1)}, bf16[144,128]{1,0:T(8,128)(2,1)S(1)}, u32[]{:S(2)}, u32[]{:S(2)}) collective-permute-start(bf16[144,128]{1,0:T(8,128)(2,1)} %filter.1), channel_id=1, source_target_pairs={{0,66},{66,0},{2,64},{64,2},{1,67},{67,1},{3,65},{65,3},{4,70},{70... | collective-permute-start | bytes 110600 | tf_op jit(solution)/shard_map/ppermute | solution.py:171
  7.0 0.3 collective-permute-start.10
  7.3 0.7 %fusion = s32[2]{0:T(128)S(1)} fusion(s32[32]{0:T(128)} %param.14, s32[]{:T(128)S(6)} %select_n.29, s32[]{:T(128)S(6)} %axis_index.64, s32[]{:T(128)S(6)} %axis_index.61), kind=kLoop, calls=%fused_computation.19 | loop fusion | flops 92 | bytes 28 | tf_op jit(solution)/shard_map/add | solution.py:201
  8.0 0.1 pad_add_fusion.meta_ref
  8.1 0.0 collective-permute-done
  8.1 0.1 collective-permute-start.1
  8.2 0.7 %collective-permute-done.5 = bf16[144,128]{1,0:T(8,128)(2,1)S(1)} collective-permute-done((bf16[144,128]{1,0:T(8,128)(2,1)}, bf16[144,128]{1,0:T(8,128)(2,1)S(1)}, u32[]{:S(2)}, u32[]{:S(2)}) %collective-permute-start.5) | collective-permute-done | bytes 36896 | tf_op jit(solution)/shard_map/ppermute | solution.py:171
  8.9 0.8 %fusion.8 = (bf16[1,2,144,128]{3,2,1,0:T(8,128)(2,1)S(1)}, bf16[2,144,128]{2,1,0:T(8,128)(2,1)S(1)}) fusion(bf16[1,144,128]{2,1,0:T(8,128)(2,1)S(1)} %bitcast.37, bf16[1,144,128]{2,1,0:T(8,128)(2,1)} %bitcast.30), kind=kLoop, calls=%fused_computation.29 | loop fusion | flops 36864 | bytes 221184 | tf_op jit(solution)/shard_map/stack | solution.py:173
  9.7 2.5 %collective-permute-start.7 = (bf16[2,144,128]{2,1,0:T(8,128)(2,1)S(1)}, bf16[2,144,128]{2,1,0:T(8,128)(2,1)S(1)}, u32[]{:S(2)}, u32[]{:S(2)}) collective-permute-start(bf16[2,144,128]{2,1,0:T(8,128)(2,1)S(1)} %get-tuple-element.14), channel_id=1, source_target_pairs={{0,32},{16,48},{32,0},{48,16},{1,33},{17,49},{33,1},{49,17},{2,34}... | collective-permute-start | bytes 221192 | tf_op jit(solution)/shard_map/ppermute | solution.py:173
  12.1 0.3 collective-permute-start.6
  12.4 2.4 %collective-permute-start.8 = (bf16[2,144,128]{2,1,0:T(8,128)(2,1)S(1)}, bf16[2,144,128]{2,1,0:T(8,128)(2,1)S(1)}, u32[]{:S(2)}, u32[]{:S(2)}) collective-permute-start(bf16[2,144,128]{2,1,0:T(8,128)(2,1)S(1)} %get-tuple-element.14), channel_id=1, source_target_pairs={{0,48},{16,0},{32,16},{48,32},{1,49},{17,1},{33,17},{49,33},{2,50}... | collective-permute-start | bytes 221192 | tf_op jit(solution)/shard_map/ppermute | solution.py:173
  14.8 0.0 collective-permute-done.1
  14.8 3.7 %collective-permute-start.3 = (bf16[2,2,2,16,256]{4,3,2,1,0:T(8,128)(2,1)S(1)}, bf16[2,2,2,16,256]{4,3,2,1,0:T(8,128)(2,1)S(1)}, u32[]{:S(2)}, u32[]{:S(2)}) collective-permute-start(bf16[2,2,2,16,256]{4,3,2,1,0:T(8,128)(2,1)S(1)} %get-tuple-element.16), channel_id=1, source_target_pairs={{0,8},{4,12},{8,0},{12,4},{1,9},{5,13},{9,1},{13,5},{2,10},{6,14},... | collective-permute-start | bytes 196616 | tf_op jit(solution)/shard_map/ppermute | solution.py:174
  18.5 0.0 collective-permute-done.7
  18.5 0.7 %collective-permute-start.2 = (bf16[2,2,2,16,256]{4,3,2,1,0:T(8,128)(2,1)S(1)}, bf16[2,2,2,16,256]{4,3,2,1,0:T(8,128)(2,1)S(1)}, u32[]{:S(2)}, u32[]{:S(2)}) collective-permute-start(bf16[2,2,2,16,256]{4,3,2,1,0:T(8,128)(2,1)S(1)} %get-tuple-element.16), channel_id=1, source_target_pairs={{0,4},{4,8},{8,12},{12,0},{1,5},{5,9},{9,13},{13,1},{2,6},{6,10},{... | collective-permute-start | bytes 196616 | tf_op jit(solution)/shard_map/ppermute | solution.py:174
  19.2 0.0 collective-permute-done.6
  19.2 1.9 %collective-permute-start.4 = (bf16[2,2,2,16,256]{4,3,2,1,0:T(8,128)(2,1)S(1)}, bf16[2,2,2,16,256]{4,3,2,1,0:T(8,128)(2,1)S(1)}, u32[]{:S(2)}, u32[]{:S(2)}) collective-permute-start(bf16[2,2,2,16,256]{4,3,2,1,0:T(8,128)(2,1)S(1)} %get-tuple-element.16), channel_id=1, source_target_pairs={{0,12},{4,0},{8,4},{12,8},{1,13},{5,1},{9,5},{13,9},{2,14},{6,2},{... | collective-permute-start | bytes 196616 | tf_op jit(solution)/shard_map/ppermute | solution.py:174
  21.2 0.0 collective-permute-done.8
  21.2 2.9 %collective-permute-start.9 = (bf16[4,2,144,128]{3,2,1,0:T(8,128)(2,1)S(1)}, bf16[4,2,144,128]{3,2,1,0:T(8,128)(2,1)}, u32[]{:S(2)}, u32[]{:S(2)}) collective-permute-start(bf16[4,2,144,128]{3,2,1,0:T(8,128)(2,1)S(1)} %pad_maximum_fusion.1), channel_id=1, source_target_pairs={{0,1},{1,0},{2,3},{3,2},{4,5},{5,4},{6,7},{7,6},{8,9},{9,8},{10,11... | collective-permute-start | bytes 884744 | tf_op jit(solution)/shard_map/ppermute | solution.py:175
  24.1 3.9 %templates.2 = (bf16[12,128,512]{2,1,0:T(8,128)(2,1)}, f32[12,8,512]{2,1,0:T(8,128)}) custom-call(bf16[12,128,128]{2,1,0:T(8,128)(2,1)} %t_ref.1, bf16[128,512]{1,0:T(8,128)(2,1)} %constant.86.clone.trow_ref, bf16[144,256]{1,0:T(8,128)(2,1)} %constant.87.clone.tcol_ref), custom_call_target="tpu_custom_call" | custom-call | flops 960000000 | bytes 2000000 | tf_op jit(solution)/shard_map/templates/pallas_call | solution.py:178
  28.0 0.0 collective-permute-done.3
  28.0 0.0 collective-permute-done.2
  28.0 0.0 collective-permute-done.4
  28.0 0.0 copy-start
  28.1 0.0 copy-start.2
  28.1 0.0 copy-start.3
  28.1 0.0 copy-start.4
  28.1 0.0 copy-start.6
  28.1 0.0 copy-start.7
  28.1 0.0 collective-permute-done.10.t_ref
  28.1 4.1 %templates.3 = (bf16[12,128,512]{2,1,0:T(8,128)(2,1)}, f32[12,8,512]{2,1,0:T(8,128)}) custom-call(bf16[12,128,128]{2,1,0:T(8,128)(2,1)} %collective-permute-done.10.t_ref, bf16[128,512]{1,0:T(8,128)(2,1)} %constant.86.clone.trow_ref, bf16[144,256]{1,0:T(8,128)(2,1)} %constant.87.clone.tcol_ref), custom_call_target="tpu_custom_call" | custom-call | flops 960000000 | bytes 2000000 | tf_op jit(solution)/shard_map/templates/pallas_call | solution.py:178
  32.2 0.0 collective-permute-done.9
  32.2 1.0 %pad_maximum_fusion.fil_ref = bf16[2,8,144,128]{3,2,1,0:T(8,128)(2,1)S(1)} fusion(bf16[1,8,144,128]{3,2,1,0:T(8,128)(2,1)} %bitcast.19, bf16[1,8,144,128]{3,2,1,0:T(8,128)(2,1)S(1)} %bitcast.28), kind=kLoop, calls=%fused_computation | loop fusion | flops 294912 | bytes 1179648 | tf_op jit(solution)/shard_map/stack | solution.py:175
  33.2 0.0 copy-done
  33.2 0.0 copy-done.2
  33.2 0.0 copy-done.3
  33.3 0.0 copy-done.4
  33.3 0.0 copy-done.6
  33.3 0.0 copy-done.7
  33.3 0.0 copy-start.1
  33.3 1.4 %copy-done.1 = bf16[12,128,512]{2,1,0:T(8,128)(2,1)S(1)} copy-done((bf16[12,128,512]{2,1,0:T(8,128)(2,1)S(1)}, bf16[12,128,512]{2,1,0:T(8,128)(2,1)}, u32[]{:S(2)}) %copy-start.1) | copy-done | bytes 1572888
  34.7 0.9 %copy-done.5 = f32[12,8,512]{2,1,0:T(8,128)S(1)} copy-done((f32[12,8,512]{2,1,0:T(8,128)S(1)}, f32[12,8,512]{2,1,0:T(8,128)}, u32[]{:S(2)}) %copy-start.5) | copy-done | bytes 196632
  35.6 11.2 %correlate.1 = f32[16,2,16,256]{3,2,1,0:T(8,128)S(1)} custom-call(s32[5]{0:T(128)S(1)} %pad_add_fusion.meta_ref, bf16[4,2,2,2,16,256]{5,4,3,2,1,0:T(8,128)(2,1)S(1)} %pad_maximum_fusion.2.img_ref, bf16[2,8,144,128]{3,2,1,0:T(8,128)(2,1)S(1)} %pad_maximum_fusion.fil_ref, bf16[12,128,512]{2,1,0:T(8,128)(2,1)S(1)} %copy-done, ...), custom_call_target="tpu_custom_call" | custom-call | tf_op jit(solution)/shard_map/correlate/pallas_call | solution.py:205
  46.8 12.6 %all_to_all.5 = f32[16,2,16,256]{3,2,1,0:T(8,128)S(1)} all-to-all(f32[16,2,16,256]{3,2,1,0:T(8,128)S(1)} %correlate.1), channel_id=1, replica_groups=mesh['yh'=2,'x'=4,'z'=4,'yl'=2,'c'=2] {'z','yl','c'}, dimensions={0} | all-to-all | bytes 1048576 | tf_op jit(solution)/shard_map/all_to_all | solution.py:231
  59.4 0.7 %bitcast_reduce_fusion = f32[4,16,256]{2,1,0:T(8,128)} fusion(f32[8,4,16,256]{3,2,1,0:T(8,128)S(1)} %bitcast.27), kind=kLoop, calls=%fused_computation.1 | loop fusion | flops 114688 | bytes 589824 | tf_op jit(solution)/shard_map/reduce_max | solution.py:232
  (5 shorter events, 0.1 us)
Async XLA Ops:
  0.7 7.3 %collective-permute-start = (bf16[2,16,256]{2,1,0:T(8,128)(2,1)S(1)}, bf16[2,16,256]{2,1,0:T(8,128)(2,1)S(1)}, u32[]{:S(2)}, u32[]{:S(2)}) collective-permute-start(bf16[2,16,256]{2,1,0:T(8,128)(2,1)S(1)} %get-tuple-element.20), channel_id=1, source_target_pairs={{0,1},{1,0},{2,3},{3,2},{4,5},{5,4},{6,7},{7,6},{8,9},{9,8},{10,11... | collective-permute-start | bytes 49160 | tf_op jit(solution)/shard_map/ppermute | solution.py:169
  4.1 4.7 %collective-permute-start.5 = (bf16[144,128]{1,0:T(8,128)(2,1)}, bf16[144,128]{1,0:T(8,128)(2,1)S(1)}, u32[]{:S(2)}, u32[]{:S(2)}) collective-permute-start(bf16[144,128]{1,0:T(8,128)(2,1)} %filter.1), channel_id=1, source_target_pairs={{0,66},{66,0},{2,64},{64,2},{1,67},{67,1},{3,65},{65,3},{4,70},{70... | collective-permute-start | bytes 110600 | tf_op jit(solution)/shard_map/ppermute | solution.py:171
  7.0 21.2 %collective-permute-start.10 = (bf16[12,128,128]{2,1,0:T(8,128)(2,1)}, bf16[12,128,128]{2,1,0:T(8,128)(2,1)}, u32[]{:S(2)}, u32[]{:S(2)}) collective-permute-start(bf16[12,128,128]{2,1,0:T(8,128)(2,1)} %t_ref.1), channel_id=1, source_target_pairs={{0,1},{1,0},{2,3},{3,2},{4,5},{5,4},{6,7},{7,6},{8,9},{9,8},{10,11... | collective-permute-start | bytes 1179656 | tf_op jit(solution)/shard_map/ppermute | solution.py:166
  8.1 6.7 %collective-permute-start.1 = (bf16[2,2,16,256]{3,2,1,0:T(8,128)(2,1)S(1)}, bf16[2,2,16,256]{3,2,1,0:T(8,128)(2,1)S(1)}, u32[]{:S(2)}, u32[]{:S(2)}) collective-permute-start(bf16[2,2,16,256]{3,2,1,0:T(8,128)(2,1)S(1)} %get-tuple-element.18), channel_id=1, source_target_pairs={{0,2},{2,0},{1,3},{3,1},{4,6},{6,4},{5,7},{7,5},{8,10},{10,8},{9,1... | collective-permute-start | bytes 98312 | tf_op jit(solution)/shard_map/ppermute | solution.py:172
  9.7 8.8 %collective-permute-start.7 = (bf16[2,144,128]{2,1,0:T(8,128)(2,1)S(1)}, bf16[2,144,128]{2,1,0:T(8,128)(2,1)S(1)}, u32[]{:S(2)}, u32[]{:S(2)}) collective-permute-start(bf16[2,144,128]{2,1,0:T(8,128)(2,1)S(1)} %get-tuple-element.14), channel_id=1, source_target_pairs={{0,32},{16,48},{32,0},{48,16},{1,33},{17,49},{33,1},{49,17},{2,34}... | collective-permute-start | bytes 221192 | tf_op jit(solution)/shard_map/ppermute | solution.py:173
  12.1 7.1 %collective-permute-start.6 = (bf16[2,144,128]{2,1,0:T(8,128)(2,1)S(1)}, bf16[2,144,128]{2,1,0:T(8,128)(2,1)S(1)}, u32[]{:S(2)}, u32[]{:S(2)}) collective-permute-start(bf16[2,144,128]{2,1,0:T(8,128)(2,1)S(1)} %get-tuple-element.14), channel_id=1, source_target_pairs={{0,16},{16,32},{32,48},{48,0},{1,17},{17,33},{33,49},{49,1},{2,18}... | collective-permute-start | bytes 221192 | tf_op jit(solution)/shard_map/ppermute | solution.py:173
  12.4 8.7 %collective-permute-start.8 = (bf16[2,144,128]{2,1,0:T(8,128)(2,1)S(1)}, bf16[2,144,128]{2,1,0:T(8,128)(2,1)S(1)}, u32[]{:S(2)}, u32[]{:S(2)}) collective-permute-start(bf16[2,144,128]{2,1,0:T(8,128)(2,1)S(1)} %get-tuple-element.14), channel_id=1, source_target_pairs={{0,48},{16,0},{32,16},{48,32},{1,49},{17,1},{33,17},{49,33},{2,50}... | collective-permute-start | bytes 221192 | tf_op jit(solution)/shard_map/ppermute | solution.py:173
  14.8 13.2 %collective-permute-start.3 = (bf16[2,2,2,16,256]{4,3,2,1,0:T(8,128)(2,1)S(1)}, bf16[2,2,2,16,256]{4,3,2,1,0:T(8,128)(2,1)S(1)}, u32[]{:S(2)}, u32[]{:S(2)}) collective-permute-start(bf16[2,2,2,16,256]{4,3,2,1,0:T(8,128)(2,1)S(1)} %get-tuple-element.16), channel_id=1, source_target_pairs={{0,8},{4,12},{8,0},{12,4},{1,9},{5,13},{9,1},{13,5},{2,10},{6,14},... | collective-permute-start | bytes 196616 | tf_op jit(solution)/shard_map/ppermute | solution.py:174
  18.5 9.5 %collective-permute-start.2 = (bf16[2,2,2,16,256]{4,3,2,1,0:T(8,128)(2,1)S(1)}, bf16[2,2,2,16,256]{4,3,2,1,0:T(8,128)(2,1)S(1)}, u32[]{:S(2)}, u32[]{:S(2)}) collective-permute-start(bf16[2,2,2,16,256]{4,3,2,1,0:T(8,128)(2,1)S(1)} %get-tuple-element.16), channel_id=1, source_target_pairs={{0,4},{4,8},{8,12},{12,0},{1,5},{5,9},{9,13},{13,1},{2,6},{6,10},{... | collective-permute-start | bytes 196616 | tf_op jit(solution)/shard_map/ppermute | solution.py:174
  19.2 8.7 %collective-permute-start.4 = (bf16[2,2,2,16,256]{4,3,2,1,0:T(8,128)(2,1)S(1)}, bf16[2,2,2,16,256]{4,3,2,1,0:T(8,128)(2,1)S(1)}, u32[]{:S(2)}, u32[]{:S(2)}) collective-permute-start(bf16[2,2,2,16,256]{4,3,2,1,0:T(8,128)(2,1)S(1)} %get-tuple-element.16), channel_id=1, source_target_pairs={{0,12},{4,0},{8,4},{12,8},{1,13},{5,1},{9,5},{13,9},{2,14},{6,2},{... | collective-permute-start | bytes 196616 | tf_op jit(solution)/shard_map/ppermute | solution.py:174
  21.2 11.0 %collective-permute-start.9 = (bf16[4,2,144,128]{3,2,1,0:T(8,128)(2,1)S(1)}, bf16[4,2,144,128]{3,2,1,0:T(8,128)(2,1)}, u32[]{:S(2)}, u32[]{:S(2)}) collective-permute-start(bf16[4,2,144,128]{3,2,1,0:T(8,128)(2,1)S(1)} %pad_maximum_fusion.1), channel_id=1, source_target_pairs={{0,1},{1,0},{2,3},{3,2},{4,5},{5,4},{6,7},{7,6},{8,9},{9,8},{10,11... | collective-permute-start | bytes 884744 | tf_op jit(solution)/shard_map/ppermute | solution.py:175
  28.0 5.2 %copy-start = (bf16[12,128,512]{2,1,0:T(8,128)(2,1)S(1)}, bf16[12,128,512]{2,1,0:T(8,128)(2,1)}, u32[]{:S(2)}) copy-start(bf16[12,128,512]{2,1,0:T(8,128)(2,1)} %get-tuple-element.9.t0_ref) | copy-start | bytes 4718596
  28.1 5.2 %copy-start.2 = (bf16[512,512]{1,0:T(8,128)(2,1)S(1)}, bf16[512,512]{1,0:T(8,128)(2,1)}, u32[]{:S(2)}) copy-start(bf16[512,512]{1,0:T(8,128)(2,1)} %constant.88.clone.inv1_ref) | copy-start | bytes 1572868
  28.1 5.2 %copy-start.3 = (bf16[256,512]{1,0:T(8,128)(2,1)S(1)}, bf16[256,512]{1,0:T(8,128)(2,1)}, u32[]{:S(2)}) copy-start(bf16[256,512]{1,0:T(8,128)(2,1)} %constant.84.clone.row_ref) | copy-start | bytes 786436
  28.1 5.2 %copy-start.4 = (f32[12,8,512]{2,1,0:T(8,128)S(1)}, f32[12,8,512]{2,1,0:T(8,128)}, u32[]{:S(2)}) copy-start(f32[12,8,512]{2,1,0:T(8,128)} %get-tuple-element.11.n0_ref) | copy-start | bytes 589828
  28.1 5.2 %copy-start.6 = (bf16[144,512]{1,0:T(8,128)(2,1)S(1)}, bf16[144,512]{1,0:T(8,128)(2,1)}, u32[]{:S(2)}) copy-start(bf16[144,512]{1,0:T(8,128)(2,1)} %constant.85.clone.col_ref) | copy-start | bytes 442372
  28.1 5.2 %copy-start.7 = (bf16[256,256]{1,0:T(8,128)(2,1)S(1)}, bf16[256,256]{1,0:T(8,128)(2,1)}, u32[]{:S(2)}) copy-start(bf16[256,256]{1,0:T(8,128)(2,1)} %constant.89.clone.inv2_ref) | copy-start | bytes 393220
  33.3 1.4 %copy-start.1 = (bf16[12,128,512]{2,1,0:T(8,128)(2,1)S(1)}, bf16[12,128,512]{2,1,0:T(8,128)(2,1)}, u32[]{:S(2)}) copy-start(bf16[12,128,512]{2,1,0:T(8,128)(2,1)} %get-tuple-element.10.t1_ref) | copy-start | bytes 4718596
  34.7 0.9 %copy-start.5 = (f32[12,8,512]{2,1,0:T(8,128)S(1)}, f32[12,8,512]{2,1,0:T(8,128)}, u32[]{:S(2)}) copy-start(f32[12,8,512]{2,1,0:T(8,128)} %get-tuple-element.12.n1_ref) | copy-start | bytes 589828

commit v2 on v1

v2 whole, which is shorter than its diff:
```python
import jax
import jax.numpy as jnp
import ml_dtypes
import numpy as np
from jax import lax
from jax.experimental import pallas as pl
from jax.experimental.pallas import tpu as pltpu
from jax.sharding import Mesh
from jax.sharding import PartitionSpec as P

BF = jnp.bfloat16
F32 = jnp.float32
S = 256
Q = 128
HR = 144
OD = 12
NB = 3
RC = 32
MIB = 1024 * 1024


def tables():
    idx = np.arange(S)
    phase = 2.0 * np.pi * ((idx[:, None] * idx[None, :]) % S) / S
    cos = np.cos(phase).astype(ml_dtypes.bfloat16).astype(np.float32)
    sin = np.sin(phase).astype(ml_dtypes.bfloat16).astype(np.float32)
    return cos, sin


def constants():
    c, s = tables()
    cat = np.concatenate
    bf = lambda a: np.asarray(a, np.float32).astype(ml_dtypes.bfloat16)
    row = bf(cat([c, -s], 1))
    col = bf(cat([c, s], 1)[:HR])
    trow = bf(cat([c[:Q], -s[:Q]], 1))
    tcol = bf(cat([c[:, :Q], s[:, :Q]], 1)[:HR])
    inv1 = bf(cat([cat([c, s], 1), cat([-s, c], 1)], 0))
    wre = 2.0 * c[:, :Q]
    wre[:, 0] = c[:, 0]
    wim = -2.0 * s[:, :Q]
    wim[:, 0] = c[:, Q]
    inv2 = bf(cat([wre, wim], 1))
    return row, col, trow, tcol, inv1, inv2


def dot(a, b):
    return jnp.dot(a, b, preferred_element_type=F32)


def place(index):
    return index // 64, index // 16 % 4, index // 4 % 4, index // 2 % 2, index % 2


def fetch(pairs, sems):
    copies = [pltpu.make_async_copy(a, b, sems.at[i]) for i, (a, b) in enumerate(pairs)]
    for copy in copies:
        copy.start()
    return copies


def prep_kernel(
    index_ref, f_hbm, img_hbm, t_hbm, trow_hbm, tcol_hbm,
    fil_ref, split_ref, t_ref, trow_ref, tcol_ref,
    f_ref, img_ref, sems,
):
    core = index_ref[0] % 2
    copies = fetch(
        [
            (img_hbm, img_ref),
            (f_hbm, f_ref),
            (t_hbm, t_ref),
            (trow_hbm, trow_ref),
            (tcol_hbm, tcol_ref),
        ],
        sems,
    )
    a = lax.broadcasted_iota(jnp.int32, (S, S), 0)
    b = lax.broadcasted_iota(jnp.int32, (S, S), 1)
    flip = jnp.where((a + b) % S == 0, 1.0, 0.0).astype(BF)
    copies[0].wait()
    split_ref[0] = img_ref[pl.ds(2 * core, 2)]
    split_ref[1] = img_ref[pl.ds(2 - 2 * core, 2)]
    copies[1].wait()
    f = f_ref[0]
    hi = f.astype(BF)
    lo = (f - hi.astype(F32)).astype(BF)
    rows = flip[:HR]
    turned = dot(dot(rows, hi).astype(BF), flip) + dot(dot(rows, lo).astype(BF), flip)
    sym = (0.5 * (f[:HR] + turned)).astype(BF)
    fil_ref[...] = jnp.where(core == 0, sym[:, :Q], sym[:, Q:])
    for copy in copies[2:]:
        copy.wait()


def template_kernel(t_ref, trow_ref, tcol_ref, out_ref, nyq_ref, rhs_ref):
    count = t_ref.shape[0]
    rows = dot(t_ref[...].reshape(count * Q, Q), trow_ref[...]).astype(BF)
    for o in range(count):
        re = rows[o * Q : (o + 1) * Q, :S]
        im = rows[o * Q : (o + 1) * Q, S:]
        rhs_ref[o, :Q, :S] = re
        rhs_ref[o, :Q, S:] = im
        rhs_ref[o, Q:, :S] = im
        rhs_ref[o, Q:, S:] = -re
    first = lax.broadcasted_iota(jnp.int32, (8, 2 * S), 0) == 0
    for o in range(count):
        spec = dot(tcol_ref[...], rhs_ref[o])
        out_ref[o] = spec[:Q].astype(BF)
        nyq_ref[o] = jnp.where(first, spec[Q : Q + 8].astype(BF).astype(F32), 0.0)


def tile_kernel(index_ref, *refs):
    imgs, (row_ref, col_ref, spec_ref, x_ref, r_ref) = refs[:2], refs[2:]
    _, _, z, yl, core = place(index_ref[0])
    for t in range(2):
        for zs in range(4):
            for ys in range(2):
                for cs in range(2):
                    side = z if zs < 2 else 3 - z
                    if zs % 2:
                        side = side + 1 - side % 2 * 2
                    block = side * 4 + (yl + ys) % 2 * 2 + (core + cs) % 2
                    at = pl.multiple_of(block * 16, 16)
                    x_ref[t, pl.ds(at, 16), :] = imgs[cs][ys, zs // 2, zs % 2, t]
    for t in range(2):
        rows = dot(x_ref[t], row_ref[...]).astype(BF)
        re, im = rows[:, :S], rows[:, S:]
        r_ref[t, :S, :S] = re
        r_ref[t, :S, S:] = im
        r_ref[t, S:, :S] = im
        r_ref[t, S:, S:] = -re
    for t in range(2):
        spec_ref[t] = dot(col_ref[...], r_ref[t])


def main_kernel(
    index_ref, bins_ref, spec_ref, fa_ref, fb_ref,
    t0_ref, t1_ref, n0_ref, n1_ref, inv1_ref, inv2_ref,
    out_ref,
    h_ref, hn_ref, p_ref, q_ref, c_ref, s_ref,
):
    yh, x, _, _, core = place(index_ref[0])
    for t in range(2):
        name = bins_ref[(yh * 4 + x) * 4 + 2 * core + t]
        xs = (x // 2 + name % 4 // 2) % 2
        xn = (x + name + xs) % 2
        ys = (name // 4 + yh) % 2
        fa = fa_ref[xs, xn, ys].astype(F32)
        fb = fb_ref[xs, xn, ys].astype(F32)
        lo = jnp.where(core == 0, fa, fb)
        hi = jnp.where(core == 0, fb, fa)
        spec = spec_ref[t] * jnp.concatenate([lo, hi, lo, hi], axis=1)
        h_ref[t] = spec[:Q]
        hn_ref[t] = spec[Q : Q + 8]
    out_ref[...] = jnp.full(out_ref.shape, -jnp.inf, F32)

    count = 4 * NB

    def chunk(k, carry):
        for b in range(NB):
            o = k * NB + b
            for i, (t_ref, n_ref) in enumerate(((t0_ref, n0_ref), (t1_ref, n1_ref))):
                for r in range(0, Q, 16):
                    rows = slice(r, r + 16)
                    tr = t_ref[o, rows, :S].astype(F32)
                    ti = t_ref[o, rows, S:].astype(F32)
                    for t in range(2):
                        at = (b * 4 + i * 2 + t) * Q + r
                        hr, hi = h_ref[t, rows, :S], h_ref[t, rows, S:]
                        pr = tr * hr + ti * hi
                        pi = tr * hi - ti * hr
                        if r == 0:
                            nr, ni = n_ref[o, :, :S], n_ref[o, :, S:]
                            mr, mi = hn_ref[t, :, :S], hn_ref[t, :, S:]
                            pr0 = pr[:8] - (nr * mi - ni * mr)
                            pi0 = pi[:8] + (nr * mr + ni * mi)
                            pr = jnp.concatenate([pr0, pr[8:]], axis=0)
                            pi = jnp.concatenate([pi0, pi[8:]], axis=0)
                        p_ref[at : at + 16, :S] = pr.astype(BF)
                        p_ref[at : at + 16, S:] = pi.astype(BF)
        half = dot(p_ref[...], inv1_ref[...]).astype(BF)
        for j in range(count):
            q_ref[j, :Q] = half[j * Q : (j + 1) * Q, :S]
            q_ref[j, Q:] = half[j * Q : (j + 1) * Q, S:]
        for j in range(count):
            c_ref[j] = dot(inv2_ref[...], q_ref[j])
            power = jnp.zeros((8, Q), F32)
            for r in range(0, S, RC):
                part = c_ref[j, r : r + RC]
                part = part * part
                power += jnp.sum((part[:, :Q] + part[:, Q:]).reshape(RC // 8, 8, Q), axis=0)
            s_ref[j] = power
        total = jnp.sum(jnp.sum(s_ref[...], axis=1), axis=1, keepdims=True)
        scale = lax.rsqrt(total * (1.0 / (S * S)) + 1e-06)
        scales = [jnp.broadcast_to(scale[j : j + 1], (8, Q)) for j in range(count)]
        for t in range(2):
            for r in range(0, S, RC):
                spots = [(r + a, l * Q) for a in range(0, RC, 8) for l in range(2)]
                view = [
                    (row // 16, t, slice(row % 16, row % 16 + 8), slice(lane, lane + Q))
                    for row, lane in spots
                ]
                best = [out_ref[v] for v in view]
                for j in range(t, count, 2):
                    for i, (row, lane) in enumerate(spots):
                        corr = c_ref[j, row : row + 8, lane : lane + Q]
                        best[i] = jnp.maximum(best[i], corr * scales[j])
                for v, value in zip(view, best):
                    out_ref[v] = value
        return carry

    lax.fori_loop(0, OD // NB, chunk, 0)


def shards(tile_images, templates, filters, tile_bins):
    row, col, trow, tcol, inv1, inv2 = [jnp.asarray(a) for a in constants()]
    index = lax.axis_index(("yh", "x", "z", "yl", "c")).reshape(1)
    swap = [(0, 1), (1, 0)]
    ring = lambda s: [(i, (i + s) % 4) for i in range(4)]
    smem = pl.BlockSpec(memory_space=pltpu.SMEM)
    vmem = pl.BlockSpec(memory_space=pltpu.VMEM)
    hbm = pl.BlockSpec(memory_space=pltpu.HBM)
    tie = lax.optimization_barrier

    def spectra(t):
        return pl.pallas_call(
            template_kernel,
            out_shape=(
                jax.ShapeDtypeStruct((OD, Q, 2 * S), BF),
                jax.ShapeDtypeStruct((OD, 8, 2 * S), F32),
            ),
            in_specs=[vmem, vmem, vmem],
            out_specs=(vmem, vmem),
            scratch_shapes=[pltpu.VMEM((OD, 2 * Q, 2 * S), BF)],
            compiler_params=pltpu.CompilerParams(vmem_limit_bytes=16 * MIB),
            cost_estimate=pl.CostEstimate(
                flops=OD * 90_000_000, bytes_accessed=2_000_000, transcendentals=0
            ),
            name="templates",
        )(t, trow, tcol)

    like = lambda a: jax.ShapeDtypeStruct(a.shape, a.dtype)
    far = lambda a: pltpu.with_memory_space_constraint(a, pltpu.HBM)
    fil, img, own_templates, trow, tcol = pl.pallas_call(
        prep_kernel,
        out_shape=(
            jax.ShapeDtypeStruct((HR, Q), BF),
            jax.ShapeDtypeStruct((2, 2, 16, S), BF),
            like(templates),
            like(trow),
            like(tcol),
        ),
        in_specs=[smem] + [hbm] * 5,
        out_specs=(vmem,) * 5,
        scratch_shapes=[
            pltpu.VMEM((1, S, S), F32),
            pltpu.VMEM((4, 16, S), BF),
            pltpu.SemaphoreType.DMA((5,)),
        ],
        compiler_params=pltpu.CompilerParams(vmem_limit_bytes=8 * MIB),
        name="prep",
    )(index, far(filters), far(tile_images), far(templates), far(trow), far(tcol))
    near, across = [(0, 1), (1, 0), (2, 3), (3, 2)], [(0, 3), (3, 0), (1, 2), (2, 1)]
    fil_y = lax.ppermute(fil, ("yh", "yl"), across)
    img_z = lax.ppermute(img, "z", near)
    other_templates = lax.ppermute(own_templates, "c", swap)
    t0, n0 = spectra(own_templates)
    other_templates, img_z, fil_y, t0, n0 = tie((other_templates, img_z, fil_y, t0, n0))
    fil = jnp.stack([fil, fil_y])
    img = jnp.stack([img, img_z], axis=1)
    fil_x = lax.ppermute(fil, "x", near)
    img_z = lax.ppermute(img, "z", across)
    t1, n1 = spectra(other_templates)
    fil_x, img_z, t1, n1 = tie((fil_x, img_z, t1, n1))
    fil = jnp.stack([fil, fil_x])
    img = jnp.stack([img, img_z], axis=1)
    fil_x = lax.ppermute(fil, "x", across)
    img_y = lax.ppermute(img, "yl", swap)
    fil_x, img_y = tie((fil_x, img_y))
    fil_a = jnp.stack([fil, fil_x])
    img_a = jnp.stack([img, img_y], axis=1)
    img_b = lax.ppermute(img_a[1], "c", swap)
    fil_b = lax.ppermute(fil_a, "c", swap)
    spec = pl.pallas_call(
        tile_kernel,
        out_shape=jax.ShapeDtypeStruct((2, HR, 2 * S), F32),
        in_specs=[smem] + [vmem] * 4,
        out_specs=vmem,
        scratch_shapes=[pltpu.VMEM((2, S, S), BF), pltpu.VMEM((2, 2 * S, 2 * S), BF)],
        compiler_params=pltpu.CompilerParams(vmem_limit_bytes=8 * MIB),
        cost_estimate=pl.CostEstimate(
            flops=800_000_000, bytes_accessed=1_000_000, transcendentals=0
        ),
        name="tiles",
    )(index, img_a[0], img_b, row, col)
    fil_b, spec = tie((fil_b, spec))

    count = 4 * NB
    part = pl.pallas_call(
        main_kernel,
        out_shape=jax.ShapeDtypeStruct((16, 2, 16, S), F32),
        in_specs=[smem, smem] + [vmem] * 9,
        out_specs=vmem,
        scratch_shapes=[
            pltpu.VMEM((2, Q, 2 * S), F32),
            pltpu.VMEM((2, 8, 2 * S), F32),
            pltpu.VMEM((count * Q, 2 * S), BF),
            pltpu.VMEM((count, S, S), BF),
            pltpu.VMEM((count, S, S), F32),
            pltpu.VMEM((count, 8, Q), F32),
        ],
        compiler_params=pltpu.CompilerParams(vmem_limit_bytes=24 * MIB),
        name="correlate",
    )(index, tile_bins, spec, fil_a, fil_b, t0, t1, n0, n1, inv1, inv2)

    got = lax.all_to_all(part.astype(jnp.float16), ("z", "yl", "c"), 0, 0)
    return jnp.max(got.astype(F32).reshape(8, 4, 16, S), axis=0)


def solution(mesh):
    fine = Mesh(mesh.devices.reshape(2, 4, 4, 2, 2), ("yh", "x", "z", "yl", "c"))
    tile, orient = ("yh", "x"), ("z", "yl", "c")
    placed = (P(tile, orient, None), P(orient, None, None), P(tile, None, None), P())
    return jax.shard_map(
        shards, mesh=fine, in_specs=placed, out_specs=P(tile, orient, None), check_vma=False
    )
```

time: 60.6 us -> 45.8 us (0.76)
  Pallas kernels: 21.2 us -> 11.5 us
  waiting for transfers between devices: 0.73 us -> 6.71 us
  local copies, waits for them, and re-layouts: 3.1 us -> 0.03 us
  blocking collectives: 12.6 us -> 9.92 us
  other arithmetic: 3.38 us -> 0.83 us
  starting transfers between devices: 18.9 us -> 16.4 us
    pallas_call x4 -> x5, Pallas kernels: 21.2 us -> 11.5 us  [the longest x1 7.57 us: shards(): pl.pallas_call(main_kernel, out_shape=jax.ShapeDtypeStruct((16, 2, 16, S)...]
    ppermute x11 -> x9, waiting for transfers between devices: 0.73 us -> 6.71 us  [the longest x1 3.8 us: shards(): img_y = lax.ppermute(img, 'yl', swap)]
    all_to_all x1, blocking collectives: 12.6 us -> 9.92 us  [shards(): got = lax.all_to_all(part.astype(jnp.float16), ('z', 'yl', 'c'), 0, 0)]
    ppermute x11 -> x9, starting transfers between devices: 18.9 us -> 16.4 us  [the longest x1 4.09 us: shards(): fil_b = lax.ppermute(fil_a, 'c', swap)]
    unnamed x16 -> x10, local copies, waits for them, and re-layouts: 2.36 us -> 0.03 us
    another operation x6 -> x5, other arithmetic: 1.89 us -> 0.09 us  [the longest x2 0.05 us: shards(): fil_a = jnp.stack([fil, fil_x])]
    add x1 -> x0, other arithmetic: 0.75 us -> none  [shards(): slots = (x - own % 4 + 4) % 4 * 2 + (own // 4 + yh) % 2]
    another operation x1 -> x0, local copies, waits for them, and re-layouts: 0.74 us -> none  [shards(): img = jnp.stack([keep, lax.ppermute(give, 'c', swap)])]
  transfers between devices with their start and end apart: 11 -> 9, of which waited for: 1 -> 4; matrix products, arithmetic and copies ran while one was open for 3% -> 0% of each run, Pallas kernels for 17% -> 6%
where the time goes in v2:
time: 45.8 us; the launch traced here: 45.6 us
  starting transfers between devices  16.4 us (36%)
  Pallas kernels  11.5 us (25%)
  blocking collectives  9.92 us (22%)
  waiting for transfers between devices  6.71 us (15%)
  other arithmetic  0.83 us (2%)
    all_to_all x1, blocking collectives, shards(): got = lax.all_to_all(part.astype(jnp.float16), ('z', 'yl', 'c'), 0, 0)  9.92 us
    pallas_call x1, Pallas kernels, shards(): pl.pallas_call(main_kernel, out_shape=jax.ShapeDtypeStruct((16, 2, 16, S)...  7.57 us
    ppermute x1, starting transfers between devices, shards(): fil_b = lax.ppermute(fil_a, 'c', swap)  4.09 us
    ppermute x1, waiting for transfers between devices, shards(): img_y = lax.ppermute(img, 'yl', swap)  3.8 us
    ppermute x1, starting transfers between devices, shards(): fil_y = lax.ppermute(fil, ('yh', 'yl'), across)  2.73 us
    ppermute x1, starting transfers between devices, shards(): fil_x = lax.ppermute(fil, 'x', across)  2.56 us
    ppermute x1, starting transfers between devices, shards(): img_z = lax.ppermute(img, 'z', across)  2.32 us
    pallas_call x2, Pallas kernels, spectra(): pl.pallas_call(template_kernel, out_shape=(jax.ShapeDtypeStruct((OD, Q, 2...  2.01 us
  transfers between devices with their start and end apart: 9, of which 4 were waited for; matrix products, arithmetic and copies ran while one was open for 0% of the time, Pallas kernels for 6%

profile of v2, /device:TPU:1, one launch (start us, length us, event | category | flops | bytes accessed | tf_op | source)
XLA Modules:
  0.0 45.6 jit_solution(18373597178320733119)
XLA Ops:
  0.0 1.4 %prep.1 = (bf16[144,128]{1,0:T(8,128)(2,1)S(1)}, bf16[2,2,16,256]{3,2,1,0:T(8,128)(2,1)S(1)}, bf16[12,128,128]{2,1,0:T(8,128)(2,1)S(1)}, bf16[128,512]{1,0:T(8,128)(2,1)S(1)}, bf16[144,256]{1,0:T(8,128)(2,1)S(1)}) custom-call(s32[1]{0:T(128)} %bitcast.index_ref, f32[1,256,256]{2,1,0:T(8,128)} %f_hbm.1, bf16[4,16,256]{2,1,0:T(8,128)(2,1)} %img_hbm.1, ...), custom_call_target="tpu_custom_call" | custom-call | tf_op jit(solution)/shard_map/prep/pallas_call | solution.py:245
  1.4 1.5 %collective-permute-start = (bf16[12,128,128]{2,1,0:T(8,128)(2,1)S(1)}, bf16[12,128,128]{2,1,0:T(8,128)(2,1)S(1)}, u32[]{:S(2)}, u32[]{:S(2)}) collective-permute-start(bf16[12,128,128]{2,1,0:T(8,128)(2,1)S(1)} %get-tuple-element.28.t_ref), channel_id=1, source_target_pairs={{0,1},{1,0},{2,3},{3,2},{4,5},{5,4},{6,7},{7,6},{8,9},{9,8},{10,11... | collective-permute-start | bytes 1179656 | tf_op jit(solution)/shard_map/ppermute | solution.py:267
  2.9 1.7 %collective-permute-start.1 = (bf16[2,2,16,256]{3,2,1,0:T(8,128)(2,1)S(1)}, bf16[2,2,16,256]{3,2,1,0:T(8,128)(2,1)S(1)}, u32[]{:S(2)}, u32[]{:S(2)}) collective-permute-start(bf16[2,2,16,256]{3,2,1,0:T(8,128)(2,1)S(1)} %get-tuple-element.29), channel_id=1, source_target_pairs={{0,4},{4,0},{8,12},{12,8},{1,5},{5,1},{9,13},{13,9},{2,6},{6,2},{1... | collective-permute-start | bytes 98312 | tf_op jit(solution)/shard_map/ppermute | solution.py:266
  4.7 2.7 %collective-permute-start.2 = (bf16[144,128]{1,0:T(8,128)(2,1)S(1)}, bf16[144,128]{1,0:T(8,128)(2,1)S(1)}, u32[]{:S(2)}, u32[]{:S(2)}) collective-permute-start(bf16[144,128]{1,0:T(8,128)(2,1)S(1)} %get-tuple-element.27), channel_id=1, source_target_pairs={{0,66},{66,0},{2,64},{64,2},{1,67},{67,1},{3,65},{65,3},{4,70},{70... | collective-permute-start | bytes 110600 | tf_op jit(solution)/shard_map/ppermute | solution.py:265
  7.4 1.0 %templates.2 = (bf16[12,128,512]{2,1,0:T(8,128)(2,1)S(1)}, f32[12,8,512]{2,1,0:T(8,128)S(1)}) custom-call(bf16[12,128,128]{2,1,0:T(8,128)(2,1)S(1)} %get-tuple-element.28.t_ref, bf16[128,512]{1,0:T(8,128)(2,1)S(1)} %get-tuple-element.30.trow_ref, bf16[144,256]{1,0:T(8,128)(2,1)S(1)} %get-tuple-element.31.tcol_ref), custom_call_target="tpu_custom_call" | custom-call | flops 1080000000 | bytes 2000000 | tf_op jit(solution)/shard_map/templates/pallas_call | solution.py:227
  8.4 0.0 collective-permute-done.1
  8.4 0.3 collective-permute-done.2
  8.7 0.0 collective-permute-done.t_ref
  8.8 2.3 %collective-permute-start.4 = (bf16[2,2,2,16,256]{4,3,2,1,0:T(8,128)(2,1)S(1)}, bf16[2,2,2,16,256]{4,3,2,1,0:T(8,128)(2,1)S(1)}, u32[]{:S(2)}, u32[]{:S(2)}) collective-permute-start(bf16[2,2,2,16,256]{4,3,2,1,0:T(8,128)(2,1)S(1)} %get-tuple-element.58), channel_id=1, source_target_pairs={{0,12},{12,0},{4,8},{8,4},{1,13},{13,1},{5,9},{9,5},{2,14},{14,2},... | collective-permute-start | bytes 196616 | tf_op jit(solution)/shard_map/ppermute | solution.py:273
  11.1 1.3 %collective-permute-start.3 = (bf16[2,144,128]{2,1,0:T(8,128)(2,1)S(1)}, bf16[2,144,128]{2,1,0:T(8,128)(2,1)S(1)}, u32[]{:S(2)}, u32[]{:S(2)}) collective-permute-start(bf16[2,144,128]{2,1,0:T(8,128)(2,1)S(1)} %get-tuple-element.56), channel_id=1, source_target_pairs={{0,16},{16,0},{32,48},{48,32},{1,17},{17,1},{33,49},{49,33},{2,18}... | collective-permute-start | bytes 221192 | tf_op jit(solution)/shard_map/ppermute | solution.py:272
  12.4 1.0 %templates.3 = (bf16[12,128,512]{2,1,0:T(8,128)(2,1)S(1)}, f32[12,8,512]{2,1,0:T(8,128)S(1)}) custom-call(bf16[12,128,128]{2,1,0:T(8,128)(2,1)S(1)} %collective-permute-done.t_ref, bf16[128,512]{1,0:T(8,128)(2,1)S(1)} %get-tuple-element.30.trow_ref, bf16[144,256]{1,0:T(8,128)(2,1)S(1)} %get-tuple-element.31.tcol_ref), custom_call_target="tpu_custom_call" | custom-call | flops 1080000000 | bytes 2000000 | tf_op jit(solution)/shard_map/templates/pallas_call | solution.py:227
  13.4 0.0 copy-start.3
  13.4 0.0 copy-start.4
  13.4 0.0 collective-permute-done.4
  13.4 1.2 %collective-permute-done.3 = bf16[2,144,128]{2,1,0:T(8,128)(2,1)S(1)} collective-permute-done((bf16[2,144,128]{2,1,0:T(8,128)(2,1)S(1)}, bf16[2,144,128]{2,1,0:T(8,128)(2,1)S(1)}, u32[]{:S(2)}, u32[]{:S(2)}) %collective-permute-start.3) | collective-permute-done | bytes 73760 | tf_op jit(solution)/shard_map/ppermute | solution.py:272
  14.7 2.6 %collective-permute-start.5 = (bf16[2,2,144,128]{3,2,1,0:T(8,128)(2,1)S(1)}, bf16[2,2,144,128]{3,2,1,0:T(8,128)(2,1)S(1)}, u32[]{:S(2)}, u32[]{:S(2)}) collective-permute-start(bf16[2,2,144,128]{3,2,1,0:T(8,128)(2,1)S(1)} %get-tuple-element.52), channel_id=1, source_target_pairs={{0,48},{48,0},{16,32},{32,16},{1,49},{49,1},{17,33},{33,17},{2,50}... | collective-permute-start | bytes 442376 | tf_op jit(solution)/shard_map/ppermute | solution.py:278
  17.3 0.1 collective-permute-start.6
  17.4 3.8 %collective-permute-done.6 = bf16[2,2,2,2,16,256]{5,4,3,2,1,0:T(8,128)(2,1)S(1)} collective-permute-done((bf16[2,2,2,2,16,256]{5,4,3,2,1,0:T(8,128)(2,1)S(1)}, bf16[2,2,2,2,16,256]{5,4,3,2,1,0:T(8,128)(2,1)S(1)}, u32[]{:S(2)}, u32[]{:S(2)}) %collective-permute-start.6) | collective-permute-done | bytes 131104 | tf_op jit(solution)/shard_map/ppermute | solution.py:279
  21.2 0.0 collective-permute-done.5
  21.2 4.1 %collective-permute-start.7 = (bf16[2,2,2,144,128]{4,3,2,1,0:T(8,128)(2,1)S(1)}, bf16[2,2,2,144,128]{4,3,2,1,0:T(8,128)(2,1)S(1)}, u32[]{:S(2)}, u32[]{:S(2)}) collective-permute-start(bf16[2,2,2,144,128]{4,3,2,1,0:T(8,128)(2,1)S(1)} %pad_maximum_fusion.fa_ref), channel_id=1, source_target_pairs={{0,1},{1,0},{2,3},{3,2},{4,5},{5,4},{6,7},{7,6},{8,9},{9,8},{10,11... | collective-permute-start | bytes 884744 | tf_op jit(solution)/shard_map/ppermute | solution.py:284
  25.3 0.0 copy-start
  25.3 0.0 copy-start.1
  25.4 0.0 copy-start.2
  25.4 0.1 collective-permute-start.8
  25.5 1.3 %collective-permute-done.8.refs_1_ = bf16[2,2,2,2,16,256]{5,4,3,2,1,0:T(8,128)(2,1)S(1)} collective-permute-done((bf16[2,2,2,2,16,256]{5,4,3,2,1,0:T(8,128)(2,1)S(1)}, bf16[2,2,2,2,16,256]{5,4,3,2,1,0:T(8,128)(2,1)S(1)}, u32[]{:S(2)}, u32[]{:S(2)}) %collective-permute-start.8) | collective-permute-done | bytes 131104 | tf_op jit(solution)/shard_map/ppermute | solution.py:283
  26.8 0.0 copy-done.3
  26.8 0.0 copy-done.4
  26.8 0.5 %tiles.1.spec_ref = f32[2,144,512]{2,1,0:T(8,128)S(1)} custom-call(s32[1]{0:T(128)} %bitcast.index_ref, bf16[2,2,2,2,16,256]{5,4,3,2,1,0:T(8,128)(2,1)S(1)} %get-tuple-element.50.refs_0_, bf16[2,2,2,2,16,256]{5,4,3,2,1,0:T(8,128)(2,1)S(1)} %collective-permute-done.8.refs_1_, bf16[256,512]{1,0:T(8,128)(2,1)S(1)} %copy-done.3, bf16[144,512]{1,0:T(8,128)(2,1)S(1)} %copy-done.4), custom_call_target="tpu_custom_call" | custom-call | flops 800000000 | bytes 1000000 | tf_op jit(solution)/shard_map/tiles/pallas_call | solution.py:285
  27.4 0.0 collective-permute-done.7.fb_ref
  27.4 0.0 copy-done
  27.4 0.0 copy-done.1
  27.4 0.0 copy-done.2
  27.4 7.6 %correlate.1 = f32[16,2,16,256]{3,2,1,0:T(8,128)S(1)} custom-call(s32[1]{0:T(128)} %bitcast.index_ref, s32[32]{0:T(128)S(1)} %copy-done.2, f32[2,144,512]{2,1,0:T(8,128)S(1)} %tiles.1.spec_ref, bf16[2,2,2,144,128]{4,3,2,1,0:T(8,128)(2,1)S(1)} %pad_maximum_fusion.fa_ref, bf16[2,2,2,144,128]{4,3,2,1,0:T(8,128)(2,1)S(1)} %collective-permute-done.7.fb_ref, ...), custom_call_target="tpu_custom_call" | custom-call | tf_op jit(solution)/shard_map/correlate/pallas_call | solution.py:300
  35.0 9.9 %all_to_all.5 = f16[16,2,16,256]{3,2,1,0:T(8,128)(2,1)S(1)} all-to-all(f16[16,2,16,256]{3,2,1,0:T(8,128)(2,1)S(1)} %convert_element_type.4), channel_id=1, replica_groups=mesh['yh'=2,'x'=4,'z'=4,'yl'=2,'c'=2] {'z','yl','c'}, dimensions={0} | all-to-all | bytes 524288 | tf_op jit(solution)/shard_map/all_to_all | solution.py:317
  44.9 0.7 %convert_reduce_fusion = f32[4,16,256]{2,1,0:T(8,128)} fusion(f16[8,4,16,256]{3,2,1,0:T(8,128)(2,1)S(1)} %bitcast.31), kind=kLoop, calls=%fused_computation | loop fusion | flops 245760 | bytes 327680 | tf_op jit(solution)/shard_map/reduce_max | solution.py:318
  (7 shorter events, 0.2 us)
Async XLA Ops:
  1.4 7.3 %collective-permute-start = (bf16[12,128,128]{2,1,0:T(8,128)(2,1)S(1)}, bf16[12,128,128]{2,1,0:T(8,128)(2,1)S(1)}, u32[]{:S(2)}, u32[]{:S(2)}) collective-permute-start(bf16[12,128,128]{2,1,0:T(8,128)(2,1)S(1)} %get-tuple-element.28.t_ref), channel_id=1, source_target_pairs={{0,1},{1,0},{2,3},{3,2},{4,5},{5,4},{6,7},{7,6},{8,9},{9,8},{10,11... | collective-permute-start | bytes 1179656 | tf_op jit(solution)/shard_map/ppermute | solution.py:267
  2.9 5.5 %collective-permute-start.1 = (bf16[2,2,16,256]{3,2,1,0:T(8,128)(2,1)S(1)}, bf16[2,2,16,256]{3,2,1,0:T(8,128)(2,1)S(1)}, u32[]{:S(2)}, u32[]{:S(2)}) collective-permute-start(bf16[2,2,16,256]{3,2,1,0:T(8,128)(2,1)S(1)} %get-tuple-element.29), channel_id=1, source_target_pairs={{0,4},{4,0},{8,12},{12,8},{1,5},{5,1},{9,13},{13,9},{2,6},{6,2},{1... | collective-permute-start | bytes 98312 | tf_op jit(solution)/shard_map/ppermute | solution.py:266
  4.7 4.1 %collective-permute-start.2 = (bf16[144,128]{1,0:T(8,128)(2,1)S(1)}, bf16[144,128]{1,0:T(8,128)(2,1)S(1)}, u32[]{:S(2)}, u32[]{:S(2)}) collective-permute-start(bf16[144,128]{1,0:T(8,128)(2,1)S(1)} %get-tuple-element.27), channel_id=1, source_target_pairs={{0,66},{66,0},{2,64},{64,2},{1,67},{67,1},{3,65},{65,3},{4,70},{70... | collective-permute-start | bytes 110600 | tf_op jit(solution)/shard_map/ppermute | solution.py:265
  8.8 4.7 %collective-permute-start.4 = (bf16[2,2,2,16,256]{4,3,2,1,0:T(8,128)(2,1)S(1)}, bf16[2,2,2,16,256]{4,3,2,1,0:T(8,128)(2,1)S(1)}, u32[]{:S(2)}, u32[]{:S(2)}) collective-permute-start(bf16[2,2,2,16,256]{4,3,2,1,0:T(8,128)(2,1)S(1)} %get-tuple-element.58), channel_id=1, source_target_pairs={{0,12},{12,0},{4,8},{8,4},{1,13},{13,1},{5,9},{9,5},{2,14},{14,2},... | collective-permute-start | bytes 196616 | tf_op jit(solution)/shard_map/ppermute | solution.py:273
  11.1 3.6 %collective-permute-start.3 = (bf16[2,144,128]{2,1,0:T(8,128)(2,1)S(1)}, bf16[2,144,128]{2,1,0:T(8,128)(2,1)S(1)}, u32[]{:S(2)}, u32[]{:S(2)}) collective-permute-start(bf16[2,144,128]{2,1,0:T(8,128)(2,1)S(1)} %get-tuple-element.56), channel_id=1, source_target_pairs={{0,16},{16,0},{32,48},{48,32},{1,17},{17,1},{33,49},{49,33},{2,18}... | collective-permute-start | bytes 221192 | tf_op jit(solution)/shard_map/ppermute | solution.py:272
  13.4 13.4 %copy-start.3 = (bf16[256,512]{1,0:T(8,128)(2,1)S(1)}, bf16[256,512]{1,0:T(8,128)(2,1)}, u32[]{:S(2)}) copy-start(bf16[256,512]{1,0:T(8,128)(2,1)} %constant.41.clone.refs_2_) | copy-start | bytes 786436
  13.4 13.4 %copy-start.4 = (bf16[144,512]{1,0:T(8,128)(2,1)S(1)}, bf16[144,512]{1,0:T(8,128)(2,1)}, u32[]{:S(2)}) copy-start(bf16[144,512]{1,0:T(8,128)(2,1)} %constant.42.clone.refs_3_) | copy-start | bytes 442372
  14.7 6.5 %collective-permute-start.5 = (bf16[2,2,144,128]{3,2,1,0:T(8,128)(2,1)S(1)}, bf16[2,2,144,128]{3,2,1,0:T(8,128)(2,1)S(1)}, u32[]{:S(2)}, u32[]{:S(2)}) collective-permute-start(bf16[2,2,144,128]{3,2,1,0:T(8,128)(2,1)S(1)} %get-tuple-element.52), channel_id=1, source_target_pairs={{0,48},{48,0},{16,32},{32,16},{1,49},{49,1},{17,33},{33,17},{2,50}... | collective-permute-start | bytes 442376 | tf_op jit(solution)/shard_map/ppermute | solution.py:278
  17.3 3.9 %collective-permute-start.6 = (bf16[2,2,2,2,16,256]{5,4,3,2,1,0:T(8,128)(2,1)S(1)}, bf16[2,2,2,2,16,256]{5,4,3,2,1,0:T(8,128)(2,1)S(1)}, u32[]{:S(2)}, u32[]{:S(2)}) collective-permute-start(bf16[2,2,2,2,16,256]{5,4,3,2,1,0:T(8,128)(2,1)S(1)} %get-tuple-element.54), channel_id=1, source_target_pairs={{0,2},{2,0},{1,3},{3,1},{4,6},{6,4},{5,7},{7,5},{8,10},{10,8},{9,1... | collective-permute-start | bytes 393224 | tf_op jit(solution)/shard_map/ppermute | solution.py:279
  21.2 6.1 %collective-permute-start.7 = (bf16[2,2,2,144,128]{4,3,2,1,0:T(8,128)(2,1)S(1)}, bf16[2,2,2,144,128]{4,3,2,1,0:T(8,128)(2,1)S(1)}, u32[]{:S(2)}, u32[]{:S(2)}) collective-permute-start(bf16[2,2,2,144,128]{4,3,2,1,0:T(8,128)(2,1)S(1)} %pad_maximum_fusion.fa_ref), channel_id=1, source_target_pairs={{0,1},{1,0},{2,3},{3,2},{4,5},{5,4},{6,7},{7,6},{8,9},{9,8},{10,11... | collective-permute-start | bytes 884744 | tf_op jit(solution)/shard_map/ppermute | solution.py:284
  25.3 2.0 %copy-start = (bf16[512,512]{1,0:T(8,128)(2,1)S(1)}, bf16[512,512]{1,0:T(8,128)(2,1)}, u32[]{:S(2)}) copy-start(bf16[512,512]{1,0:T(8,128)(2,1)} %constant.45.clone.inv1_ref) | copy-start | bytes 1572868
  25.3 2.0 %copy-start.1 = (bf16[256,256]{1,0:T(8,128)(2,1)S(1)}, bf16[256,256]{1,0:T(8,128)(2,1)}, u32[]{:S(2)}) copy-start(bf16[256,256]{1,0:T(8,128)(2,1)} %constant.46.clone.inv2_ref) | copy-start | bytes 393220
  25.4 2.0 %copy-start.2 = (s32[32]{0:T(128)S(1)}, s32[32]{0:T(128)}, u32[]{:S(2)}) copy-start(s32[32]{0:T(128)} %bins_ref.1) | copy-start | bytes 388
  25.4 1.4 %collective-permute-start.8 = (bf16[2,2,2,2,16,256]{5,4,3,2,1,0:T(8,128)(2,1)S(1)}, bf16[2,2,2,2,16,256]{5,4,3,2,1,0:T(8,128)(2,1)S(1)}, u32[]{:S(2)}, u32[]{:S(2)}) collective-permute-start(bf16[2,2,2,2,16,256]{5,4,3,2,1,0:T(8,128)(2,1)S(1)} %get-tuple-element.49), channel_id=1, source_target_pairs={{0,1},{1,0},{2,3},{3,2},{4,5},{5,4},{6,7},{7,6},{8,9},{9,8},{10,11... | collective-permute-start | bytes 393224 | tf_op jit(solution)/shard_map/ppermute | solution.py:283

commit v3 on v2

--- a/solution.py
+++ b/solution.py
@@ -31,11 +31,14 @@
     c, s = tables()
     cat = np.concatenate
     bf = lambda a: np.asarray(a, np.float32).astype(ml_dtypes.bfloat16)
-    row = bf(cat([c, -s], 1))
+    even, odd = np.arange(0, S, 2), np.arange(1, S, 2)
+    order = cat([even, odd])
+    row = bf(cat([c[:, order], -s[:, order]], 1))
     col = bf(cat([c, s], 1)[:HR])
-    trow = bf(cat([c[:Q], -s[:Q]], 1))
+    trow = bf(cat([c[:Q, order], -s[:Q, order]], 1))
     tcol = bf(cat([c[:, :Q], s[:, :Q]], 1)[:HR])
-    inv1 = bf(cat([cat([c, s], 1), cat([-s, c], 1)], 0))
+    turn = lambda k: cat([cat([c[k, :Q], s[k, :Q]], 1), cat([-s[k, :Q], c[k, :Q]], 1)], 0)
+    inv1 = bf(np.stack([turn(even), turn(odd)]))
     wre = 2.0 * c[:, :Q]
     wre[:, 0] = c[:, 0]
     wim = -2.0 * s[:, :Q]
@@ -88,6 +91,8 @@
     rows = flip[:HR]
     turned = dot(dot(rows, hi).astype(BF), flip) + dot(dot(rows, lo).astype(BF), flip)
     sym = (0.5 * (f[:HR] + turned)).astype(BF)
+    order = jnp.where(a == jnp.where(b < Q, 2 * b, 2 * b - (S - 1)), 1.0, 0.0).astype(BF)
+    sym = dot(sym, order).astype(BF)
     fil_ref[...] = jnp.where(core == 0, sym[:, :Q], sym[:, Q:])
     for copy in copies[2:]:
         copy.wait()
@@ -138,7 +143,7 @@
     index_ref, bins_ref, spec_ref, fa_ref, fb_ref,
     t0_ref, t1_ref, n0_ref, n1_ref, inv1_ref, inv2_ref,
     out_ref,
-    h_ref, hn_ref, p_ref, q_ref, c_ref, s_ref,
+    h_ref, hn_ref, p_ref, e_ref, o_ref, q_ref, c_ref, s_ref,
 ):
     yh, x, _, _, core = place(index_ref[0])
     for t in range(2):
@@ -177,12 +182,21 @@
                             pi0 = pi[:8] + (nr * mr + ni * mi)
                             pr = jnp.concatenate([pr0, pr[8:]], axis=0)
                             pi = jnp.concatenate([pi0, pi[8:]], axis=0)
-                        p_ref[at : at + 16, :S] = pr.astype(BF)
-                        p_ref[at : at + 16, S:] = pi.astype(BF)
-        half = dot(p_ref[...], inv1_ref[...]).astype(BF)
+                        pr, pi = pr.astype(BF), pi.astype(BF)
+                        p_ref[0, at : at + 16, :Q] = pr[:, :Q]
+                        p_ref[0, at : at + 16, Q:] = pi[:, :Q]
+                        p_ref[1, at : at + 16, :Q] = pr[:, Q:]
+                        p_ref[1, at : at + 16, Q:] = pi[:, Q:]
+        e_ref[...] = dot(p_ref[0], inv1_ref[0])
+        o_ref[...] = dot(p_ref[1], inv1_ref[1])
         for j in range(count):
-            q_ref[j, :Q] = half[j * Q : (j + 1) * Q, :S]
-            q_ref[j, Q:] = half[j * Q : (j + 1) * Q, S:]
+            for r in range(0, Q, 16):
+                at = j * Q + r
+                for lane in (0, Q):
+                    even = e_ref[at : at + 16, lane : lane + Q]
+                    odd = o_ref[at : at + 16, lane : lane + Q]
+                    q_ref[j, lane + r : lane + r + 16, :Q] = (even + odd).astype(BF)
+                    q_ref[j, lane + r : lane + r + 16, Q:] = (even - odd).astype(BF)
         for j in range(count):
             c_ref[j] = dot(inv2_ref[...], q_ref[j])
             power = jnp.zeros((8, Q), F32)
@@ -305,7 +319,9 @@
         scratch_shapes=[
             pltpu.VMEM((2, Q, 2 * S), F32),
             pltpu.VMEM((2, 8, 2 * S), F32),
-            pltpu.VMEM((count * Q, 2 * S), BF),
+            pltpu.VMEM((2, count * Q, S), BF),
+            pltpu.VMEM((count * Q, S), F32),
+            pltpu.VMEM((count * Q, S), F32),
             pltpu.VMEM((count, S, S), BF),
             pltpu.VMEM((count, S, S), F32),
             pltpu.VMEM((count, 8, Q), F32),

time: 45.8 us -> 44.7 us (0.976)
  Pallas kernels: 11.5 us -> 10.5 us
    pallas_call x1, Pallas kernels: 7.57 us -> 6.37 us  [shards(): pl.pallas_call(main_kernel, out_shape=jax.ShapeDtypeStruct((16, 2, 16, S)...]
where the time goes in v3:
time: 44.7 us; the launch traced here: 44.5 us
  starting transfers between devices  16.4 us (37%)
  Pallas kernels  10.5 us (23%)
  blocking collectives  9.92 us (22%)
  waiting for transfers between devices  6.7 us (15%)
  other arithmetic  0.83 us (2%)
    all_to_all x1, blocking collectives, shards(): got = lax.all_to_all(part.astype(jnp.float16), ('z', 'yl', 'c'), 0, 0)  9.92 us
    pallas_call x1, Pallas kernels, shards(): pl.pallas_call(main_kernel, out_shape=jax.ShapeDtypeStruct((16, 2, 16, S)...  6.37 us
    ppermute x1, starting transfers between devices, shards(): fil_b = lax.ppermute(fil_a, 'c', swap)  4.09 us
    ppermute x1, waiting for transfers between devices, shards(): img_y = lax.ppermute(img, 'yl', swap)  3.8 us
    ppermute x1, starting transfers between devices, shards(): fil_y = lax.ppermute(fil, ('yh', 'yl'), across)  2.73 us
    ppermute x1, starting transfers between devices, shards(): fil_x = lax.ppermute(fil, 'x', across)  2.56 us
    ppermute x1, starting transfers between devices, shards(): img_z = lax.ppermute(img, 'z', across)  2.32 us
    pallas_call x2, Pallas kernels, spectra(): pl.pallas_call(template_kernel, out_shape=(jax.ShapeDtypeStruct((OD, Q, 2...  2.02 us
  transfers between devices with their start and end apart: 9, of which 4 were waited for; matrix products, arithmetic and copies ran while one was open for 0% of the time, Pallas kernels for 6%

profile of v3, /device:TPU:1, one launch (start us, length us, event | category | flops | bytes accessed | tf_op | source)
XLA Modules:
  0.0 44.5 jit_solution(1375747791867735666)
XLA Ops:
  0.0 1.5 %prep.1 = (bf16[144,128]{1,0:T(8,128)(2,1)S(1)}, bf16[2,2,16,256]{3,2,1,0:T(8,128)(2,1)S(1)}, bf16[12,128,128]{2,1,0:T(8,128)(2,1)S(1)}, bf16[128,512]{1,0:T(8,128)(2,1)S(1)}, bf16[144,256]{1,0:T(8,128)(2,1)S(1)}) custom-call(s32[1]{0:T(128)} %bitcast.index_ref, f32[1,256,256]{2,1,0:T(8,128)} %f_hbm.1, bf16[4,16,256]{2,1,0:T(8,128)(2,1)} %img_hbm.1, ...), custom_call_target="tpu_custom_call" | custom-call | tf_op jit(solution)/shard_map/prep/pallas_call | solution.py:259
  1.5 1.5 %collective-permute-start = (bf16[12,128,128]{2,1,0:T(8,128)(2,1)S(1)}, bf16[12,128,128]{2,1,0:T(8,128)(2,1)S(1)}, u32[]{:S(2)}, u32[]{:S(2)}) collective-permute-start(bf16[12,128,128]{2,1,0:T(8,128)(2,1)S(1)} %get-tuple-element.28.t_ref), channel_id=1, source_target_pairs={{0,1},{1,0},{2,3},{3,2},{4,5},{5,4},{6,7},{7,6},{8,9},{9,8},{10,11... | collective-permute-start | bytes 1179656 | tf_op jit(solution)/shard_map/ppermute | solution.py:281
  3.0 1.7 %collective-permute-start.1 = (bf16[2,2,16,256]{3,2,1,0:T(8,128)(2,1)S(1)}, bf16[2,2,16,256]{3,2,1,0:T(8,128)(2,1)S(1)}, u32[]{:S(2)}, u32[]{:S(2)}) collective-permute-start(bf16[2,2,16,256]{3,2,1,0:T(8,128)(2,1)S(1)} %get-tuple-element.29), channel_id=1, source_target_pairs={{0,4},{4,0},{8,12},{12,8},{1,5},{5,1},{9,13},{13,9},{2,6},{6,2},{1... | collective-permute-start | bytes 98312 | tf_op jit(solution)/shard_map/ppermute | solution.py:280
  4.8 2.7 %collective-permute-start.2 = (bf16[144,128]{1,0:T(8,128)(2,1)S(1)}, bf16[144,128]{1,0:T(8,128)(2,1)S(1)}, u32[]{:S(2)}, u32[]{:S(2)}) collective-permute-start(bf16[144,128]{1,0:T(8,128)(2,1)S(1)} %get-tuple-element.27), channel_id=1, source_target_pairs={{0,66},{66,0},{2,64},{64,2},{1,67},{67,1},{3,65},{65,3},{4,70},{70... | collective-permute-start | bytes 110600 | tf_op jit(solution)/shard_map/ppermute | solution.py:279
  7.5 1.0 %templates.2 = (bf16[12,128,512]{2,1,0:T(8,128)(2,1)S(1)}, f32[12,8,512]{2,1,0:T(8,128)S(1)}) custom-call(bf16[12,128,128]{2,1,0:T(8,128)(2,1)S(1)} %get-tuple-element.28.t_ref, bf16[128,512]{1,0:T(8,128)(2,1)S(1)} %get-tuple-element.30.trow_ref, bf16[144,256]{1,0:T(8,128)(2,1)S(1)} %get-tuple-element.31.tcol_ref), custom_call_target="tpu_custom_call" | custom-call | flops 1080000000 | bytes 2000000 | tf_op jit(solution)/shard_map/templates/pallas_call | solution.py:241
  8.5 0.0 collective-permute-done.1
  8.5 0.3 collective-permute-done.2
  8.9 0.0 collective-permute-done.t_ref
  8.9 2.3 %collective-permute-start.4 = (bf16[2,2,2,16,256]{4,3,2,1,0:T(8,128)(2,1)S(1)}, bf16[2,2,2,16,256]{4,3,2,1,0:T(8,128)(2,1)S(1)}, u32[]{:S(2)}, u32[]{:S(2)}) collective-permute-start(bf16[2,2,2,16,256]{4,3,2,1,0:T(8,128)(2,1)S(1)} %get-tuple-element.58), channel_id=1, source_target_pairs={{0,12},{12,0},{4,8},{8,4},{1,13},{13,1},{5,9},{9,5},{2,14},{14,2},... | collective-permute-start | bytes 196616 | tf_op jit(solution)/shard_map/ppermute | solution.py:287
  11.2 1.3 %collective-permute-start.3 = (bf16[2,144,128]{2,1,0:T(8,128)(2,1)S(1)}, bf16[2,144,128]{2,1,0:T(8,128)(2,1)S(1)}, u32[]{:S(2)}, u32[]{:S(2)}) collective-permute-start(bf16[2,144,128]{2,1,0:T(8,128)(2,1)S(1)} %get-tuple-element.56), channel_id=1, source_target_pairs={{0,16},{16,0},{32,48},{48,32},{1,17},{17,1},{33,49},{49,33},{2,18}... | collective-permute-start | bytes 221192 | tf_op jit(solution)/shard_map/ppermute | solution.py:286
  12.5 1.0 %templates.3 = (bf16[12,128,512]{2,1,0:T(8,128)(2,1)S(1)}, f32[12,8,512]{2,1,0:T(8,128)S(1)}) custom-call(bf16[12,128,128]{2,1,0:T(8,128)(2,1)S(1)} %collective-permute-done.t_ref, bf16[128,512]{1,0:T(8,128)(2,1)S(1)} %get-tuple-element.30.trow_ref, bf16[144,256]{1,0:T(8,128)(2,1)S(1)} %get-tuple-element.31.tcol_ref), custom_call_target="tpu_custom_call" | custom-call | flops 1080000000 | bytes 2000000 | tf_op jit(solution)/shard_map/templates/pallas_call | solution.py:241
  13.5 0.0 copy-start.3
  13.5 0.0 copy-start.4
  13.5 0.0 collective-permute-done.4
  13.6 1.2 %collective-permute-done.3 = bf16[2,144,128]{2,1,0:T(8,128)(2,1)S(1)} collective-permute-done((bf16[2,144,128]{2,1,0:T(8,128)(2,1)S(1)}, bf16[2,144,128]{2,1,0:T(8,128)(2,1)S(1)}, u32[]{:S(2)}, u32[]{:S(2)}) %collective-permute-start.3) | collective-permute-done | bytes 73760 | tf_op jit(solution)/shard_map/ppermute | solution.py:286
  14.8 2.6 %collective-permute-start.5 = (bf16[2,2,144,128]{3,2,1,0:T(8,128)(2,1)S(1)}, bf16[2,2,144,128]{3,2,1,0:T(8,128)(2,1)S(1)}, u32[]{:S(2)}, u32[]{:S(2)}) collective-permute-start(bf16[2,2,144,128]{3,2,1,0:T(8,128)(2,1)S(1)} %get-tuple-element.52), channel_id=1, source_target_pairs={{0,48},{48,0},{16,32},{32,16},{1,49},{49,1},{17,33},{33,17},{2,50}... | collective-permute-start | bytes 442376 | tf_op jit(solution)/shard_map/ppermute | solution.py:292
  17.4 0.1 collective-permute-start.6
  17.5 3.8 %collective-permute-done.6 = bf16[2,2,2,2,16,256]{5,4,3,2,1,0:T(8,128)(2,1)S(1)} collective-permute-done((bf16[2,2,2,2,16,256]{5,4,3,2,1,0:T(8,128)(2,1)S(1)}, bf16[2,2,2,2,16,256]{5,4,3,2,1,0:T(8,128)(2,1)S(1)}, u32[]{:S(2)}, u32[]{:S(2)}) %collective-permute-start.6) | collective-permute-done | bytes 131104 | tf_op jit(solution)/shard_map/ppermute | solution.py:293
  21.3 0.0 collective-permute-done.5
  21.3 4.1 %collective-permute-start.7 = (bf16[2,2,2,144,128]{4,3,2,1,0:T(8,128)(2,1)S(1)}, bf16[2,2,2,144,128]{4,3,2,1,0:T(8,128)(2,1)S(1)}, u32[]{:S(2)}, u32[]{:S(2)}) collective-permute-start(bf16[2,2,2,144,128]{4,3,2,1,0:T(8,128)(2,1)S(1)} %pad_maximum_fusion.fa_ref), channel_id=1, source_target_pairs={{0,1},{1,0},{2,3},{3,2},{4,5},{5,4},{6,7},{7,6},{8,9},{9,8},{10,11... | collective-permute-start | bytes 884744 | tf_op jit(solution)/shard_map/ppermute | solution.py:298
  25.4 0.0 copy-start
  25.5 0.0 copy-start.1
  25.5 0.0 copy-start.2
  25.5 0.1 collective-permute-start.8
  25.6 1.3 %collective-permute-done.8.refs_1_ = bf16[2,2,2,2,16,256]{5,4,3,2,1,0:T(8,128)(2,1)S(1)} collective-permute-done((bf16[2,2,2,2,16,256]{5,4,3,2,1,0:T(8,128)(2,1)S(1)}, bf16[2,2,2,2,16,256]{5,4,3,2,1,0:T(8,128)(2,1)S(1)}, u32[]{:S(2)}, u32[]{:S(2)}) %collective-permute-start.8) | collective-permute-done | bytes 131104 | tf_op jit(solution)/shard_map/ppermute | solution.py:297
  26.9 0.0 copy-done.3
  26.9 0.0 copy-done.4
  26.9 0.5 %tiles.1.spec_ref = f32[2,144,512]{2,1,0:T(8,128)S(1)} custom-call(s32[1]{0:T(128)} %bitcast.index_ref, bf16[2,2,2,2,16,256]{5,4,3,2,1,0:T(8,128)(2,1)S(1)} %get-tuple-element.50.refs_0_, bf16[2,2,2,2,16,256]{5,4,3,2,1,0:T(8,128)(2,1)S(1)} %collective-permute-done.8.refs_1_, bf16[256,512]{1,0:T(8,128)(2,1)S(1)} %copy-done.3, bf16[144,512]{1,0:T(8,128)(2,1)S(1)} %copy-done.4), custom_call_target="tpu_custom_call" | custom-call | flops 800000000 | bytes 1000000 | tf_op jit(solution)/shard_map/tiles/pallas_call | solution.py:299
  27.5 0.0 collective-permute-done.7.fb_ref
  27.5 0.0 copy-done
  27.5 0.0 copy-done.1
  27.5 0.0 copy-done.2
  27.5 6.4 %correlate.1 = f32[16,2,16,256]{3,2,1,0:T(8,128)S(1)} custom-call(s32[1]{0:T(128)} %bitcast.index_ref, s32[32]{0:T(128)S(1)} %copy-done.2, f32[2,144,512]{2,1,0:T(8,128)S(1)} %tiles.1.spec_ref, bf16[2,2,2,144,128]{4,3,2,1,0:T(8,128)(2,1)S(1)} %pad_maximum_fusion.fa_ref, bf16[2,2,2,144,128]{4,3,2,1,0:T(8,128)(2,1)S(1)} %collective-permute-done.7.fb_ref, ...), custom_call_target="tpu_custom_call" | custom-call | tf_op jit(solution)/shard_map/correlate/pallas_call | solution.py:314
  33.9 9.9 %all_to_all.5 = f16[16,2,16,256]{3,2,1,0:T(8,128)(2,1)S(1)} all-to-all(f16[16,2,16,256]{3,2,1,0:T(8,128)(2,1)S(1)} %convert_element_type.4), channel_id=1, replica_groups=mesh['yh'=2,'x'=4,'z'=4,'yl'=2,'c'=2] {'z','yl','c'}, dimensions={0} | all-to-all | bytes 524288 | tf_op jit(solution)/shard_map/all_to_all | solution.py:333
  43.9 0.7 %convert_reduce_fusion = f32[4,16,256]{2,1,0:T(8,128)} fusion(f16[8,4,16,256]{3,2,1,0:T(8,128)(2,1)S(1)} %bitcast.31), kind=kLoop, calls=%fused_computation | loop fusion | flops 245760 | bytes 327680 | tf_op jit(solution)/shard_map/reduce_max | solution.py:334
  (7 shorter events, 0.2 us)
Async XLA Ops:
  1.5 7.3 %collective-permute-start = (bf16[12,128,128]{2,1,0:T(8,128)(2,1)S(1)}, bf16[12,128,128]{2,1,0:T(8,128)(2,1)S(1)}, u32[]{:S(2)}, u32[]{:S(2)}) collective-permute-start(bf16[12,128,128]{2,1,0:T(8,128)(2,1)S(1)} %get-tuple-element.28.t_ref), channel_id=1, source_target_pairs={{0,1},{1,0},{2,3},{3,2},{4,5},{5,4},{6,7},{7,6},{8,9},{9,8},{10,11... | collective-permute-start | bytes 1179656 | tf_op jit(solution)/shard_map/ppermute | solution.py:281
  3.0 5.5 %collective-permute-start.1 = (bf16[2,2,16,256]{3,2,1,0:T(8,128)(2,1)S(1)}, bf16[2,2,16,256]{3,2,1,0:T(8,128)(2,1)S(1)}, u32[]{:S(2)}, u32[]{:S(2)}) collective-permute-start(bf16[2,2,16,256]{3,2,1,0:T(8,128)(2,1)S(1)} %get-tuple-element.29), channel_id=1, source_target_pairs={{0,4},{4,0},{8,12},{12,8},{1,5},{5,1},{9,13},{13,9},{2,6},{6,2},{1... | collective-permute-start | bytes 98312 | tf_op jit(solution)/shard_map/ppermute | solution.py:280
  4.8 4.1 %collective-permute-start.2 = (bf16[144,128]{1,0:T(8,128)(2,1)S(1)}, bf16[144,128]{1,0:T(8,128)(2,1)S(1)}, u32[]{:S(2)}, u32[]{:S(2)}) collective-permute-start(bf16[144,128]{1,0:T(8,128)(2,1)S(1)} %get-tuple-element.27), channel_id=1, source_target_pairs={{0,66},{66,0},{2,64},{64,2},{1,67},{67,1},{3,65},{65,3},{4,70},{70... | collective-permute-start | bytes 110600 | tf_op jit(solution)/shard_map/ppermute | solution.py:279
  8.9 4.7 %collective-permute-start.4 = (bf16[2,2,2,16,256]{4,3,2,1,0:T(8,128)(2,1)S(1)}, bf16[2,2,2,16,256]{4,3,2,1,0:T(8,128)(2,1)S(1)}, u32[]{:S(2)}, u32[]{:S(2)}) collective-permute-start(bf16[2,2,2,16,256]{4,3,2,1,0:T(8,128)(2,1)S(1)} %get-tuple-element.58), channel_id=1, source_target_pairs={{0,12},{12,0},{4,8},{8,4},{1,13},{13,1},{5,9},{9,5},{2,14},{14,2},... | collective-permute-start | bytes 196616 | tf_op jit(solution)/shard_map/ppermute | solution.py:287
  11.2 3.6 %collective-permute-start.3 = (bf16[2,144,128]{2,1,0:T(8,128)(2,1)S(1)}, bf16[2,144,128]{2,1,0:T(8,128)(2,1)S(1)}, u32[]{:S(2)}, u32[]{:S(2)}) collective-permute-start(bf16[2,144,128]{2,1,0:T(8,128)(2,1)S(1)} %get-tuple-element.56), channel_id=1, source_target_pairs={{0,16},{16,0},{32,48},{48,32},{1,17},{17,1},{33,49},{49,33},{2,18}... | collective-permute-start | bytes 221192 | tf_op jit(solution)/shard_map/ppermute | solution.py:286
  13.5 13.4 %copy-start.3 = (bf16[256,512]{1,0:T(8,128)(2,1)S(1)}, bf16[256,512]{1,0:T(8,128)(2,1)}, u32[]{:S(2)}) copy-start(bf16[256,512]{1,0:T(8,128)(2,1)} %constant.41.clone.refs_2_) | copy-start | bytes 786436
  13.5 13.4 %copy-start.4 = (bf16[144,512]{1,0:T(8,128)(2,1)S(1)}, bf16[144,512]{1,0:T(8,128)(2,1)}, u32[]{:S(2)}) copy-start(bf16[144,512]{1,0:T(8,128)(2,1)} %constant.42.clone.refs_3_) | copy-start | bytes 442372
  14.8 6.5 %collective-permute-start.5 = (bf16[2,2,144,128]{3,2,1,0:T(8,128)(2,1)S(1)}, bf16[2,2,144,128]{3,2,1,0:T(8,128)(2,1)S(1)}, u32[]{:S(2)}, u32[]{:S(2)}) collective-permute-start(bf16[2,2,144,128]{3,2,1,0:T(8,128)(2,1)S(1)} %get-tuple-element.52), channel_id=1, source_target_pairs={{0,48},{48,0},{16,32},{32,16},{1,49},{49,1},{17,33},{33,17},{2,50}... | collective-permute-start | bytes 442376 | tf_op jit(solution)/shard_map/ppermute | solution.py:292
  17.4 3.9 %collective-permute-start.6 = (bf16[2,2,2,2,16,256]{5,4,3,2,1,0:T(8,128)(2,1)S(1)}, bf16[2,2,2,2,16,256]{5,4,3,2,1,0:T(8,128)(2,1)S(1)}, u32[]{:S(2)}, u32[]{:S(2)}) collective-permute-start(bf16[2,2,2,2,16,256]{5,4,3,2,1,0:T(8,128)(2,1)S(1)} %get-tuple-element.54), channel_id=1, source_target_pairs={{0,2},{2,0},{1,3},{3,1},{4,6},{6,4},{5,7},{7,5},{8,10},{10,8},{9,1... | collective-permute-start | bytes 393224 | tf_op jit(solution)/shard_map/ppermute | solution.py:293
  21.3 6.1 %collective-permute-start.7 = (bf16[2,2,2,144,128]{4,3,2,1,0:T(8,128)(2,1)S(1)}, bf16[2,2,2,144,128]{4,3,2,1,0:T(8,128)(2,1)S(1)}, u32[]{:S(2)}, u32[]{:S(2)}) collective-permute-start(bf16[2,2,2,144,128]{4,3,2,1,0:T(8,128)(2,1)S(1)} %pad_maximum_fusion.fa_ref), channel_id=1, source_target_pairs={{0,1},{1,0},{2,3},{3,2},{4,5},{5,4},{6,7},{7,6},{8,9},{9,8},{10,11... | collective-permute-start | bytes 884744 | tf_op jit(solution)/shard_map/ppermute | solution.py:298
  25.4 2.0 %copy-start = (bf16[2,256,256]{2,1,0:T(8,128)(2,1)S(1)}, bf16[2,256,256]{2,1,0:T(8,128)(2,1)}, u32[]{:S(2)}) copy-start(bf16[2,256,256]{2,1,0:T(8,128)(2,1)} %constant.45.clone.inv1_ref) | copy-start | bytes 786436
  25.5 2.0 %copy-start.1 = (bf16[256,256]{1,0:T(8,128)(2,1)S(1)}, bf16[256,256]{1,0:T(8,128)(2,1)}, u32[]{:S(2)}) copy-start(bf16[256,256]{1,0:T(8,128)(2,1)} %constant.46.clone.inv2_ref) | copy-start | bytes 393220
  25.5 2.0 %copy-start.2 = (s32[32]{0:T(128)S(1)}, s32[32]{0:T(128)}, u32[]{:S(2)}) copy-start(s32[32]{0:T(128)} %bins_ref.1) | copy-start | bytes 388
  25.5 1.4 %collective-permute-start.8 = (bf16[2,2,2,2,16,256]{5,4,3,2,1,0:T(8,128)(2,1)S(1)}, bf16[2,2,2,2,16,256]{5,4,3,2,1,0:T(8,128)(2,1)S(1)}, u32[]{:S(2)}, u32[]{:S(2)}) collective-permute-start(bf16[2,2,2,2,16,256]{5,4,3,2,1,0:T(8,128)(2,1)S(1)} %get-tuple-element.49), channel_id=1, source_target_pairs={{0,1},{1,0},{2,3},{3,2},{4,5},{5,4},{6,7},{7,6},{8,9},{9,8},{10,11... | collective-permute-start | bytes 393224 | tf_op jit(solution)/shard_map/ppermute | solution.py:297

commit v4 on v3

--- a/solution.py
+++ b/solution.py
@@ -80,7 +80,10 @@
     )
     a = lax.broadcasted_iota(jnp.int32, (S, S), 0)
     b = lax.broadcasted_iota(jnp.int32, (S, S), 1)
-    flip = jnp.where((a + b) % S == 0, 1.0, 0.0).astype(BF)
+    ordered = jnp.where(b < Q, 2 * b, 2 * b - (S - 1))
+    pick = lambda mask: jnp.where(mask, 1.0, 0.0).astype(BF)
+    flip = pick((a + b) % S == 0)[:HR]
+    same, turned = pick(a == ordered), pick((a + ordered) % S == 0)
     copies[0].wait()
     split_ref[0] = img_ref[pl.ds(2 * core, 2)]
     split_ref[1] = img_ref[pl.ds(2 - 2 * core, 2)]
@@ -88,11 +91,10 @@
     f = f_ref[0]
     hi = f.astype(BF)
     lo = (f - hi.astype(F32)).astype(BF)
-    rows = flip[:HR]
-    turned = dot(dot(rows, hi).astype(BF), flip) + dot(dot(rows, lo).astype(BF), flip)
-    sym = (0.5 * (f[:HR] + turned)).astype(BF)
-    order = jnp.where(a == jnp.where(b < Q, 2 * b, 2 * b - (S - 1)), 1.0, 0.0).astype(BF)
-    sym = dot(sym, order).astype(BF)
+    both = dot(flip, jnp.concatenate([hi, lo], axis=1)).astype(BF)
+    terms = jnp.concatenate([hi[:HR], lo[:HR], both], axis=1)
+    sums = dot(terms, jnp.concatenate([same, same, turned, turned], axis=0))
+    sym = (0.5 * sums).astype(BF)
     fil_ref[...] = jnp.where(core == 0, sym[:, :Q], sym[:, Q:])
     for copy in copies[2:]:
         copy.wait()
@@ -280,18 +282,17 @@
     img_z = lax.ppermute(img, "z", near)
     other_templates = lax.ppermute(own_templates, "c", swap)
     t0, n0 = spectra(own_templates)
-    other_templates, img_z, fil_y, t0, n0 = tie((other_templates, img_z, fil_y, t0, n0))
+    fil_y, t0, n0 = tie((fil_y, t0, n0))
     fil = jnp.stack([fil, fil_y])
     img = jnp.stack([img, img_z], axis=1)
     fil_x = lax.ppermute(fil, "x", near)
     img_z = lax.ppermute(img, "z", across)
     t1, n1 = spectra(other_templates)
-    fil_x, img_z, t1, n1 = tie((fil_x, img_z, t1, n1))
+    fil_x, t1, n1 = tie((fil_x, t1, n1))
     fil = jnp.stack([fil, fil_x])
     img = jnp.stack([img, img_z], axis=1)
     fil_x = lax.ppermute(fil, "x", across)
     img_y = lax.ppermute(img, "yl", swap)
-    fil_x, img_y = tie((fil_x, img_y))
     fil_a = jnp.stack([fil, fil_x])
     img_a = jnp.stack([img, img_y], axis=1)
     img_b = lax.ppermute(img_a[1], "c", swap)

time: 44.7 us -> 43.9 us (0.982)
  waiting for transfers between devices: 6.7 us -> 4.7 us
  blocking collectives: 9.92 us -> 10.7 us
    ppermute x1, waiting for transfers between devices: 3.8 us -> 0.01 us  [shards(): img_y = lax.ppermute(img, 'yl', swap)]
    ppermute x1, waiting for transfers between devices: 0.01 us -> 2.57 us  [shards(): fil_x = lax.ppermute(fil, 'x', across)]
    ppermute x1, starting transfers between devices: 0.1 us -> 1.44 us  [shards(): img_b = lax.ppermute(img_a[1], 'c', swap)]
    ppermute x1, starting transfers between devices: 4.09 us -> 3.11 us  [shards(): fil_b = lax.ppermute(fil_a, 'c', swap)]
    all_to_all x1, blocking collectives: 9.92 us -> 10.7 us  [shards(): got = lax.all_to_all(part.astype(jnp.float16), ('z', 'yl', 'c'), 0, 0)]
  transfers between devices with their start and end apart: 9 -> 9, of which waited for: 4 -> 3; matrix products, arithmetic and copies ran while one was open for 0% -> 0% of each run, Pallas kernels for 6% -> 6%
where the time goes in v4:
time: 43.9 us; the launch traced here: 43.6 us
  starting transfers between devices  16.8 us (38%)
  blocking collectives  10.7 us (24%)
  Pallas kernels  10.3 us (23%)
  waiting for transfers between devices  4.7 us (11%)
  other arithmetic  0.83 us (2%)
    all_to_all x1, blocking collectives, shards(): got = lax.all_to_all(part.astype(jnp.float16), ('z', 'yl', 'c'), 0, 0)  10.7 us
    pallas_call x1, Pallas kernels, shards(): pl.pallas_call(main_kernel, out_shape=jax.ShapeDtypeStruct((16, 2, 16, S)...  6.37 us
    ppermute x1, starting transfers between devices, shards(): fil_b = lax.ppermute(fil_a, 'c', swap)  3.11 us
    ppermute x1, starting transfers between devices, shards(): fil_y = lax.ppermute(fil, ('yh', 'yl'), across)  2.73 us
    ppermute x1, waiting for transfers between devices, shards(): fil_x = lax.ppermute(fil, 'x', across)  2.57 us
    ppermute x1, starting transfers between devices, shards(): fil_x = lax.ppermute(fil, 'x', across)  2.55 us
    ppermute x1, starting transfers between devices, shards(): img_z = lax.ppermute(img, 'z', across)  2.31 us
    pallas_call x2, Pallas kernels, spectra(): pl.pallas_call(template_kernel, out_shape=(jax.ShapeDtypeStruct((OD, Q, 2...  2.02 us
  transfers between devices with their start and end apart: 9, of which 3 were waited for; matrix products, arithmetic and copies ran while one was open for 0% of the time, Pallas kernels for 6%

profile of v4, /device:TPU:1, one launch (start us, length us, event | category | flops | bytes accessed | tf_op | source)
XLA Modules:
  0.0 43.6 jit_solution(5178496728895339824)
XLA Ops:
  0.0 1.4 %prep.1 = (bf16[144,128]{1,0:T(8,128)(2,1)S(1)}, bf16[2,2,16,256]{3,2,1,0:T(8,128)(2,1)S(1)}, bf16[12,128,128]{2,1,0:T(8,128)(2,1)S(1)}, bf16[128,512]{1,0:T(8,128)(2,1)S(1)}, bf16[144,256]{1,0:T(8,128)(2,1)S(1)}) custom-call(s32[1]{0:T(128)} %bitcast.index_ref, f32[1,256,256]{2,1,0:T(8,128)} %f_hbm.1, bf16[4,16,256]{2,1,0:T(8,128)(2,1)} %img_hbm.1, ...), custom_call_target="tpu_custom_call" | custom-call | tf_op jit(solution)/shard_map/prep/pallas_call | solution.py:261
  1.4 1.5 %collective-permute-start.2 = (bf16[12,128,128]{2,1,0:T(8,128)(2,1)S(1)}, bf16[12,128,128]{2,1,0:T(8,128)(2,1)S(1)}, u32[]{:S(2)}, u32[]{:S(2)}) collective-permute-start(bf16[12,128,128]{2,1,0:T(8,128)(2,1)S(1)} %get-tuple-element.23.t_ref), channel_id=1, source_target_pairs={{0,1},{1,0},{2,3},{3,2},{4,5},{5,4},{6,7},{7,6},{8,9},{9,8},{10,11... | collective-permute-start | bytes 1179656 | tf_op jit(solution)/shard_map/ppermute | solution.py:283
  2.9 1.7 %collective-permute-start.5 = (bf16[2,2,16,256]{3,2,1,0:T(8,128)(2,1)S(1)}, bf16[2,2,16,256]{3,2,1,0:T(8,128)(2,1)S(1)}, u32[]{:S(2)}, u32[]{:S(2)}) collective-permute-start(bf16[2,2,16,256]{3,2,1,0:T(8,128)(2,1)S(1)} %get-tuple-element.32), channel_id=1, source_target_pairs={{0,4},{4,0},{8,12},{12,8},{1,5},{5,1},{9,13},{13,9},{2,6},{6,2},{1... | collective-permute-start | bytes 98312 | tf_op jit(solution)/shard_map/ppermute | solution.py:282
  4.6 2.7 %collective-permute-start = (bf16[144,128]{1,0:T(8,128)(2,1)S(1)}, bf16[144,128]{1,0:T(8,128)(2,1)S(1)}, u32[]{:S(2)}, u32[]{:S(2)}) collective-permute-start(bf16[144,128]{1,0:T(8,128)(2,1)S(1)} %get-tuple-element.22), channel_id=1, source_target_pairs={{0,66},{66,0},{2,64},{64,2},{1,67},{67,1},{3,65},{65,3},{4,70},{70... | collective-permute-start | bytes 110600 | tf_op jit(solution)/shard_map/ppermute | solution.py:281
  7.4 1.0 %templates.2 = (bf16[12,128,512]{2,1,0:T(8,128)(2,1)S(1)}, f32[12,8,512]{2,1,0:T(8,128)S(1)}) custom-call(bf16[12,128,128]{2,1,0:T(8,128)(2,1)S(1)} %get-tuple-element.23.t_ref, bf16[128,512]{1,0:T(8,128)(2,1)S(1)} %get-tuple-element.24.trow_ref, bf16[144,256]{1,0:T(8,128)(2,1)S(1)} %get-tuple-element.25.tcol_ref), custom_call_target="tpu_custom_call" | custom-call | flops 1080000000 | bytes 2000000 | tf_op jit(solution)/shard_map/templates/pallas_call | solution.py:243
  8.4 0.0 collective-permute-done.5
  8.4 2.3 %collective-permute-start.6 = (bf16[2,2,2,16,256]{4,3,2,1,0:T(8,128)(2,1)S(1)}, bf16[2,2,2,16,256]{4,3,2,1,0:T(8,128)(2,1)S(1)}, u32[]{:S(2)}, u32[]{:S(2)}) collective-permute-start(bf16[2,2,2,16,256]{4,3,2,1,0:T(8,128)(2,1)S(1)} %get-tuple-element.48), channel_id=1, source_target_pairs={{0,12},{12,0},{4,8},{8,4},{1,13},{13,1},{5,9},{9,5},{2,14},{14,2},... | collective-permute-start | bytes 196616 | tf_op jit(solution)/shard_map/ppermute | solution.py:289
  10.7 0.0 collective-permute-done
  10.7 1.3 %collective-permute-start.1 = (bf16[2,144,128]{2,1,0:T(8,128)(2,1)S(1)}, bf16[2,144,128]{2,1,0:T(8,128)(2,1)S(1)}, u32[]{:S(2)}, u32[]{:S(2)}) collective-permute-start(bf16[2,144,128]{2,1,0:T(8,128)(2,1)S(1)} %get-tuple-element.46), channel_id=1, source_target_pairs={{0,16},{16,0},{32,48},{48,32},{1,17},{17,1},{33,49},{49,33},{2,18}... | collective-permute-start | bytes 221192 | tf_op jit(solution)/shard_map/ppermute | solution.py:288
  12.0 0.0 collective-permute-done.2.t_ref
  12.0 1.0 %templates.3 = (bf16[12,128,512]{2,1,0:T(8,128)(2,1)S(1)}, f32[12,8,512]{2,1,0:T(8,128)S(1)}) custom-call(bf16[12,128,128]{2,1,0:T(8,128)(2,1)S(1)} %collective-permute-done.2.t_ref, bf16[128,512]{1,0:T(8,128)(2,1)S(1)} %get-tuple-element.24.trow_ref, bf16[144,256]{1,0:T(8,128)(2,1)S(1)} %get-tuple-element.25.tcol_ref), custom_call_target="tpu_custom_call" | custom-call | flops 1080000000 | bytes 2000000 | tf_op jit(solution)/shard_map/templates/pallas_call | solution.py:243
  13.1 0.0 copy-start.3
  13.1 0.0 copy-start.4
  13.1 1.1 %collective-permute-done.1 = bf16[2,144,128]{2,1,0:T(8,128)(2,1)S(1)} collective-permute-done((bf16[2,144,128]{2,1,0:T(8,128)(2,1)S(1)}, bf16[2,144,128]{2,1,0:T(8,128)(2,1)S(1)}, u32[]{:S(2)}, u32[]{:S(2)}) %collective-permute-start.1) | collective-permute-done | bytes 73760 | tf_op jit(solution)/shard_map/ppermute | solution.py:288
  14.2 2.6 %collective-permute-start.3 = (bf16[2,2,144,128]{3,2,1,0:T(8,128)(2,1)S(1)}, bf16[2,2,144,128]{3,2,1,0:T(8,128)(2,1)S(1)}, u32[]{:S(2)}, u32[]{:S(2)}) collective-permute-start(bf16[2,2,144,128]{3,2,1,0:T(8,128)(2,1)S(1)} %get-tuple-element.42), channel_id=1, source_target_pairs={{0,48},{48,0},{16,32},{32,16},{1,49},{49,1},{17,33},{33,17},{2,50}... | collective-permute-start | bytes 442376 | tf_op jit(solution)/shard_map/ppermute | solution.py:294
  16.8 0.0 collective-permute-done.6
  16.8 0.1 collective-permute-start.7
  16.9 2.6 %collective-permute-done.3 = bf16[2,2,144,128]{3,2,1,0:T(8,128)(2,1)S(1)} collective-permute-done((bf16[2,2,144,128]{3,2,1,0:T(8,128)(2,1)S(1)}, bf16[2,2,144,128]{3,2,1,0:T(8,128)(2,1)S(1)}, u32[]{:S(2)}, u32[]{:S(2)}) %collective-permute-start.3) | collective-permute-done | bytes 147488 | tf_op jit(solution)/shard_map/ppermute | solution.py:294
  19.6 3.1 %collective-permute-start.4 = (bf16[2,2,2,144,128]{4,3,2,1,0:T(8,128)(2,1)S(1)}, bf16[2,2,2,144,128]{4,3,2,1,0:T(8,128)(2,1)S(1)}, u32[]{:S(2)}, u32[]{:S(2)}) collective-permute-start(bf16[2,2,2,144,128]{4,3,2,1,0:T(8,128)(2,1)S(1)} %pad_maximum_fusion.fa_ref), channel_id=1, source_target_pairs={{0,1},{1,0},{2,3},{3,2},{4,5},{5,4},{6,7},{7,6},{8,9},{9,8},{10,11... | collective-permute-start | bytes 884744 | tf_op jit(solution)/shard_map/ppermute | solution.py:299
  22.7 0.0 collective-permute-done.7
  22.7 0.0 copy-start
  22.7 0.0 copy-start.1
  22.7 0.0 copy-start.2
  22.7 1.4 %collective-permute-start.8 = (bf16[2,2,2,2,16,256]{5,4,3,2,1,0:T(8,128)(2,1)S(1)}, bf16[2,2,2,2,16,256]{5,4,3,2,1,0:T(8,128)(2,1)S(1)}, u32[]{:S(2)}, u32[]{:S(2)}) collective-permute-start(bf16[2,2,2,2,16,256]{5,4,3,2,1,0:T(8,128)(2,1)S(1)} %get-tuple-element.39), channel_id=1, source_target_pairs={{0,1},{1,0},{2,3},{3,2},{4,5},{5,4},{6,7},{7,6},{8,9},{9,8},{10,11... | collective-permute-start | bytes 393224 | tf_op jit(solution)/shard_map/ppermute | solution.py:298
  24.2 1.0 %collective-permute-done.8.refs_1_ = bf16[2,2,2,2,16,256]{5,4,3,2,1,0:T(8,128)(2,1)S(1)} collective-permute-done((bf16[2,2,2,2,16,256]{5,4,3,2,1,0:T(8,128)(2,1)S(1)}, bf16[2,2,2,2,16,256]{5,4,3,2,1,0:T(8,128)(2,1)S(1)}, u32[]{:S(2)}, u32[]{:S(2)}) %collective-permute-start.8) | collective-permute-done | bytes 131104 | tf_op jit(solution)/shard_map/ppermute | solution.py:298
  25.2 0.0 copy-done.3
  25.2 0.0 copy-done.4
  25.2 0.6 %tiles.1.spec_ref = f32[2,144,512]{2,1,0:T(8,128)S(1)} custom-call(s32[1]{0:T(128)} %bitcast.index_ref, bf16[2,2,2,2,16,256]{5,4,3,2,1,0:T(8,128)(2,1)S(1)} %get-tuple-element.40.refs_0_, bf16[2,2,2,2,16,256]{5,4,3,2,1,0:T(8,128)(2,1)S(1)} %collective-permute-done.8.refs_1_, bf16[256,512]{1,0:T(8,128)(2,1)S(1)} %copy-done.3, bf16[144,512]{1,0:T(8,128)(2,1)S(1)} %copy-done.4), custom_call_target="tpu_custom_call" | custom-call | flops 800000000 | bytes 1000000 | tf_op jit(solution)/shard_map/tiles/pallas_call | solution.py:300
  25.7 0.0 collective-permute-done.4.fb_ref
  25.7 0.0 copy-done
  25.7 0.0 copy-done.1
  25.8 0.0 copy-done.2
  25.8 6.4 %correlate.1 = f32[16,2,16,256]{3,2,1,0:T(8,128)S(1)} custom-call(s32[1]{0:T(128)} %bitcast.index_ref, s32[32]{0:T(128)S(1)} %copy-done.2, f32[2,144,512]{2,1,0:T(8,128)S(1)} %tiles.1.spec_ref, bf16[2,2,2,144,128]{4,3,2,1,0:T(8,128)(2,1)S(1)} %pad_maximum_fusion.fa_ref, bf16[2,2,2,144,128]{4,3,2,1,0:T(8,128)(2,1)S(1)} %collective-permute-done.4.fb_ref, ...), custom_call_target="tpu_custom_call" | custom-call | tf_op jit(solution)/shard_map/correlate/pallas_call | solution.py:315
  32.2 10.7 %all_to_all.5 = f16[16,2,16,256]{3,2,1,0:T(8,128)(2,1)S(1)} all-to-all(f16[16,2,16,256]{3,2,1,0:T(8,128)(2,1)S(1)} %convert_element_type.4), channel_id=1, replica_groups=mesh['yh'=2,'x'=4,'z'=4,'yl'=2,'c'=2] {'z','yl','c'}, dimensions={0} | all-to-all | bytes 524288 | tf_op jit(solution)/shard_map/all_to_all | solution.py:334
  42.9 0.7 %convert_reduce_fusion = f32[4,16,256]{2,1,0:T(8,128)} fusion(f16[8,4,16,256]{3,2,1,0:T(8,128)(2,1)S(1)} %bitcast.31), kind=kLoop, calls=%fused_computation | loop fusion | flops 245760 | bytes 327680 | tf_op jit(solution)/shard_map/reduce_max | solution.py:335
  (7 shorter events, 0.2 us)
Async XLA Ops:
  1.4 10.7 %collective-permute-start.2 = (bf16[12,128,128]{2,1,0:T(8,128)(2,1)S(1)}, bf16[12,128,128]{2,1,0:T(8,128)(2,1)S(1)}, u32[]{:S(2)}, u32[]{:S(2)}) collective-permute-start(bf16[12,128,128]{2,1,0:T(8,128)(2,1)S(1)} %get-tuple-element.23.t_ref), channel_id=1, source_target_pairs={{0,1},{1,0},{2,3},{3,2},{4,5},{5,4},{6,7},{7,6},{8,9},{9,8},{10,11... | collective-permute-start | bytes 1179656 | tf_op jit(solution)/shard_map/ppermute | solution.py:283
  2.9 5.5 %collective-permute-start.5 = (bf16[2,2,16,256]{3,2,1,0:T(8,128)(2,1)S(1)}, bf16[2,2,16,256]{3,2,1,0:T(8,128)(2,1)S(1)}, u32[]{:S(2)}, u32[]{:S(2)}) collective-permute-start(bf16[2,2,16,256]{3,2,1,0:T(8,128)(2,1)S(1)} %get-tuple-element.32), channel_id=1, source_target_pairs={{0,4},{4,0},{8,12},{12,8},{1,5},{5,1},{9,13},{13,9},{2,6},{6,2},{1... | collective-permute-start | bytes 98312 | tf_op jit(solution)/shard_map/ppermute | solution.py:282
  4.6 6.1 %collective-permute-start = (bf16[144,128]{1,0:T(8,128)(2,1)S(1)}, bf16[144,128]{1,0:T(8,128)(2,1)S(1)}, u32[]{:S(2)}, u32[]{:S(2)}) collective-permute-start(bf16[144,128]{1,0:T(8,128)(2,1)S(1)} %get-tuple-element.22), channel_id=1, source_target_pairs={{0,66},{66,0},{2,64},{64,2},{1,67},{67,1},{3,65},{65,3},{4,70},{70... | collective-permute-start | bytes 110600 | tf_op jit(solution)/shard_map/ppermute | solution.py:281
  8.4 8.4 %collective-permute-start.6 = (bf16[2,2,2,16,256]{4,3,2,1,0:T(8,128)(2,1)S(1)}, bf16[2,2,2,16,256]{4,3,2,1,0:T(8,128)(2,1)S(1)}, u32[]{:S(2)}, u32[]{:S(2)}) collective-permute-start(bf16[2,2,2,16,256]{4,3,2,1,0:T(8,128)(2,1)S(1)} %get-tuple-element.48), channel_id=1, source_target_pairs={{0,12},{12,0},{4,8},{8,4},{1,13},{13,1},{5,9},{9,5},{2,14},{14,2},... | collective-permute-start | bytes 196616 | tf_op jit(solution)/shard_map/ppermute | solution.py:289
  10.7 3.5 %collective-permute-start.1 = (bf16[2,144,128]{2,1,0:T(8,128)(2,1)S(1)}, bf16[2,144,128]{2,1,0:T(8,128)(2,1)S(1)}, u32[]{:S(2)}, u32[]{:S(2)}) collective-permute-start(bf16[2,144,128]{2,1,0:T(8,128)(2,1)S(1)} %get-tuple-element.46), channel_id=1, source_target_pairs={{0,16},{16,0},{32,48},{48,32},{1,17},{17,1},{33,49},{49,33},{2,18}... | collective-permute-start | bytes 221192 | tf_op jit(solution)/shard_map/ppermute | solution.py:288
  13.1 12.1 %copy-start.3 = (bf16[256,512]{1,0:T(8,128)(2,1)S(1)}, bf16[256,512]{1,0:T(8,128)(2,1)}, u32[]{:S(2)}) copy-start(bf16[256,512]{1,0:T(8,128)(2,1)} %constant.41.clone.refs_2_) | copy-start | bytes 786436
  13.1 12.1 %copy-start.4 = (bf16[144,512]{1,0:T(8,128)(2,1)S(1)}, bf16[144,512]{1,0:T(8,128)(2,1)}, u32[]{:S(2)}) copy-start(bf16[144,512]{1,0:T(8,128)(2,1)} %constant.42.clone.refs_3_) | copy-start | bytes 442372
  14.2 5.3 %collective-permute-start.3 = (bf16[2,2,144,128]{3,2,1,0:T(8,128)(2,1)S(1)}, bf16[2,2,144,128]{3,2,1,0:T(8,128)(2,1)S(1)}, u32[]{:S(2)}, u32[]{:S(2)}) collective-permute-start(bf16[2,2,144,128]{3,2,1,0:T(8,128)(2,1)S(1)} %get-tuple-element.42), channel_id=1, source_target_pairs={{0,48},{48,0},{16,32},{32,16},{1,49},{49,1},{17,33},{33,17},{2,50}... | collective-permute-start | bytes 442376 | tf_op jit(solution)/shard_map/ppermute | solution.py:294
  16.8 5.9 %collective-permute-start.7 = (bf16[2,2,2,2,16,256]{5,4,3,2,1,0:T(8,128)(2,1)S(1)}, bf16[2,2,2,2,16,256]{5,4,3,2,1,0:T(8,128)(2,1)S(1)}, u32[]{:S(2)}, u32[]{:S(2)}) collective-permute-start(bf16[2,2,2,2,16,256]{5,4,3,2,1,0:T(8,128)(2,1)S(1)} %get-tuple-element.43), channel_id=1, source_target_pairs={{0,2},{2,0},{1,3},{3,1},{4,6},{6,4},{5,7},{7,5},{8,10},{10,8},{9,1... | collective-permute-start | bytes 393224 | tf_op jit(solution)/shard_map/ppermute | solution.py:295
  19.6 6.2 %collective-permute-start.4 = (bf16[2,2,2,144,128]{4,3,2,1,0:T(8,128)(2,1)S(1)}, bf16[2,2,2,144,128]{4,3,2,1,0:T(8,128)(2,1)S(1)}, u32[]{:S(2)}, u32[]{:S(2)}) collective-permute-start(bf16[2,2,2,144,128]{4,3,2,1,0:T(8,128)(2,1)S(1)} %pad_maximum_fusion.fa_ref), channel_id=1, source_target_pairs={{0,1},{1,0},{2,3},{3,2},{4,5},{5,4},{6,7},{7,6},{8,9},{9,8},{10,11... | collective-permute-start | bytes 884744 | tf_op jit(solution)/shard_map/ppermute | solution.py:299
  22.7 3.0 %copy-start = (bf16[2,256,256]{2,1,0:T(8,128)(2,1)S(1)}, bf16[2,256,256]{2,1,0:T(8,128)(2,1)}, u32[]{:S(2)}) copy-start(bf16[2,256,256]{2,1,0:T(8,128)(2,1)} %constant.45.clone.inv1_ref) | copy-start | bytes 786436
  22.7 3.0 %copy-start.1 = (bf16[256,256]{1,0:T(8,128)(2,1)S(1)}, bf16[256,256]{1,0:T(8,128)(2,1)}, u32[]{:S(2)}) copy-start(bf16[256,256]{1,0:T(8,128)(2,1)} %constant.46.clone.inv2_ref) | copy-start | bytes 393220
  22.7 3.0 %copy-start.2 = (s32[32]{0:T(128)S(1)}, s32[32]{0:T(128)}, u32[]{:S(2)}) copy-start(s32[32]{0:T(128)} %bins_ref.1) | copy-start | bytes 388
  22.7 2.4 %collective-permute-start.8 = (bf16[2,2,2,2,16,256]{5,4,3,2,1,0:T(8,128)(2,1)S(1)}, bf16[2,2,2,2,16,256]{5,4,3,2,1,0:T(8,128)(2,1)S(1)}, u32[]{:S(2)}, u32[]{:S(2)}) collective-permute-start(bf16[2,2,2,2,16,256]{5,4,3,2,1,0:T(8,128)(2,1)S(1)} %get-tuple-element.39), channel_id=1, source_target_pairs={{0,1},{1,0},{2,3},{3,2},{4,5},{5,4},{6,7},{7,6},{8,9},{9,8},{10,11... | collective-permute-start | bytes 393224 | tf_op jit(solution)/shard_map/ppermute | solution.py:298

commit v5 on v4

--- a/solution.py
+++ b/solution.py
@@ -286,14 +286,14 @@
     fil = jnp.stack([fil, fil_y])
     img = jnp.stack([img, img_z], axis=1)
     fil_x = lax.ppermute(fil, "x", near)
+    fil_w = lax.ppermute(fil, "x", across)
     img_z = lax.ppermute(img, "z", across)
     t1, n1 = spectra(other_templates)
     fil_x, t1, n1 = tie((fil_x, t1, n1))
-    fil = jnp.stack([fil, fil_x])
     img = jnp.stack([img, img_z], axis=1)
-    fil_x = lax.ppermute(fil, "x", across)
+    fil_v = lax.ppermute(fil_x, "x", across)
     img_y = lax.ppermute(img, "yl", swap)
-    fil_a = jnp.stack([fil, fil_x])
+    fil_a = jnp.stack([jnp.stack([fil, fil_x]), jnp.stack([fil_w, fil_v])])
     img_a = jnp.stack([img, img_y], axis=1)
     img_b = lax.ppermute(img_a[1], "c", swap)
     fil_b = lax.ppermute(fil_a, "c", swap)

time: 43.9 us -> 43.6 us (level)
  waiting for transfers between devices: 4.7 us -> 3.69 us
  starting transfers between devices: 16.8 us -> 17.3 us
    ppermute x1 -> x2, starting transfers between devices: 2.55 us -> 3.94 us  [the longest x1 2.12 us: shards(): fil_v = lax.ppermute(fil_x, 'x', across)]
    ppermute x1, starting transfers between devices: 1.44 us -> 0.11 us  [shards(): img_b = lax.ppermute(img_a[1], 'c', swap)]
    ppermute x1, waiting for transfers between devices: 1.13 us -> 0.01 us  [shards(): fil_x = lax.ppermute(fil, 'x', near)]
    ppermute x1, starting transfers between devices: 1.74 us -> 2.55 us  [shards(): img_z = lax.ppermute(img, 'z', near)]
    ppermute x1 -> x2, waiting for transfers between devices: 2.57 us -> 2.35 us  [the longest x1 2.34 us: shards(): fil_v = lax.ppermute(fil_x, 'x', across)]
  transfers between devices with their start and end apart: 9 -> 10, of which waited for: 3 -> 2; matrix products, arithmetic and copies ran while one was open for 0% -> 0% of each run, Pallas kernels for 6% -> 6%
where the time goes in v5:
time: 43.6 us; the launch traced here: 43.5 us
  starting transfers between devices  17.3 us (40%)
  blocking collectives  11 us (25%)
  Pallas kernels  10.3 us (24%)
  waiting for transfers between devices  3.69 us (8%)
  other arithmetic  0.84 us (2%)
    all_to_all x1, blocking collectives, shards(): got = lax.all_to_all(part.astype(jnp.float16), ('z', 'yl', 'c'), 0, 0)  11 us
    pallas_call x1, Pallas kernels, shards(): pl.pallas_call(main_kernel, out_shape=jax.ShapeDtypeStruct((16, 2, 16, S)...  6.38 us
    ppermute x1, starting transfers between devices, shards(): fil_b = lax.ppermute(fil_a, 'c', swap)  3.08 us
    ppermute x1, starting transfers between devices, shards(): fil_y = lax.ppermute(fil, ('yh', 'yl'), across)  2.73 us
    ppermute x1, starting transfers between devices, shards(): img_z = lax.ppermute(img, 'z', near)  2.55 us
    ppermute x1, waiting for transfers between devices, shards(): fil_v = lax.ppermute(fil_x, 'x', across)  2.34 us
    ppermute x1, starting transfers between devices, shards(): img_z = lax.ppermute(img, 'z', across)  2.31 us
    ppermute x1, starting transfers between devices, shards(): fil_v = lax.ppermute(fil_x, 'x', across)  2.12 us
  transfers between devices with their start and end apart: 10, of which 2 were waited for; matrix products, arithmetic and copies ran while one was open for 0% of the time, Pallas kernels for 6%

profile of v5, /device:TPU:1, one launch (start us, length us, event | category | flops | bytes accessed | tf_op | source)
XLA Modules:
  0.0 43.5 jit_solution(7652254145529357948)
XLA Ops:
  0.0 1.4 %prep.1 = (bf16[144,128]{1,0:T(8,128)(2,1)S(1)}, bf16[2,2,16,256]{3,2,1,0:T(8,128)(2,1)S(1)}, bf16[12,128,128]{2,1,0:T(8,128)(2,1)S(1)}, bf16[128,512]{1,0:T(8,128)(2,1)S(1)}, bf16[144,256]{1,0:T(8,128)(2,1)S(1)}) custom-call(s32[1]{0:T(128)} %bitcast.index_ref, f32[1,256,256]{2,1,0:T(8,128)} %f_hbm.1, bf16[4,16,256]{2,1,0:T(8,128)(2,1)} %img_hbm.1, ...), custom_call_target="tpu_custom_call" | custom-call | tf_op jit(solution)/shard_map/prep/pallas_call | solution.py:261
  1.4 2.5 %collective-permute-start.6 = (bf16[2,2,16,256]{3,2,1,0:T(8,128)(2,1)S(1)}, bf16[2,2,16,256]{3,2,1,0:T(8,128)(2,1)S(1)}, u32[]{:S(2)}, u32[]{:S(2)}) collective-permute-start(bf16[2,2,16,256]{3,2,1,0:T(8,128)(2,1)S(1)} %get-tuple-element.32), channel_id=1, source_target_pairs={{0,4},{4,0},{8,12},{12,8},{1,5},{5,1},{9,13},{13,9},{2,6},{6,2},{1... | collective-permute-start | bytes 98312 | tf_op jit(solution)/shard_map/ppermute | solution.py:282
  3.9 2.7 %collective-permute-start = (bf16[144,128]{1,0:T(8,128)(2,1)S(1)}, bf16[144,128]{1,0:T(8,128)(2,1)S(1)}, u32[]{:S(2)}, u32[]{:S(2)}) collective-permute-start(bf16[144,128]{1,0:T(8,128)(2,1)S(1)} %get-tuple-element.22), channel_id=1, source_target_pairs={{0,66},{66,0},{2,64},{64,2},{1,67},{67,1},{3,65},{65,3},{4,70},{70... | collective-permute-start | bytes 110600 | tf_op jit(solution)/shard_map/ppermute | solution.py:281
  6.7 1.2 %collective-permute-start.2 = (bf16[12,128,128]{2,1,0:T(8,128)(2,1)S(1)}, bf16[12,128,128]{2,1,0:T(8,128)(2,1)S(1)}, u32[]{:S(2)}, u32[]{:S(2)}) collective-permute-start(bf16[12,128,128]{2,1,0:T(8,128)(2,1)S(1)} %get-tuple-element.23.t_ref), channel_id=1, source_target_pairs={{0,1},{1,0},{2,3},{3,2},{4,5},{5,4},{6,7},{7,6},{8,9},{9,8},{10,11... | collective-permute-start | bytes 1179656 | tf_op jit(solution)/shard_map/ppermute | solution.py:283
  7.9 1.0 %templates.2 = (bf16[12,128,512]{2,1,0:T(8,128)(2,1)S(1)}, f32[12,8,512]{2,1,0:T(8,128)S(1)}) custom-call(bf16[12,128,128]{2,1,0:T(8,128)(2,1)S(1)} %get-tuple-element.23.t_ref, bf16[128,512]{1,0:T(8,128)(2,1)S(1)} %get-tuple-element.24.trow_ref, bf16[144,256]{1,0:T(8,128)(2,1)S(1)} %get-tuple-element.25.tcol_ref), custom_call_target="tpu_custom_call" | custom-call | flops 1080000000 | bytes 2000000 | tf_op jit(solution)/shard_map/templates/pallas_call | solution.py:243
  8.9 0.0 collective-permute-done.6
  9.0 2.3 %collective-permute-start.7 = (bf16[2,2,2,16,256]{4,3,2,1,0:T(8,128)(2,1)S(1)}, bf16[2,2,2,16,256]{4,3,2,1,0:T(8,128)(2,1)S(1)}, u32[]{:S(2)}, u32[]{:S(2)}) collective-permute-start(bf16[2,2,2,16,256]{4,3,2,1,0:T(8,128)(2,1)S(1)} %get-tuple-element.46), channel_id=1, source_target_pairs={{0,12},{12,0},{4,8},{8,4},{1,13},{13,1},{5,9},{9,5},{2,14},{14,2},... | collective-permute-start | bytes 196616 | tf_op jit(solution)/shard_map/ppermute | solution.py:290
  11.3 0.0 collective-permute-done
  11.3 1.3 %collective-permute-start.1 = (bf16[2,144,128]{2,1,0:T(8,128)(2,1)S(1)}, bf16[2,144,128]{2,1,0:T(8,128)(2,1)S(1)}, u32[]{:S(2)}, u32[]{:S(2)}) collective-permute-start(bf16[2,144,128]{2,1,0:T(8,128)(2,1)S(1)} %get-tuple-element.44), channel_id=1, source_target_pairs={{0,16},{16,0},{32,48},{48,32},{1,17},{17,1},{33,49},{49,33},{2,18}... | collective-permute-start | bytes 221192 | tf_op jit(solution)/shard_map/ppermute | solution.py:288
  12.6 1.8 %collective-permute-start.3 = (bf16[2,144,128]{2,1,0:T(8,128)(2,1)S(1)}, bf16[2,144,128]{2,1,0:T(8,128)(2,1)S(1)}, u32[]{:S(2)}, u32[]{:S(2)}) collective-permute-start(bf16[2,144,128]{2,1,0:T(8,128)(2,1)S(1)} %get-tuple-element.44), channel_id=1, source_target_pairs={{0,48},{48,0},{16,32},{32,16},{1,49},{49,1},{17,33},{33,17},{2,50}... | collective-permute-start | bytes 221192 | tf_op jit(solution)/shard_map/ppermute | solution.py:289
  14.4 0.0 collective-permute-done.7
  14.4 0.1 collective-permute-start.8
  14.5 0.0 collective-permute-done.2.t_ref
  14.5 1.0 %templates.3 = (bf16[12,128,512]{2,1,0:T(8,128)(2,1)S(1)}, f32[12,8,512]{2,1,0:T(8,128)S(1)}) custom-call(bf16[12,128,128]{2,1,0:T(8,128)(2,1)S(1)} %collective-permute-done.2.t_ref, bf16[128,512]{1,0:T(8,128)(2,1)S(1)} %get-tuple-element.24.trow_ref, bf16[144,256]{1,0:T(8,128)(2,1)S(1)} %get-tuple-element.25.tcol_ref), custom_call_target="tpu_custom_call" | custom-call | flops 1080000000 | bytes 2000000 | tf_op jit(solution)/shard_map/templates/pallas_call | solution.py:243
  15.6 0.0 copy-start.3
  15.6 0.0 copy-start.4
  15.6 0.0 collective-permute-done.1
  15.6 2.1 %collective-permute-start.4 = (bf16[2,144,128]{2,1,0:T(8,128)(2,1)S(1)}, bf16[2,144,128]{2,1,0:T(8,128)(2,1)S(1)}, u32[]{:S(2)}, u32[]{:S(2)}) collective-permute-start(bf16[2,144,128]{2,1,0:T(8,128)(2,1)S(1)} %collective-permute-done.1), channel_id=1, source_target_pairs={{0,48},{48,0},{16,32},{32,16},{1,49},{49,1},{17,33},{33,17},{2,50}... | collective-permute-start | bytes 221192 | tf_op jit(solution)/shard_map/ppermute | solution.py:294
  17.7 0.0 collective-permute-done.3
  17.7 2.3 %collective-permute-done.4 = bf16[2,144,128]{2,1,0:T(8,128)(2,1)S(1)} collective-permute-done((bf16[2,144,128]{2,1,0:T(8,128)(2,1)S(1)}, bf16[2,144,128]{2,1,0:T(8,128)(2,1)S(1)}, u32[]{:S(2)}, u32[]{:S(2)}) %collective-permute-start.4) | collective-permute-done | bytes 73760 | tf_op jit(solution)/shard_map/ppermute | solution.py:294
  20.1 3.1 %collective-permute-start.5 = (bf16[2,2,2,144,128]{4,3,2,1,0:T(8,128)(2,1)S(1)}, bf16[2,2,2,144,128]{4,3,2,1,0:T(8,128)(2,1)S(1)}, u32[]{:S(2)}, u32[]{:S(2)}) collective-permute-start(bf16[2,2,2,144,128]{4,3,2,1,0:T(8,128)(2,1)S(1)} %pad_maximum_fusion.fa_ref), channel_id=1, source_target_pairs={{0,1},{1,0},{2,3},{3,2},{4,5},{5,4},{6,7},{7,6},{8,9},{9,8},{10,11... | collective-permute-start | bytes 884744 | tf_op jit(solution)/shard_map/ppermute | solution.py:299
  23.2 0.0 collective-permute-done.8
  23.3 0.0 copy-start
  23.3 0.0 copy-start.1
  23.3 0.0 copy-start.2
  23.3 0.1 collective-permute-start.9
  23.4 1.3 %collective-permute-done.9.refs_1_ = bf16[2,2,2,2,16,256]{5,4,3,2,1,0:T(8,128)(2,1)S(1)} collective-permute-done((bf16[2,2,2,2,16,256]{5,4,3,2,1,0:T(8,128)(2,1)S(1)}, bf16[2,2,2,2,16,256]{5,4,3,2,1,0:T(8,128)(2,1)S(1)}, u32[]{:S(2)}, u32[]{:S(2)}) %collective-permute-start.9) | collective-permute-done | bytes 131104 | tf_op jit(solution)/shard_map/ppermute | solution.py:298
  24.7 0.0 copy-done.3
  24.7 0.0 copy-done.4
  24.7 0.5 %tiles.1.spec_ref = f32[2,144,512]{2,1,0:T(8,128)S(1)} custom-call(s32[1]{0:T(128)} %bitcast.index_ref, bf16[2,2,2,2,16,256]{5,4,3,2,1,0:T(8,128)(2,1)S(1)} %get-tuple-element.40.refs_0_, bf16[2,2,2,2,16,256]{5,4,3,2,1,0:T(8,128)(2,1)S(1)} %collective-permute-done.9.refs_1_, bf16[256,512]{1,0:T(8,128)(2,1)S(1)} %copy-done.3, bf16[144,512]{1,0:T(8,128)(2,1)S(1)} %copy-done.4), custom_call_target="tpu_custom_call" | custom-call | flops 800000000 | bytes 1000000 | tf_op jit(solution)/shard_map/tiles/pallas_call | solution.py:300
  25.3 0.0 collective-permute-done.5.fb_ref
  25.3 0.0 copy-done
  25.3 0.0 copy-done.1
  25.3 0.0 copy-done.2
  25.3 6.4 %correlate.1 = f32[16,2,16,256]{3,2,1,0:T(8,128)S(1)} custom-call(s32[1]{0:T(128)} %bitcast.index_ref, s32[32]{0:T(128)S(1)} %copy-done.2, f32[2,144,512]{2,1,0:T(8,128)S(1)} %tiles.1.spec_ref, bf16[2,2,2,144,128]{4,3,2,1,0:T(8,128)(2,1)S(1)} %pad_maximum_fusion.fa_ref, bf16[2,2,2,144,128]{4,3,2,1,0:T(8,128)(2,1)S(1)} %collective-permute-done.5.fb_ref, ...), custom_call_target="tpu_custom_call" | custom-call | tf_op jit(solution)/shard_map/correlate/pallas_call | solution.py:315
  31.8 11.0 %all_to_all.5 = f16[16,2,16,256]{3,2,1,0:T(8,128)(2,1)S(1)} all-to-all(f16[16,2,16,256]{3,2,1,0:T(8,128)(2,1)S(1)} %convert_element_type.4), channel_id=1, replica_groups=mesh['yh'=2,'x'=4,'z'=4,'yl'=2,'c'=2] {'z','yl','c'}, dimensions={0} | all-to-all | bytes 524288 | tf_op jit(solution)/shard_map/all_to_all | solution.py:334
  42.8 0.7 %convert_reduce_fusion = f32[4,16,256]{2,1,0:T(8,128)} fusion(f16[8,4,16,256]{3,2,1,0:T(8,128)(2,1)S(1)} %bitcast.34), kind=kLoop, calls=%fused_computation | loop fusion | flops 245760 | bytes 327680 | tf_op jit(solution)/shard_map/reduce_max | solution.py:335
  (8 shorter events, 0.2 us)
Async XLA Ops:
  1.4 7.5 %collective-permute-start.6 = (bf16[2,2,16,256]{3,2,1,0:T(8,128)(2,1)S(1)}, bf16[2,2,16,256]{3,2,1,0:T(8,128)(2,1)S(1)}, u32[]{:S(2)}, u32[]{:S(2)}) collective-permute-start(bf16[2,2,16,256]{3,2,1,0:T(8,128)(2,1)S(1)} %get-tuple-element.32), channel_id=1, source_target_pairs={{0,4},{4,0},{8,12},{12,8},{1,5},{5,1},{9,13},{13,9},{2,6},{6,2},{1... | collective-permute-start | bytes 98312 | tf_op jit(solution)/shard_map/ppermute | solution.py:282
  3.9 7.3 %collective-permute-start = (bf16[144,128]{1,0:T(8,128)(2,1)S(1)}, bf16[144,128]{1,0:T(8,128)(2,1)S(1)}, u32[]{:S(2)}, u32[]{:S(2)}) collective-permute-start(bf16[144,128]{1,0:T(8,128)(2,1)S(1)} %get-tuple-element.22), channel_id=1, source_target_pairs={{0,66},{66,0},{2,64},{64,2},{1,67},{67,1},{3,65},{65,3},{4,70},{70... | collective-permute-start | bytes 110600 | tf_op jit(solution)/shard_map/ppermute | solution.py:281
  6.7 7.9 %collective-permute-start.2 = (bf16[12,128,128]{2,1,0:T(8,128)(2,1)S(1)}, bf16[12,128,128]{2,1,0:T(8,128)(2,1)S(1)}, u32[]{:S(2)}, u32[]{:S(2)}) collective-permute-start(bf16[12,128,128]{2,1,0:T(8,128)(2,1)S(1)} %get-tuple-element.23.t_ref), channel_id=1, source_target_pairs={{0,1},{1,0},{2,3},{3,2},{4,5},{5,4},{6,7},{7,6},{8,9},{9,8},{10,11... | collective-permute-start | bytes 1179656 | tf_op jit(solution)/shard_map/ppermute | solution.py:283
  9.0 5.4 %collective-permute-start.7 = (bf16[2,2,2,16,256]{4,3,2,1,0:T(8,128)(2,1)S(1)}, bf16[2,2,2,16,256]{4,3,2,1,0:T(8,128)(2,1)S(1)}, u32[]{:S(2)}, u32[]{:S(2)}) collective-permute-start(bf16[2,2,2,16,256]{4,3,2,1,0:T(8,128)(2,1)S(1)} %get-tuple-element.46), channel_id=1, source_target_pairs={{0,12},{12,0},{4,8},{8,4},{1,13},{13,1},{5,9},{9,5},{2,14},{14,2},... | collective-permute-start | bytes 196616 | tf_op jit(solution)/shard_map/ppermute | solution.py:290
  11.3 4.3 %collective-permute-start.1 = (bf16[2,144,128]{2,1,0:T(8,128)(2,1)S(1)}, bf16[2,144,128]{2,1,0:T(8,128)(2,1)S(1)}, u32[]{:S(2)}, u32[]{:S(2)}) collective-permute-start(bf16[2,144,128]{2,1,0:T(8,128)(2,1)S(1)} %get-tuple-element.44), channel_id=1, source_target_pairs={{0,16},{16,0},{32,48},{48,32},{1,17},{17,1},{33,49},{49,33},{2,18}... | collective-permute-start | bytes 221192 | tf_op jit(solution)/shard_map/ppermute | solution.py:288
  12.6 5.1 %collective-permute-start.3 = (bf16[2,144,128]{2,1,0:T(8,128)(2,1)S(1)}, bf16[2,144,128]{2,1,0:T(8,128)(2,1)S(1)}, u32[]{:S(2)}, u32[]{:S(2)}) collective-permute-start(bf16[2,144,128]{2,1,0:T(8,128)(2,1)S(1)} %get-tuple-element.44), channel_id=1, source_target_pairs={{0,48},{48,0},{16,32},{32,16},{1,49},{49,1},{17,33},{33,17},{2,50}... | collective-permute-start | bytes 221192 | tf_op jit(solution)/shard_map/ppermute | solution.py:289
  14.4 8.8 %collective-permute-start.8 = (bf16[2,2,2,2,16,256]{5,4,3,2,1,0:T(8,128)(2,1)S(1)}, bf16[2,2,2,2,16,256]{5,4,3,2,1,0:T(8,128)(2,1)S(1)}, u32[]{:S(2)}, u32[]{:S(2)}) collective-permute-start(bf16[2,2,2,2,16,256]{5,4,3,2,1,0:T(8,128)(2,1)S(1)} %get-tuple-element.41), channel_id=1, source_target_pairs={{0,2},{2,0},{1,3},{3,1},{4,6},{6,4},{5,7},{7,5},{8,10},{10,8},{9,1... | collective-permute-start | bytes 393224 | tf_op jit(solution)/shard_map/ppermute | solution.py:295
  15.6 9.2 %copy-start.3 = (bf16[256,512]{1,0:T(8,128)(2,1)S(1)}, bf16[256,512]{1,0:T(8,128)(2,1)}, u32[]{:S(2)}) copy-start(bf16[256,512]{1,0:T(8,128)(2,1)} %constant.41.clone.refs_2_) | copy-start | bytes 786436
  15.6 9.2 %copy-start.4 = (bf16[144,512]{1,0:T(8,128)(2,1)S(1)}, bf16[144,512]{1,0:T(8,128)(2,1)}, u32[]{:S(2)}) copy-start(bf16[144,512]{1,0:T(8,128)(2,1)} %constant.42.clone.refs_3_) | copy-start | bytes 442372
  15.6 4.5 %collective-permute-start.4 = (bf16[2,144,128]{2,1,0:T(8,128)(2,1)S(1)}, bf16[2,144,128]{2,1,0:T(8,128)(2,1)S(1)}, u32[]{:S(2)}, u32[]{:S(2)}) collective-permute-start(bf16[2,144,128]{2,1,0:T(8,128)(2,1)S(1)} %collective-permute-done.1), channel_id=1, source_target_pairs={{0,48},{48,0},{16,32},{32,16},{1,49},{49,1},{17,33},{33,17},{2,50}... | collective-permute-start | bytes 221192 | tf_op jit(solution)/shard_map/ppermute | solution.py:294
  20.1 5.1 %collective-permute-start.5 = (bf16[2,2,2,144,128]{4,3,2,1,0:T(8,128)(2,1)S(1)}, bf16[2,2,2,144,128]{4,3,2,1,0:T(8,128)(2,1)S(1)}, u32[]{:S(2)}, u32[]{:S(2)}) collective-permute-start(bf16[2,2,2,144,128]{4,3,2,1,0:T(8,128)(2,1)S(1)} %pad_maximum_fusion.fa_ref), channel_id=1, source_target_pairs={{0,1},{1,0},{2,3},{3,2},{4,5},{5,4},{6,7},{7,6},{8,9},{9,8},{10,11... | collective-permute-start | bytes 884744 | tf_op jit(solution)/shard_map/ppermute | solution.py:299
  23.3 2.0 %copy-start = (bf16[2,256,256]{2,1,0:T(8,128)(2,1)S(1)}, bf16[2,256,256]{2,1,0:T(8,128)(2,1)}, u32[]{:S(2)}) copy-start(bf16[2,256,256]{2,1,0:T(8,128)(2,1)} %constant.45.clone.inv1_ref) | copy-start | bytes 786436
  23.3 2.0 %copy-start.1 = (bf16[256,256]{1,0:T(8,128)(2,1)S(1)}, bf16[256,256]{1,0:T(8,128)(2,1)}, u32[]{:S(2)}) copy-start(bf16[256,256]{1,0:T(8,128)(2,1)} %constant.46.clone.inv2_ref) | copy-start | bytes 393220
  23.3 2.0 %copy-start.2 = (s32[32]{0:T(128)S(1)}, s32[32]{0:T(128)}, u32[]{:S(2)}) copy-start(s32[32]{0:T(128)} %bins_ref.1) | copy-start | bytes 388
  23.3 1.4 %collective-permute-start.9 = (bf16[2,2,2,2,16,256]{5,4,3,2,1,0:T(8,128)(2,1)S(1)}, bf16[2,2,2,2,16,256]{5,4,3,2,1,0:T(8,128)(2,1)S(1)}, u32[]{:S(2)}, u32[]{:S(2)}) collective-permute-start(bf16[2,2,2,2,16,256]{5,4,3,2,1,0:T(8,128)(2,1)S(1)} %get-tuple-element.39), channel_id=1, source_target_pairs={{0,1},{1,0},{2,3},{3,2},{4,5},{5,4},{6,7},{7,6},{8,9},{9,8},{10,11... | collective-permute-start | bytes 393224 | tf_op jit(solution)/shard_map/ppermute | solution.py:298

commit v6 on v5

--- a/solution.py
+++ b/solution.py
@@ -70,8 +70,8 @@
     core = index_ref[0] % 2
     copies = fetch(
         [
+            (f_hbm, f_ref),
             (img_hbm, img_ref),
-            (f_hbm, f_ref),
             (t_hbm, t_ref),
             (trow_hbm, trow_ref),
             (tcol_hbm, tcol_ref),
@@ -85,9 +85,6 @@
     flip = pick((a + b) % S == 0)[:HR]
     same, turned = pick(a == ordered), pick((a + ordered) % S == 0)
     copies[0].wait()
-    split_ref[0] = img_ref[pl.ds(2 * core, 2)]
-    split_ref[1] = img_ref[pl.ds(2 - 2 * core, 2)]
-    copies[1].wait()
     f = f_ref[0]
     hi = f.astype(BF)
     lo = (f - hi.astype(F32)).astype(BF)
@@ -96,6 +93,9 @@
     sums = dot(terms, jnp.concatenate([same, same, turned, turned], axis=0))
     sym = (0.5 * sums).astype(BF)
     fil_ref[...] = jnp.where(core == 0, sym[:, :Q], sym[:, Q:])
+    copies[1].wait()
+    split_ref[0] = img_ref[pl.ds(2 * core, 2)]
+    split_ref[1] = img_ref[pl.ds(2 - 2 * core, 2)]
     for copy in copies[2:]:
         copy.wait()
 
@@ -279,7 +279,8 @@
     )(index, far(filters), far(tile_images), far(templates), far(trow), far(tcol))
     near, across = [(0, 1), (1, 0), (2, 3), (3, 2)], [(0, 3), (3, 0), (1, 2), (2, 1)]
     fil_y = lax.ppermute(fil, ("yh", "yl"), across)
-    img_z = lax.ppermute(img, "z", near)
+    img_z = lax.ppermute(tile_images, "z", near).reshape(2, 2, 16, S)
+    img_z = jnp.where(lax.axis_index("c") == 0, img_z, img_z[::-1])
     other_templates = lax.ppermute(own_templates, "c", swap)
     t0, n0 = spectra(own_templates)
     fil_y, t0, n0 = tie((fil_y, t0, n0))

time: 43.6 us -> 43.6 us (level)
  blocking collectives: 11 us -> 11.9 us
  starting transfers between devices: 17.3 us -> 16.5 us
    ppermute x1, starting transfers between devices: 3.08 us -> 2.18 us  [shards(): fil_b = lax.ppermute(fil_a, 'c', swap)]
    all_to_all x1, blocking collectives: 11 us -> 11.9 us  [shards(): got = lax.all_to_all(part.astype(jnp.float16), ('z', 'yl', 'c'), 0, 0)]
  transfers between devices with their start and end apart: 10 -> 10, of which waited for: 2 -> 2; matrix products, arithmetic and copies ran while one was open for 0% -> 0% of each run, Pallas kernels for 6% -> 9%
where the time goes in v6:
time: 43.6 us; the launch traced here: 43.4 us
  starting transfers between devices  16.5 us (38%)
  blocking collectives  11.9 us (27%)
  Pallas kernels  10.3 us (24%)
  waiting for transfers between devices  3.67 us (8%)
  other arithmetic  0.85 us (2%)
    all_to_all x1, blocking collectives, shards(): got = lax.all_to_all(part.astype(jnp.float16), ('z', 'yl', 'c'), 0, 0)  11.9 us
    pallas_call x1, Pallas kernels, shards(): pl.pallas_call(main_kernel, out_shape=jax.ShapeDtypeStruct((16, 2, 16, S)...  6.34 us
    ppermute x1, starting transfers between devices, shards(): fil_y = lax.ppermute(fil, ('yh', 'yl'), across)  2.81 us
    ppermute x1, starting transfers between devices, shards(): img_z = lax.ppermute(tile_images, 'z', near).reshape(2, 2, 16, S)  2.47 us
    ppermute x1, waiting for transfers between devices, shards(): fil_v = lax.ppermute(fil_x, 'x', across)  2.33 us
    ppermute x1, starting transfers between devices, shards(): img_z = lax.ppermute(img, 'z', across)  2.31 us
    ppermute x1, starting transfers between devices, shards(): fil_b = lax.ppermute(fil_a, 'c', swap)  2.18 us
    ppermute x1, starting transfers between devices, shards(): fil_v = lax.ppermute(fil_x, 'x', across)  2.14 us
  transfers between devices with their start and end apart: 10, of which 2 were waited for; matrix products, arithmetic and copies ran while one was open for 0% of the time, Pallas kernels for 9%

profile of v6, /device:TPU:1, one launch (start us, length us, event | category | flops | bytes accessed | tf_op | source)
XLA Modules:
  0.0 43.4 jit_solution(2867111823589996308)
XLA Ops:
  0.0 2.5 %collective-permute-start.6 = (bf16[4,16,256]{2,1,0:T(8,128)(2,1)}, bf16[4,16,256]{2,1,0:T(8,128)(2,1)S(1)}, u32[]{:S(2)}, u32[]{:S(2)}) collective-permute-start(bf16[4,16,256]{2,1,0:T(8,128)(2,1)} %img_hbm.1), channel_id=1, source_target_pairs={{0,4},{4,0},{8,12},{12,8},{1,5},{5,1},{9,13},{13,9},{2,6},{6,2},{1... | collective-permute-start | bytes 98312 | tf_op jit(solution)/shard_map/ppermute | solution.py:282
  2.5 1.4 %prep.1 = (bf16[144,128]{1,0:T(8,128)(2,1)S(1)}, bf16[2,2,16,256]{3,2,1,0:T(8,128)(2,1)S(1)}, bf16[12,128,128]{2,1,0:T(8,128)(2,1)S(1)}, bf16[128,512]{1,0:T(8,128)(2,1)S(1)}, bf16[144,256]{1,0:T(8,128)(2,1)S(1)}) custom-call(s32[1]{0:T(128)} %bitcast.index_ref, f32[1,256,256]{2,1,0:T(8,128)} %f_hbm.1, bf16[4,16,256]{2,1,0:T(8,128)(2,1)} %img_hbm.1, ...), custom_call_target="tpu_custom_call" | custom-call | tf_op jit(solution)/shard_map/prep/pallas_call | solution.py:261
  3.8 2.8 %collective-permute-start = (bf16[144,128]{1,0:T(8,128)(2,1)S(1)}, bf16[144,128]{1,0:T(8,128)(2,1)S(1)}, u32[]{:S(2)}, u32[]{:S(2)}) collective-permute-start(bf16[144,128]{1,0:T(8,128)(2,1)S(1)} %get-tuple-element.22), channel_id=1, source_target_pairs={{0,66},{66,0},{2,64},{64,2},{1,67},{67,1},{3,65},{65,3},{4,70},{70... | collective-permute-start | bytes 110600 | tf_op jit(solution)/shard_map/ppermute | solution.py:281
  6.7 1.2 %collective-permute-start.2 = (bf16[12,128,128]{2,1,0:T(8,128)(2,1)S(1)}, bf16[12,128,128]{2,1,0:T(8,128)(2,1)S(1)}, u32[]{:S(2)}, u32[]{:S(2)}) collective-permute-start(bf16[12,128,128]{2,1,0:T(8,128)(2,1)S(1)} %get-tuple-element.23.t_ref), channel_id=1, source_target_pairs={{0,1},{1,0},{2,3},{3,2},{4,5},{5,4},{6,7},{7,6},{8,9},{9,8},{10,11... | collective-permute-start | bytes 1179656 | tf_op jit(solution)/shard_map/ppermute | solution.py:284
  7.9 1.0 %templates.2 = (bf16[12,128,512]{2,1,0:T(8,128)(2,1)S(1)}, f32[12,8,512]{2,1,0:T(8,128)S(1)}) custom-call(bf16[12,128,128]{2,1,0:T(8,128)(2,1)S(1)} %get-tuple-element.23.t_ref, bf16[128,512]{1,0:T(8,128)(2,1)S(1)} %get-tuple-element.24.trow_ref, bf16[144,256]{1,0:T(8,128)(2,1)S(1)} %get-tuple-element.25.tcol_ref), custom_call_target="tpu_custom_call" | custom-call | flops 1080000000 | bytes 2000000 | tf_op jit(solution)/shard_map/templates/pallas_call | solution.py:243
  8.9 0.0 collective-permute-done.6
  9.0 2.3 %collective-permute-start.7 = (bf16[2,2,2,16,256]{4,3,2,1,0:T(8,128)(2,1)S(1)}, bf16[2,2,2,16,256]{4,3,2,1,0:T(8,128)(2,1)S(1)}, u32[]{:S(2)}, u32[]{:S(2)}) collective-permute-start(bf16[2,2,2,16,256]{4,3,2,1,0:T(8,128)(2,1)S(1)} %get-tuple-element.46), channel_id=1, source_target_pairs={{0,12},{12,0},{4,8},{8,4},{1,13},{13,1},{5,9},{9,5},{2,14},{14,2},... | collective-permute-start | bytes 196616 | tf_op jit(solution)/shard_map/ppermute | solution.py:291
  11.3 0.0 collective-permute-done
  11.3 1.3 %collective-permute-start.1 = (bf16[2,144,128]{2,1,0:T(8,128)(2,1)S(1)}, bf16[2,144,128]{2,1,0:T(8,128)(2,1)S(1)}, u32[]{:S(2)}, u32[]{:S(2)}) collective-permute-start(bf16[2,144,128]{2,1,0:T(8,128)(2,1)S(1)} %get-tuple-element.44), channel_id=1, source_target_pairs={{0,16},{16,0},{32,48},{48,32},{1,17},{17,1},{33,49},{49,33},{2,18}... | collective-permute-start | bytes 221192 | tf_op jit(solution)/shard_map/ppermute | solution.py:289
  12.6 1.8 %collective-permute-start.3 = (bf16[2,144,128]{2,1,0:T(8,128)(2,1)S(1)}, bf16[2,144,128]{2,1,0:T(8,128)(2,1)S(1)}, u32[]{:S(2)}, u32[]{:S(2)}) collective-permute-start(bf16[2,144,128]{2,1,0:T(8,128)(2,1)S(1)} %get-tuple-element.44), channel_id=1, source_target_pairs={{0,48},{48,0},{16,32},{32,16},{1,49},{49,1},{17,33},{33,17},{2,50}... | collective-permute-start | bytes 221192 | tf_op jit(solution)/shard_map/ppermute | solution.py:290
  14.4 0.0 collective-permute-done.7
  14.4 0.1 collective-permute-start.8
  14.5 0.0 collective-permute-done.2.t_ref
  14.5 1.0 %templates.3 = (bf16[12,128,512]{2,1,0:T(8,128)(2,1)S(1)}, f32[12,8,512]{2,1,0:T(8,128)S(1)}) custom-call(bf16[12,128,128]{2,1,0:T(8,128)(2,1)S(1)} %collective-permute-done.2.t_ref, bf16[128,512]{1,0:T(8,128)(2,1)S(1)} %get-tuple-element.24.trow_ref, bf16[144,256]{1,0:T(8,128)(2,1)S(1)} %get-tuple-element.25.tcol_ref), custom_call_target="tpu_custom_call" | custom-call | flops 1080000000 | bytes 2000000 | tf_op jit(solution)/shard_map/templates/pallas_call | solution.py:243
  15.6 0.0 copy-start.3
  15.6 0.0 copy-start.4
  15.6 0.0 collective-permute-done.1
  15.6 2.1 %collective-permute-start.4 = (bf16[2,144,128]{2,1,0:T(8,128)(2,1)S(1)}, bf16[2,144,128]{2,1,0:T(8,128)(2,1)S(1)}, u32[]{:S(2)}, u32[]{:S(2)}) collective-permute-start(bf16[2,144,128]{2,1,0:T(8,128)(2,1)S(1)} %collective-permute-done.1), channel_id=1, source_target_pairs={{0,48},{48,0},{16,32},{32,16},{1,49},{49,1},{17,33},{33,17},{2,50}... | collective-permute-start | bytes 221192 | tf_op jit(solution)/shard_map/ppermute | solution.py:295
  17.8 0.0 collective-permute-done.3
  17.8 2.3 %collective-permute-done.4 = bf16[2,144,128]{2,1,0:T(8,128)(2,1)S(1)} collective-permute-done((bf16[2,144,128]{2,1,0:T(8,128)(2,1)S(1)}, bf16[2,144,128]{2,1,0:T(8,128)(2,1)S(1)}, u32[]{:S(2)}, u32[]{:S(2)}) %collective-permute-start.4) | collective-permute-done | bytes 73760 | tf_op jit(solution)/shard_map/ppermute | solution.py:295
  20.1 2.2 %collective-permute-start.5 = (bf16[2,2,2,144,128]{4,3,2,1,0:T(8,128)(2,1)S(1)}, bf16[2,2,2,144,128]{4,3,2,1,0:T(8,128)(2,1)S(1)}, u32[]{:S(2)}, u32[]{:S(2)}) collective-permute-start(bf16[2,2,2,144,128]{4,3,2,1,0:T(8,128)(2,1)S(1)} %pad_maximum_fusion.fa_ref), channel_id=1, source_target_pairs={{0,1},{1,0},{2,3},{3,2},{4,5},{5,4},{6,7},{7,6},{8,9},{9,8},{10,11... | collective-permute-start | bytes 884744 | tf_op jit(solution)/shard_map/ppermute | solution.py:300
  22.3 0.0 collective-permute-done.8
  22.4 0.0 copy-start
  22.4 0.0 copy-start.1
  22.4 0.0 copy-start.2
  22.4 0.1 collective-permute-start.9
  22.5 1.3 %collective-permute-done.9.refs_1_ = bf16[2,2,2,2,16,256]{5,4,3,2,1,0:T(8,128)(2,1)S(1)} collective-permute-done((bf16[2,2,2,2,16,256]{5,4,3,2,1,0:T(8,128)(2,1)S(1)}, bf16[2,2,2,2,16,256]{5,4,3,2,1,0:T(8,128)(2,1)S(1)}, u32[]{:S(2)}, u32[]{:S(2)}) %collective-permute-start.9) | collective-permute-done | bytes 131104 | tf_op jit(solution)/shard_map/ppermute | solution.py:299
  23.8 0.0 copy-done.3
  23.8 0.0 copy-done.4
  23.8 0.5 %tiles.1.spec_ref = f32[2,144,512]{2,1,0:T(8,128)S(1)} custom-call(s32[1]{0:T(128)} %bitcast.index_ref, bf16[2,2,2,2,16,256]{5,4,3,2,1,0:T(8,128)(2,1)S(1)} %get-tuple-element.40.refs_0_, bf16[2,2,2,2,16,256]{5,4,3,2,1,0:T(8,128)(2,1)S(1)} %collective-permute-done.9.refs_1_, bf16[256,512]{1,0:T(8,128)(2,1)S(1)} %copy-done.3, bf16[144,512]{1,0:T(8,128)(2,1)S(1)} %copy-done.4), custom_call_target="tpu_custom_call" | custom-call | flops 800000000 | bytes 1000000 | tf_op jit(solution)/shard_map/tiles/pallas_call | solution.py:301
  24.4 0.0 collective-permute-done.5.fb_ref
  24.4 0.0 copy-done
  24.4 0.0 copy-done.1
  24.4 0.0 copy-done.2
  24.4 6.3 %correlate.1 = f32[16,2,16,256]{3,2,1,0:T(8,128)S(1)} custom-call(s32[1]{0:T(128)} %bitcast.index_ref, s32[32]{0:T(128)S(1)} %copy-done.2, f32[2,144,512]{2,1,0:T(8,128)S(1)} %tiles.1.spec_ref, bf16[2,2,2,144,128]{4,3,2,1,0:T(8,128)(2,1)S(1)} %pad_maximum_fusion.fa_ref, bf16[2,2,2,144,128]{4,3,2,1,0:T(8,128)(2,1)S(1)} %collective-permute-done.5.fb_ref, ...), custom_call_target="tpu_custom_call" | custom-call | tf_op jit(solution)/shard_map/correlate/pallas_call | solution.py:316
  30.8 11.9 %all_to_all.5 = f16[16,2,16,256]{3,2,1,0:T(8,128)(2,1)S(1)} all-to-all(f16[16,2,16,256]{3,2,1,0:T(8,128)(2,1)S(1)} %convert_element_type.4), channel_id=1, replica_groups=mesh['yh'=2,'x'=4,'z'=4,'yl'=2,'c'=2] {'z','yl','c'}, dimensions={0} | all-to-all | bytes 524288 | tf_op jit(solution)/shard_map/all_to_all | solution.py:335
  42.7 0.7 %convert_reduce_fusion = f32[4,16,256]{2,1,0:T(8,128)} fusion(f16[8,4,16,256]{3,2,1,0:T(8,128)(2,1)S(1)} %bitcast.36), kind=kLoop, calls=%fused_computation | loop fusion | flops 245760 | bytes 327680 | tf_op jit(solution)/shard_map/reduce_max | solution.py:336
  (9 shorter events, 0.2 us)
Async XLA Ops:
  0.0 8.9 %collective-permute-start.6 = (bf16[4,16,256]{2,1,0:T(8,128)(2,1)}, bf16[4,16,256]{2,1,0:T(8,128)(2,1)S(1)}, u32[]{:S(2)}, u32[]{:S(2)}) collective-permute-start(bf16[4,16,256]{2,1,0:T(8,128)(2,1)} %img_hbm.1), channel_id=1, source_target_pairs={{0,4},{4,0},{8,12},{12,8},{1,5},{5,1},{9,13},{13,9},{2,6},{6,2},{1... | collective-permute-start | bytes 98312 | tf_op jit(solution)/shard_map/ppermute | solution.py:282
  3.8 7.4 %collective-permute-start = (bf16[144,128]{1,0:T(8,128)(2,1)S(1)}, bf16[144,128]{1,0:T(8,128)(2,1)S(1)}, u32[]{:S(2)}, u32[]{:S(2)}) collective-permute-start(bf16[144,128]{1,0:T(8,128)(2,1)S(1)} %get-tuple-element.22), channel_id=1, source_target_pairs={{0,66},{66,0},{2,64},{64,2},{1,67},{67,1},{3,65},{65,3},{4,70},{70... | collective-permute-start | bytes 110600 | tf_op jit(solution)/shard_map/ppermute | solution.py:281
  6.7 7.9 %collective-permute-start.2 = (bf16[12,128,128]{2,1,0:T(8,128)(2,1)S(1)}, bf16[12,128,128]{2,1,0:T(8,128)(2,1)S(1)}, u32[]{:S(2)}, u32[]{:S(2)}) collective-permute-start(bf16[12,128,128]{2,1,0:T(8,128)(2,1)S(1)} %get-tuple-element.23.t_ref), channel_id=1, source_target_pairs={{0,1},{1,0},{2,3},{3,2},{4,5},{5,4},{6,7},{7,6},{8,9},{9,8},{10,11... | collective-permute-start | bytes 1179656 | tf_op jit(solution)/shard_map/ppermute | solution.py:284
  9.0 5.5 %collective-permute-start.7 = (bf16[2,2,2,16,256]{4,3,2,1,0:T(8,128)(2,1)S(1)}, bf16[2,2,2,16,256]{4,3,2,1,0:T(8,128)(2,1)S(1)}, u32[]{:S(2)}, u32[]{:S(2)}) collective-permute-start(bf16[2,2,2,16,256]{4,3,2,1,0:T(8,128)(2,1)S(1)} %get-tuple-element.46), channel_id=1, source_target_pairs={{0,12},{12,0},{4,8},{8,4},{1,13},{13,1},{5,9},{9,5},{2,14},{14,2},... | collective-permute-start | bytes 196616 | tf_op jit(solution)/shard_map/ppermute | solution.py:291
  11.3 4.3 %collective-permute-start.1 = (bf16[2,144,128]{2,1,0:T(8,128)(2,1)S(1)}, bf16[2,144,128]{2,1,0:T(8,128)(2,1)S(1)}, u32[]{:S(2)}, u32[]{:S(2)}) collective-permute-start(bf16[2,144,128]{2,1,0:T(8,128)(2,1)S(1)} %get-tuple-element.44), channel_id=1, source_target_pairs={{0,16},{16,0},{32,48},{48,32},{1,17},{17,1},{33,49},{49,33},{2,18}... | collective-permute-start | bytes 221192 | tf_op jit(solution)/shard_map/ppermute | solution.py:289
  12.6 5.2 %collective-permute-start.3 = (bf16[2,144,128]{2,1,0:T(8,128)(2,1)S(1)}, bf16[2,144,128]{2,1,0:T(8,128)(2,1)S(1)}, u32[]{:S(2)}, u32[]{:S(2)}) collective-permute-start(bf16[2,144,128]{2,1,0:T(8,128)(2,1)S(1)} %get-tuple-element.44), channel_id=1, source_target_pairs={{0,48},{48,0},{16,32},{32,16},{1,49},{49,1},{17,33},{33,17},{2,50}... | collective-permute-start | bytes 221192 | tf_op jit(solution)/shard_map/ppermute | solution.py:290
  14.4 7.9 %collective-permute-start.8 = (bf16[2,2,2,2,16,256]{5,4,3,2,1,0:T(8,128)(2,1)S(1)}, bf16[2,2,2,2,16,256]{5,4,3,2,1,0:T(8,128)(2,1)S(1)}, u32[]{:S(2)}, u32[]{:S(2)}) collective-permute-start(bf16[2,2,2,2,16,256]{5,4,3,2,1,0:T(8,128)(2,1)S(1)} %get-tuple-element.41), channel_id=1, source_target_pairs={{0,2},{2,0},{1,3},{3,1},{4,6},{6,4},{5,7},{7,5},{8,10},{10,8},{9,1... | collective-permute-start | bytes 393224 | tf_op jit(solution)/shard_map/ppermute | solution.py:296
  15.6 8.3 %copy-start.3 = (bf16[256,512]{1,0:T(8,128)(2,1)S(1)}, bf16[256,512]{1,0:T(8,128)(2,1)}, u32[]{:S(2)}) copy-start(bf16[256,512]{1,0:T(8,128)(2,1)} %constant.43.clone.refs_2_) | copy-start | bytes 786436
  15.6 8.3 %copy-start.4 = (bf16[144,512]{1,0:T(8,128)(2,1)S(1)}, bf16[144,512]{1,0:T(8,128)(2,1)}, u32[]{:S(2)}) copy-start(bf16[144,512]{1,0:T(8,128)(2,1)} %constant.44.clone.refs_3_) | copy-start | bytes 442372
  15.6 4.5 %collective-permute-start.4 = (bf16[2,144,128]{2,1,0:T(8,128)(2,1)S(1)}, bf16[2,144,128]{2,1,0:T(8,128)(2,1)S(1)}, u32[]{:S(2)}, u32[]{:S(2)}) collective-permute-start(bf16[2,144,128]{2,1,0:T(8,128)(2,1)S(1)} %collective-permute-done.1), channel_id=1, source_target_pairs={{0,48},{48,0},{16,32},{32,16},{1,49},{49,1},{17,33},{33,17},{2,50}... | collective-permute-start | bytes 221192 | tf_op jit(solution)/shard_map/ppermute | solution.py:295
  20.1 4.2 %collective-permute-start.5 = (bf16[2,2,2,144,128]{4,3,2,1,0:T(8,128)(2,1)S(1)}, bf16[2,2,2,144,128]{4,3,2,1,0:T(8,128)(2,1)S(1)}, u32[]{:S(2)}, u32[]{:S(2)}) collective-permute-start(bf16[2,2,2,144,128]{4,3,2,1,0:T(8,128)(2,1)S(1)} %pad_maximum_fusion.fa_ref), channel_id=1, source_target_pairs={{0,1},{1,0},{2,3},{3,2},{4,5},{5,4},{6,7},{7,6},{8,9},{9,8},{10,11... | collective-permute-start | bytes 884744 | tf_op jit(solution)/shard_map/ppermute | solution.py:300
  22.4 2.0 %copy-start = (bf16[2,256,256]{2,1,0:T(8,128)(2,1)S(1)}, bf16[2,256,256]{2,1,0:T(8,128)(2,1)}, u32[]{:S(2)}) copy-start(bf16[2,256,256]{2,1,0:T(8,128)(2,1)} %constant.47.clone.inv1_ref) | copy-start | bytes 786436
  22.4 2.0 %copy-start.1 = (bf16[256,256]{1,0:T(8,128)(2,1)S(1)}, bf16[256,256]{1,0:T(8,128)(2,1)}, u32[]{:S(2)}) copy-start(bf16[256,256]{1,0:T(8,128)(2,1)} %constant.48.clone.inv2_ref) | copy-start | bytes 393220
  22.4 2.0 %copy-start.2 = (s32[32]{0:T(128)S(1)}, s32[32]{0:T(128)}, u32[]{:S(2)}) copy-start(s32[32]{0:T(128)} %bins_ref.1) | copy-start | bytes 388
  22.4 1.4 %collective-permute-start.9 = (bf16[2,2,2,2,16,256]{5,4,3,2,1,0:T(8,128)(2,1)S(1)}, bf16[2,2,2,2,16,256]{5,4,3,2,1,0:T(8,128)(2,1)S(1)}, u32[]{:S(2)}, u32[]{:S(2)}) collective-permute-start(bf16[2,2,2,2,16,256]{5,4,3,2,1,0:T(8,128)(2,1)S(1)} %get-tuple-element.39), channel_id=1, source_target_pairs={{0,1},{1,0},{2,3},{3,2},{4,5},{5,4},{6,7},{7,6},{8,9},{9,8},{10,11... | collective-permute-start | bytes 393224 | tf_op jit(solution)/shard_map/ppermute | solution.py:299
